TPU v7x, 32 devices: a whole 2x2x4 slice. The times are simulated.
32 devices in a mesh: transit: 8 (over z, y), lateral: 4 (over x, core).
Axes of the slice: x: 2, y: 2, z: 4, core: 2. Of those that a mesh axis runs over, the one named last changes fastest.
Arguments:
- displacement: float32 [6, 512, 512], P(None, 'transit', 'lateral'), may hold values from -3.06 to 3.06
- velocity: float32 [6, 512, 512], P(None, 'transit', 'lateral'), may hold values from -6.3 to 6.3
- damage: float32 [512, 512], P('transit', 'lateral'), may hold values from 0 to 0.3
- strength: float32 [512, 512], P('transit', 'lateral'), may hold values from 0.3 to 3
- contact: int32 [512, 512], P('transit', 'lateral'), may hold values 0 or 1
- flaw_cells: int32 [8, 4, 32], P('transit', 'lateral'), may hold values from 0 to 8191, as said below
Outputs:
- new_displacement: float32 [6, 512, 512], P(None, 'transit', 'lateral')
- new_velocity: float32 [6, 512, 512], P(None, 'transit', 'lateral')
- new_damage: float32 [512, 512], P('transit', 'lateral')
Inputs may be any that keep to these rules, and one draw needn't show every extreme that they name: `flaw_cells`: entry [t, l, j] is the node (row * 128 + column) of the tile with transit index t and lateral index l, a tile holding 64 x 128 nodes; entries may repeat.
All inputs are finite; a program needn't handle non-finite values. No bound on the sum of `contact` on one device may be relied on, other than what follows from the above.
Results may differ from a plain program's by a relative error of at most 0.0001.
Values sent between devices are 32-bit elements; how exact they have to be, the bound alone decides.
No kernel may reach another device: no remote copies, remote signals or barrier semaphores. Data moves between devices by JAX's collectives and lax.ppermute only.
A program may use at most 64 MiB of HBM per device.

v0:
```python
import math

import jax
import jax.numpy as jnp
import numpy as np
from jax import lax
from jax.sharding import PartitionSpec as P

STEPS = 2
RADIUS = 8


lap_stiffness = (1.0, 1.0, 0.0, 0.5, 0.5, 0.2)
viscous_coef = 0.2
along_pairs = ((2, 3, 1.0, 0.8), (1, 5, 1.0, 0.3))
across_pairs = ((2, 4, 1.0, 0.8), (0, 5, -1.0, 0.3))
contact_stiff = 2.0
hull_goal = (1.5, 0.0, -0.5, 0.0, 0.0, 0.0)
hull_select = (1.0, 0.0, 1.0, 0.0, 0.0, 0.0)
time_step = 0.4
keep_rate = 0.95
flaw_weaken = 0.6
soften_scale = 6.0
spread_denominator = 32.0
fibre_depth = (-0.75, -0.25, 0.25, 0.75)
channel_threshold = (0.6, 0.6, 1.2, 0.6, 0.6, 1.2, 0.6, 0.6, 1.2, 0.6, 0.6, 1.2, 1.5, 1.5, 1.2, 1.0)


def with_halo(shard, sides, width):
    for axis, dim in sides:
        count, length = (lax.axis_size(axis), shard.shape[dim])
        up = [(i, (i + 1) % count) for i in range(count - 1)]
        down = [(j, i) for i, j in up]
        last = lax.slice_in_dim(shard, length - width, length, axis=dim)
        first = lax.slice_in_dim(shard, 0, width, axis=dim)
        before = lax.ppermute(last, axis, up)
        after = lax.ppermute(first, axis, down)
        shard = jnp.concatenate([before, shard, after], axis=dim)
    return shard


def channel_table():
    coef_table = np.zeros((16, 9), np.float32)
    for fibre_idx in range(4):
        for component in range(3):
            coef_table[3 * fibre_idx + component, component] = 1.0
            coef_table[3 * fibre_idx + component, 3 + component] = fibre_depth[fibre_idx]
    coef_table[12, 6] = 1.0
    coef_table[13, 7] = 1.0
    coef_table[14, 8] = 1.0
    coef_table[15, 5] = 1.0
    return jnp.asarray(coef_table)


def neighbours(padded):
    return (
        padded[..., 2:, 1:-1],
        padded[..., :-2, 1:-1],
        padded[..., 1:-1, 2:],
        padded[..., 1:-1, :-2],
    )


def strain_fields(middle, beside_all):
    plus_x, minus_x, plus_y, minus_y = beside_all
    slope_x = 0.5 * (plus_x - minus_x)
    slope_y = 0.5 * (plus_y - minus_y)
    return jnp.stack(
        [
            slope_x[0],
            slope_y[1],
            slope_y[0] + slope_x[1],
            slope_x[3],
            slope_y[4],
            slope_y[3] + slope_x[4],
            slope_x[2] - middle[3],
            slope_y[2] - middle[4],
            0.5 * (slope_x[1] - slope_y[0]) - middle[5],
        ]
    )


def edge_force(middle, other, sense, pairs):
    change = other - middle
    pieces = [
        lap_stiffness[comp_idx] * change[comp_idx] + viscous_coef * change[6 + comp_idx]
        for comp_idx in range(6)
    ]
    for lead_comp, turn_comp, sign_lead, stiff_coef in pairs:
        shear_term = sign_lead * sense * change[lead_comp] - 0.5 * (
            middle[turn_comp] + other[turn_comp]
        )
        pieces[lead_comp] = pieces[lead_comp] + sense * sign_lead * stiff_coef * shear_term
        pieces[turn_comp] = pieces[turn_comp] + 0.5 * stiff_coef * shear_term
    return jnp.stack(pieces)


def band_matrix(length):
    row_pos = lax.broadcasted_iota(jnp.int32, (length, length + 2 * RADIUS), 0)
    col_pos = lax.broadcasted_iota(jnp.int32, (length, length + 2 * RADIUS), 1)
    offset = (col_pos - row_pos - RADIUS).astype(jnp.float32)
    within = jnp.abs(offset) <= RADIUS
    return jnp.where(within, jnp.exp(-offset * offset / spread_denominator), 0.0)


def coverage_line(start_pos, total_len, length):
    band = band_matrix(length)
    position = start_pos + jnp.arange(length + 2 * RADIUS, dtype=jnp.int32) - RADIUS
    inside = ((position >= 0) & (position < total_len)).astype(jnp.float32)
    return jnp.dot(band, inside, precision=lax.Precision.HIGHEST)


def block_rows(length):
    return math.gcd(length, 128)


def along_product(field):
    length = field.shape[1] - 2 * RADIUS
    block = block_rows(length)
    band = band_matrix(block)
    windows = jnp.stack([field], 1)
    result = jnp.einsum("ij,knjl->knil", band, windows, precision=lax.Precision.HIGHEST)
    return result.reshape(field.shape[0], length, field.shape[2])


def across_product(field):
    length = field.shape[2] - 2 * RADIUS
    block = block_rows(length)
    band = band_matrix(block)
    windows = jnp.stack([field], 2)
    result = jnp.einsum("kinj,mj->kinm", windows, band, precision=lax.Precision.HIGHEST)
    return result.reshape(field.shape[0], field.shape[1], length)


def average(energy):
    widened = with_halo(energy, (("transit", 1),), RADIUS)
    along = along_product(widened)
    widened_y = with_halo(along, (("lateral", 2),), RADIUS)
    return across_product(widened_y)


def on_device(displacement, velocity, damage, strength, contact, flaw_cells):
    rows_x, rows_y = damage.shape
    start_x = lax.axis_index("transit") * rows_x
    start_y = lax.axis_index("lateral") * rows_y
    total_x = rows_x * lax.axis_size("transit")
    total_y = rows_y * lax.axis_size("lateral")
    coverage = (
        coverage_line(start_x, total_x, rows_x)[:, None]
        * coverage_line(start_y, total_y, rows_y)[None, :]
    )
    marks = (
        jnp.zeros((rows_x * rows_y,), jnp.float32)
        .at[flaw_cells.reshape(-1)]
        .set(1.0)
        .reshape(rows_x, rows_y)
    )
    limit = strength * (1.0 - flaw_weaken * marks)
    grip = contact.astype(jnp.float32) * contact_stiff
    goal = jnp.asarray(hull_goal, jnp.float32)[:, None, None]
    select = jnp.asarray(hull_select, jnp.float32)[:, None, None]
    coef_table = channel_table()
    thresholds = jnp.asarray(channel_threshold, jnp.float32)[:, None, None]
    edge_senses = (1.0, -1.0, 1.0, -1.0)
    edge_pairs = (along_pairs, along_pairs, across_pairs, across_pairs)
    for step_idx in range(STEPS):
        state_now = jnp.concatenate([displacement, velocity], 0)
        padded = with_halo(state_now, (("transit", 1), ("lateral", 2)), 1)
        middle = padded[:, 1:-1, 1:-1]
        beside_all = neighbours(padded)
        fields = strain_fields(middle[:6], tuple((piece[:6] for piece in beside_all)))
        energy = jnp.einsum("kf,fxy->kxy", coef_table, fields, precision=lax.Precision.HIGHEST) ** 2
        raw_forces = [
            edge_force(middle, piece, sense, pairs)
            for piece, sense, pairs in zip(beside_all, edge_senses, edge_pairs)
        ]
        averaged = average(energy) / coverage
        driving = jnp.sum(jnp.maximum(averaged - limit * thresholds, 0.0), axis=0)
        damage = jnp.maximum(damage, 1.0 - jnp.exp(-driving / soften_scale))
        damage_pad = with_halo(damage, (("transit", 0), ("lateral", 1)), 1)
        damage_near = neighbours(damage_pad)
        force = jnp.zeros_like(displacement)
        for raw_piece, near in zip(raw_forces, damage_near):
            force = force + (1.0 - 0.5 * (damage + near)) * raw_piece
        force = force + grip * select * (goal - displacement)
        velocity = keep_rate * velocity + time_step * force
        displacement = displacement + time_step * velocity
    return (displacement, velocity, damage)


def solution(mesh):
    return jax.shard_map(
        on_device,
        mesh=mesh,
        in_specs=(
            P(None, "transit", "lateral"),
            P(None, "transit", "lateral"),
            P("transit", "lateral"),
            P("transit", "lateral"),
            P("transit", "lateral"),
            P("transit", "lateral", None),
        ),
        out_specs=(
            P(None, "transit", "lateral"),
            P(None, "transit", "lateral"),
            P("transit", "lateral"),
        ),
        check_vma=False,
    )
```

profile of v0, /device:TPU:25, one launch (start us, length us, event | category | flops | bytes accessed | tf_op | source)
XLA Modules:
  0.0 123.6 jit_solution(14194351325549307026)
XLA Ops:
  1.7 3.0 %collective-permute-start = (f32[12,1,128]{2,1,0:T(1,128)S(1)}, f32[12,1,128]{2,1,0:T(1,128)S(1)}, u32[]{:S(2)}, u32[]{:S(2)}) collective-permute-start(f32[12,1,128]{2,1,0:T(1,128)S(1)} %get-tuple-element.92), channel_id=1, source_target_pairs={{4,0},{8,4},{12,8},{16,12},{20,16},{24,20},{28,24},{5,1},{9,5},{13... | collective-permute-start | bytes 18440 | tf_op jit(solution)/shard_map/ppermute | solution.py:37
  4.7 2.2 %collective-permute-start.1 = (f32[12,1,128]{2,1,0:T(1,128)S(1)}, f32[12,1,128]{2,1,0:T(1,128)S(1)}, u32[]{:S(2)}, u32[]{:S(2)}) collective-permute-start(f32[12,1,128]{2,1,0:T(1,128)S(1)} %get-tuple-element.91), channel_id=1, source_target_pairs={{0,4},{4,8},{8,12},{12,16},{16,20},{20,24},{24,28},{1,5},{5,9},{9,... | collective-permute-start | bytes 18440 | tf_op jit(solution)/shard_map/ppermute | solution.py:36
  10.4 4.0 %collective-permute-start.2 = (f32[12,66,1]{1,2,0:T(1,128)S(1)}, f32[12,66,1]{1,2,0:T(1,128)S(1)}, u32[]{:S(2)}, u32[]{:S(2)}) collective-permute-start(f32[12,66,1]{1,2,0:T(1,128)S(1)} %copy.45), channel_id=1, source_target_pairs={{1,0},{2,1},{3,2},{5,4},{6,5},{7,6},{9,8},{10,9},{11,10},{13,12},{... | collective-permute-start | bytes 9512 | tf_op jit(solution)/shard_map/ppermute | solution.py:37
  14.7 3.0 %collective-permute-start.3 = (f32[12,66,1]{1,2,0:T(1,128)S(1)}, f32[12,66,1]{1,2,0:T(1,128)S(1)}, u32[]{:S(2)}, u32[]{:S(2)}) collective-permute-start(f32[12,66,1]{1,2,0:T(1,128)S(1)} %copy.47), channel_id=1, source_target_pairs={{0,1},{1,2},{2,3},{4,5},{5,6},{6,7},{8,9},{9,10},{10,11},{12,13},{... | collective-permute-start | bytes 9512 | tf_op jit(solution)/shard_map/ppermute | solution.py:36
  24.2 3.4 %collective-permute-start.4 = (f32[16,8,128]{2,0,1:T(8,128)S(1)}, f32[16,8,128]{2,0,1:T(8,128)S(1)}, u32[]{:S(2)}, u32[]{:S(2)}) collective-permute-start(f32[16,8,128]{2,0,1:T(8,128)S(1)} %get-tuple-element.59), channel_id=1, source_target_pairs={{0,4},{4,8},{8,12},{12,16},{16,20},{20,24},{24,28},{1,5},{5,9},{9,... | collective-permute-start | bytes 196616 | tf_op jit(solution)/shard_map/ppermute | solution.py:36
  28.1 2.8 %collective-permute-done.4 = f32[16,8,128]{2,0,1:T(8,128)S(1)} collective-permute-done((f32[16,8,128]{2,0,1:T(8,128)S(1)}, f32[16,8,128]{2,0,1:T(8,128)S(1)}, u32[]{:S(2)}, u32[]{:S(2)}) %collective-permute-start.4) | collective-permute-done | bytes 65568 | tf_op jit(solution)/shard_map/ppermute | solution.py:36
  32.0 2.3 %collective-permute-start.7 = (f32[16,64,8]{2,1,0:T(8,128)S(1)}, f32[16,64,8]{2,1,0:T(8,128)S(1)}, u32[]{:S(2)}, u32[]{:S(2)}) collective-permute-start(f32[16,64,8]{2,1,0:T(8,128)S(1)} %get-tuple-element.58), channel_id=1, source_target_pairs={{1,0},{2,1},{3,2},{5,4},{6,5},{7,6},{9,8},{10,9},{11,10},{13,12},{... | collective-permute-start | bytes 98312 | tf_op jit(solution)/shard_map/ppermute | solution.py:37
  34.3 4.1 %collective-permute-start.6 = (f32[16,64,8]{2,1,0:T(8,128)S(1)}, f32[16,64,8]{2,1,0:T(8,128)S(1)}, u32[]{:S(2)}, u32[]{:S(2)}) collective-permute-start(f32[16,64,8]{2,1,0:T(8,128)S(1)} %get-tuple-element.57), channel_id=1, source_target_pairs={{0,1},{1,2},{2,3},{4,5},{5,6},{6,7},{8,9},{9,10},{10,11},{12,13},{... | collective-permute-start | bytes 98312 | tf_op jit(solution)/shard_map/ppermute | solution.py:36
  38.4 4.9 %collective-permute-done.7 = f32[16,64,8]{2,1,0:T(8,128)S(1)} collective-permute-done((f32[16,64,8]{2,1,0:T(8,128)S(1)}, f32[16,64,8]{2,1,0:T(8,128)S(1)}, u32[]{:S(2)}, u32[]{:S(2)}) %collective-permute-start.7) | collective-permute-done | bytes 32800 | tf_op jit(solution)/shard_map/ppermute | solution.py:37
  46.4 2.6 %collective-permute-start.8 = (f32[1,128]{1,0:T(1,128)S(1)}, f32[1,128]{1,0:T(1,128)S(1)}, u32[]{:S(2)}, u32[]{:S(2)}) collective-permute-start(f32[1,128]{1,0:T(1,128)S(1)} %get-tuple-element.113), channel_id=1, source_target_pairs={{4,0},{8,4},{12,8},{16,12},{20,16},{24,20},{28,24},{5,1},{9,5},{13... | collective-permute-start | bytes 1544 | tf_op jit(solution)/shard_map/ppermute | solution.py:37
  49.0 2.6 %collective-permute-start.9 = (f32[1,128]{1,0:T(1,128)S(1)}, f32[1,128]{1,0:T(1,128)S(1)}, u32[]{:S(2)}, u32[]{:S(2)}) collective-permute-start(f32[1,128]{1,0:T(1,128)S(1)} %get-tuple-element.112), channel_id=1, source_target_pairs={{0,4},{4,8},{8,12},{12,16},{16,20},{20,24},{24,28},{1,5},{5,9},{9,... | collective-permute-start | bytes 1544 | tf_op jit(solution)/shard_map/ppermute | solution.py:36
  51.7 2.5 %collective-permute-done.9 = f32[1,128]{1,0:T(1,128)S(1)} collective-permute-done((f32[1,128]{1,0:T(1,128)S(1)}, f32[1,128]{1,0:T(1,128)S(1)}, u32[]{:S(2)}, u32[]{:S(2)}) %collective-permute-start.9) | collective-permute-done | bytes 544 | tf_op jit(solution)/shard_map/ppermute | solution.py:36
  56.2 5.8 %collective-permute-start.11 = (f32[66,1]{1,0:T(8,128)S(1)}, f32[66,1]{1,0:T(8,128)S(1)}, u32[]{:S(2)}, u32[]{:S(2)}) collective-permute-start(f32[66,1]{1,0:T(8,128)S(1)} %get-tuple-element.101), channel_id=1, source_target_pairs={{0,1},{1,2},{2,3},{4,5},{5,6},{6,7},{8,9},{9,10},{10,11},{12,13},{... | collective-permute-start | bytes 800 | tf_op jit(solution)/shard_map/ppermute | solution.py:36
  66.0 3.4 %collective-permute-start.13 = (f32[12,1,128]{2,1,0:T(1,128)S(1)}, f32[12,1,128]{2,1,0:T(1,128)S(1)}, u32[]{:S(2)}, u32[]{:S(2)}) collective-permute-start(f32[12,1,128]{2,1,0:T(1,128)S(1)} %get-tuple-element.85), channel_id=1, source_target_pairs={{0,4},{4,8},{8,12},{12,16},{16,20},{20,24},{24,28},{1,5},{5,9},{9,... | collective-permute-start | bytes 18440 | tf_op jit(solution)/shard_map/ppermute | solution.py:36
  71.7 1.9 %collective-permute-start.14 = (f32[12,66,1]{1,2,0:T(1,128)S(1)}, f32[12,66,1]{1,2,0:T(1,128)S(1)}, u32[]{:S(2)}, u32[]{:S(2)}) collective-permute-start(f32[12,66,1]{1,2,0:T(1,128)S(1)} %copy.51), channel_id=1, source_target_pairs={{1,0},{2,1},{3,2},{5,4},{6,5},{7,6},{9,8},{10,9},{11,10},{13,12},{... | collective-permute-start | bytes 9512 | tf_op jit(solution)/shard_map/ppermute | solution.py:37
  73.8 5.4 %collective-permute-start.15 = (f32[12,66,1]{1,2,0:T(1,128)S(1)}, f32[12,66,1]{1,2,0:T(1,128)S(1)}, u32[]{:S(2)}, u32[]{:S(2)}) collective-permute-start(f32[12,66,1]{1,2,0:T(1,128)S(1)} %copy.53), channel_id=1, source_target_pairs={{0,1},{1,2},{2,3},{4,5},{5,6},{6,7},{8,9},{9,10},{10,11},{12,13},{... | collective-permute-start | bytes 9512 | tf_op jit(solution)/shard_map/ppermute | solution.py:36
  82.4 2.6 %collective-permute-start.17 = (f32[16,8,128]{2,0,1:T(8,128)S(1)}, f32[16,8,128]{2,0,1:T(8,128)S(1)}, u32[]{:S(2)}, u32[]{:S(2)}) collective-permute-start(f32[16,8,128]{2,0,1:T(8,128)S(1)} %get-tuple-element.56), channel_id=1, source_target_pairs={{4,0},{8,4},{12,8},{16,12},{20,16},{24,20},{28,24},{5,1},{9,5},{13... | collective-permute-start | bytes 196616 | tf_op jit(solution)/shard_map/ppermute | solution.py:37
  85.0 2.7 %collective-permute-start.16 = (f32[16,8,128]{2,0,1:T(8,128)S(1)}, f32[16,8,128]{2,0,1:T(8,128)S(1)}, u32[]{:S(2)}, u32[]{:S(2)}) collective-permute-start(f32[16,8,128]{2,0,1:T(8,128)S(1)} %get-tuple-element.55), channel_id=1, source_target_pairs={{0,4},{4,8},{8,12},{12,16},{16,20},{20,24},{24,28},{1,5},{5,9},{9,... | collective-permute-start | bytes 196616 | tf_op jit(solution)/shard_map/ppermute | solution.py:36
  87.9 3.1 %collective-permute-done.16 = f32[16,8,128]{2,0,1:T(8,128)S(1)} collective-permute-done((f32[16,8,128]{2,0,1:T(8,128)S(1)}, f32[16,8,128]{2,0,1:T(8,128)S(1)}, u32[]{:S(2)}, u32[]{:S(2)}) %collective-permute-start.16) | collective-permute-done | bytes 65568 | tf_op jit(solution)/shard_map/ppermute | solution.py:36
  94.0 5.6 %collective-permute-start.18 = (f32[16,64,8]{2,1,0:T(8,128)S(1)}, f32[16,64,8]{2,1,0:T(8,128)S(1)}, u32[]{:S(2)}, u32[]{:S(2)}) collective-permute-start(f32[16,64,8]{2,1,0:T(8,128)S(1)} %get-tuple-element.53), channel_id=1, source_target_pairs={{0,1},{1,2},{2,3},{4,5},{5,6},{6,7},{8,9},{9,10},{10,11},{12,13},{... | collective-permute-start | bytes 98312 | tf_op jit(solution)/shard_map/ppermute | solution.py:36
  99.6 4.9 %collective-permute-done.19 = f32[16,64,8]{2,1,0:T(8,128)S(1)} collective-permute-done((f32[16,64,8]{2,1,0:T(8,128)S(1)}, f32[16,64,8]{2,1,0:T(8,128)S(1)}, u32[]{:S(2)}, u32[]{:S(2)}) %collective-permute-start.19) | collective-permute-done | bytes 32800 | tf_op jit(solution)/shard_map/ppermute | solution.py:37
  106.9 1.9 %collective-permute-start.20 = (f32[1,128]{1,0:T(1,128)S(1)}, f32[1,128]{1,0:T(1,128)S(1)}, u32[]{:S(2)}, u32[]{:S(2)}) collective-permute-start(f32[1,128]{1,0:T(1,128)S(1)} %get-tuple-element.111), channel_id=1, source_target_pairs={{4,0},{8,4},{12,8},{16,12},{20,16},{24,20},{28,24},{5,1},{9,5},{13... | collective-permute-start | bytes 1544 | tf_op jit(solution)/shard_map/ppermute | solution.py:37
  108.8 3.4 %collective-permute-start.21 = (f32[1,128]{1,0:T(1,128)S(1)}, f32[1,128]{1,0:T(1,128)S(1)}, u32[]{:S(2)}, u32[]{:S(2)}) collective-permute-start(f32[1,128]{1,0:T(1,128)S(1)} %get-tuple-element.110), channel_id=1, source_target_pairs={{0,4},{4,8},{8,12},{12,16},{16,20},{20,24},{24,28},{1,5},{5,9},{9,... | collective-permute-start | bytes 1544 | tf_op jit(solution)/shard_map/ppermute | solution.py:36
  116.0 5.5 %collective-permute-start.23 = (f32[66,1]{1,0:T(8,128)S(1)}, f32[66,1]{1,0:T(8,128)S(1)}, u32[]{:S(2)}, u32[]{:S(2)}) collective-permute-start(f32[66,1]{1,0:T(8,128)S(1)} %get-tuple-element.99), channel_id=1, source_target_pairs={{0,1},{1,2},{2,3},{4,5},{5,6},{6,7},{8,9},{9,10},{10,11},{12,13},{... | collective-permute-start | bytes 800 | tf_op jit(solution)/shard_map/ppermute | solution.py:36
  (154 shorter events, 38.2 us)
Async XLA Ops:
  1.7 6.6 %collective-permute-start = (f32[12,1,128]{2,1,0:T(1,128)S(1)}, f32[12,1,128]{2,1,0:T(1,128)S(1)}, u32[]{:S(2)}, u32[]{:S(2)}) collective-permute-start(f32[12,1,128]{2,1,0:T(1,128)S(1)} %get-tuple-element.92), channel_id=1, source_target_pairs={{4,0},{8,4},{12,8},{16,12},{20,16},{24,20},{28,24},{5,1},{9,5},{13... | collective-permute-start | bytes 18440 | tf_op jit(solution)/shard_map/ppermute | solution.py:37
  4.7 5.3 %collective-permute-start.1 = (f32[12,1,128]{2,1,0:T(1,128)S(1)}, f32[12,1,128]{2,1,0:T(1,128)S(1)}, u32[]{:S(2)}, u32[]{:S(2)}) collective-permute-start(f32[12,1,128]{2,1,0:T(1,128)S(1)} %get-tuple-element.91), channel_id=1, source_target_pairs={{0,4},{4,8},{8,12},{12,16},{16,20},{20,24},{24,28},{1,5},{5,9},{9,... | collective-permute-start | bytes 18440 | tf_op jit(solution)/shard_map/ppermute | solution.py:36
  10.4 7.3 %collective-permute-start.2 = (f32[12,66,1]{1,2,0:T(1,128)S(1)}, f32[12,66,1]{1,2,0:T(1,128)S(1)}, u32[]{:S(2)}, u32[]{:S(2)}) collective-permute-start(f32[12,66,1]{1,2,0:T(1,128)S(1)} %copy.45), channel_id=1, source_target_pairs={{1,0},{2,1},{3,2},{5,4},{6,5},{7,6},{9,8},{10,9},{11,10},{13,12},{... | collective-permute-start | bytes 9512 | tf_op jit(solution)/shard_map/ppermute | solution.py:37
  14.7 3.8 %collective-permute-start.3 = (f32[12,66,1]{1,2,0:T(1,128)S(1)}, f32[12,66,1]{1,2,0:T(1,128)S(1)}, u32[]{:S(2)}, u32[]{:S(2)}) collective-permute-start(f32[12,66,1]{1,2,0:T(1,128)S(1)} %copy.47), channel_id=1, source_target_pairs={{0,1},{1,2},{2,3},{4,5},{5,6},{6,7},{8,9},{9,10},{10,11},{12,13},{... | collective-permute-start | bytes 9512 | tf_op jit(solution)/shard_map/ppermute | solution.py:36
  22.2 5.8 %collective-permute-start.5 = (f32[16,8,128]{2,0,1:T(8,128)S(1)}, f32[16,8,128]{2,0,1:T(8,128)S(1)}, u32[]{:S(2)}, u32[]{:S(2)}) collective-permute-start(f32[16,8,128]{2,0,1:T(8,128)S(1)} %get-tuple-element.60), channel_id=1, source_target_pairs={{4,0},{8,4},{12,8},{16,12},{20,16},{24,20},{28,24},{5,1},{9,5},{13... | collective-permute-start | bytes 196616 | tf_op jit(solution)/shard_map/ppermute | solution.py:37
  24.2 6.7 %collective-permute-start.4 = (f32[16,8,128]{2,0,1:T(8,128)S(1)}, f32[16,8,128]{2,0,1:T(8,128)S(1)}, u32[]{:S(2)}, u32[]{:S(2)}) collective-permute-start(f32[16,8,128]{2,0,1:T(8,128)S(1)} %get-tuple-element.59), channel_id=1, source_target_pairs={{0,4},{4,8},{8,12},{12,16},{16,20},{20,24},{24,28},{1,5},{5,9},{9,... | collective-permute-start | bytes 196616 | tf_op jit(solution)/shard_map/ppermute | solution.py:36
  32.0 11.4 %collective-permute-start.7 = (f32[16,64,8]{2,1,0:T(8,128)S(1)}, f32[16,64,8]{2,1,0:T(8,128)S(1)}, u32[]{:S(2)}, u32[]{:S(2)}) collective-permute-start(f32[16,64,8]{2,1,0:T(8,128)S(1)} %get-tuple-element.58), channel_id=1, source_target_pairs={{1,0},{2,1},{3,2},{5,4},{6,5},{7,6},{9,8},{10,9},{11,10},{13,12},{... | collective-permute-start | bytes 98312 | tf_op jit(solution)/shard_map/ppermute | solution.py:37
  34.3 10.2 %collective-permute-start.6 = (f32[16,64,8]{2,1,0:T(8,128)S(1)}, f32[16,64,8]{2,1,0:T(8,128)S(1)}, u32[]{:S(2)}, u32[]{:S(2)}) collective-permute-start(f32[16,64,8]{2,1,0:T(8,128)S(1)} %get-tuple-element.57), channel_id=1, source_target_pairs={{0,1},{1,2},{2,3},{4,5},{5,6},{6,7},{8,9},{9,10},{10,11},{12,13},{... | collective-permute-start | bytes 98312 | tf_op jit(solution)/shard_map/ppermute | solution.py:36
  46.4 5.3 %collective-permute-start.8 = (f32[1,128]{1,0:T(1,128)S(1)}, f32[1,128]{1,0:T(1,128)S(1)}, u32[]{:S(2)}, u32[]{:S(2)}) collective-permute-start(f32[1,128]{1,0:T(1,128)S(1)} %get-tuple-element.113), channel_id=1, source_target_pairs={{4,0},{8,4},{12,8},{16,12},{20,16},{24,20},{28,24},{5,1},{9,5},{13... | collective-permute-start | bytes 1544 | tf_op jit(solution)/shard_map/ppermute | solution.py:37
  49.0 5.2 %collective-permute-start.9 = (f32[1,128]{1,0:T(1,128)S(1)}, f32[1,128]{1,0:T(1,128)S(1)}, u32[]{:S(2)}, u32[]{:S(2)}) collective-permute-start(f32[1,128]{1,0:T(1,128)S(1)} %get-tuple-element.112), channel_id=1, source_target_pairs={{0,4},{4,8},{8,12},{12,16},{16,20},{20,24},{24,28},{1,5},{5,9},{9,... | collective-permute-start | bytes 1544 | tf_op jit(solution)/shard_map/ppermute | solution.py:36
  54.3 7.8 %collective-permute-start.10 = (f32[66,1]{1,0:T(8,128)S(1)}, f32[66,1]{1,0:T(8,128)S(1)}, u32[]{:S(2)}, u32[]{:S(2)}) collective-permute-start(f32[66,1]{1,0:T(8,128)S(1)} %get-tuple-element.100), channel_id=1, source_target_pairs={{1,0},{2,1},{3,2},{5,4},{6,5},{7,6},{9,8},{10,9},{11,10},{13,12},{... | collective-permute-start | bytes 800 | tf_op jit(solution)/shard_map/ppermute | solution.py:37
  56.2 6.9 %collective-permute-start.11 = (f32[66,1]{1,0:T(8,128)S(1)}, f32[66,1]{1,0:T(8,128)S(1)}, u32[]{:S(2)}, u32[]{:S(2)}) collective-permute-start(f32[66,1]{1,0:T(8,128)S(1)} %get-tuple-element.101), channel_id=1, source_target_pairs={{0,1},{1,2},{2,3},{4,5},{5,6},{6,7},{8,9},{9,10},{10,11},{12,13},{... | collective-permute-start | bytes 800 | tf_op jit(solution)/shard_map/ppermute | solution.py:36
  64.0 5.3 %collective-permute-start.12 = (f32[12,1,128]{2,1,0:T(1,128)S(1)}, f32[12,1,128]{2,1,0:T(1,128)S(1)}, u32[]{:S(2)}, u32[]{:S(2)}) collective-permute-start(f32[12,1,128]{2,1,0:T(1,128)S(1)} %get-tuple-element.86), channel_id=1, source_target_pairs={{4,0},{8,4},{12,8},{16,12},{20,16},{24,20},{28,24},{5,1},{9,5},{13... | collective-permute-start | bytes 18440 | tf_op jit(solution)/shard_map/ppermute | solution.py:37
  66.0 5.3 %collective-permute-start.13 = (f32[12,1,128]{2,1,0:T(1,128)S(1)}, f32[12,1,128]{2,1,0:T(1,128)S(1)}, u32[]{:S(2)}, u32[]{:S(2)}) collective-permute-start(f32[12,1,128]{2,1,0:T(1,128)S(1)} %get-tuple-element.85), channel_id=1, source_target_pairs={{0,4},{4,8},{8,12},{12,16},{16,20},{20,24},{24,28},{1,5},{5,9},{9,... | collective-permute-start | bytes 18440 | tf_op jit(solution)/shard_map/ppermute | solution.py:36
  71.7 7.6 %collective-permute-start.14 = (f32[12,66,1]{1,2,0:T(1,128)S(1)}, f32[12,66,1]{1,2,0:T(1,128)S(1)}, u32[]{:S(2)}, u32[]{:S(2)}) collective-permute-start(f32[12,66,1]{1,2,0:T(1,128)S(1)} %copy.51), channel_id=1, source_target_pairs={{1,0},{2,1},{3,2},{5,4},{6,5},{7,6},{9,8},{10,9},{11,10},{13,12},{... | collective-permute-start | bytes 9512 | tf_op jit(solution)/shard_map/ppermute | solution.py:37
  73.8 6.1 %collective-permute-start.15 = (f32[12,66,1]{1,2,0:T(1,128)S(1)}, f32[12,66,1]{1,2,0:T(1,128)S(1)}, u32[]{:S(2)}, u32[]{:S(2)}) collective-permute-start(f32[12,66,1]{1,2,0:T(1,128)S(1)} %copy.53), channel_id=1, source_target_pairs={{0,1},{1,2},{2,3},{4,5},{5,6},{6,7},{8,9},{9,10},{10,11},{12,13},{... | collective-permute-start | bytes 9512 | tf_op jit(solution)/shard_map/ppermute | solution.py:36
  82.4 5.4 %collective-permute-start.17 = (f32[16,8,128]{2,0,1:T(8,128)S(1)}, f32[16,8,128]{2,0,1:T(8,128)S(1)}, u32[]{:S(2)}, u32[]{:S(2)}) collective-permute-start(f32[16,8,128]{2,0,1:T(8,128)S(1)} %get-tuple-element.56), channel_id=1, source_target_pairs={{4,0},{8,4},{12,8},{16,12},{20,16},{24,20},{28,24},{5,1},{9,5},{13... | collective-permute-start | bytes 196616 | tf_op jit(solution)/shard_map/ppermute | solution.py:37
  85.0 5.9 %collective-permute-start.16 = (f32[16,8,128]{2,0,1:T(8,128)S(1)}, f32[16,8,128]{2,0,1:T(8,128)S(1)}, u32[]{:S(2)}, u32[]{:S(2)}) collective-permute-start(f32[16,8,128]{2,0,1:T(8,128)S(1)} %get-tuple-element.55), channel_id=1, source_target_pairs={{0,4},{4,8},{8,12},{12,16},{16,20},{20,24},{24,28},{1,5},{5,9},{9,... | collective-permute-start | bytes 196616 | tf_op jit(solution)/shard_map/ppermute | solution.py:36
  92.0 12.5 %collective-permute-start.19 = (f32[16,64,8]{2,1,0:T(8,128)S(1)}, f32[16,64,8]{2,1,0:T(8,128)S(1)}, u32[]{:S(2)}, u32[]{:S(2)}) collective-permute-start(f32[16,64,8]{2,1,0:T(8,128)S(1)} %get-tuple-element.54), channel_id=1, source_target_pairs={{1,0},{2,1},{3,2},{5,4},{6,5},{7,6},{9,8},{10,9},{11,10},{13,12},{... | collective-permute-start | bytes 98312 | tf_op jit(solution)/shard_map/ppermute | solution.py:37
  94.0 11.7 %collective-permute-start.18 = (f32[16,64,8]{2,1,0:T(8,128)S(1)}, f32[16,64,8]{2,1,0:T(8,128)S(1)}, u32[]{:S(2)}, u32[]{:S(2)}) collective-permute-start(f32[16,64,8]{2,1,0:T(8,128)S(1)} %get-tuple-element.53), channel_id=1, source_target_pairs={{0,1},{1,2},{2,3},{4,5},{5,6},{6,7},{8,9},{9,10},{10,11},{12,13},{... | collective-permute-start | bytes 98312 | tf_op jit(solution)/shard_map/ppermute | solution.py:36
  106.9 5.3 %collective-permute-start.20 = (f32[1,128]{1,0:T(1,128)S(1)}, f32[1,128]{1,0:T(1,128)S(1)}, u32[]{:S(2)}, u32[]{:S(2)}) collective-permute-start(f32[1,128]{1,0:T(1,128)S(1)} %get-tuple-element.111), channel_id=1, source_target_pairs={{4,0},{8,4},{12,8},{16,12},{20,16},{24,20},{28,24},{5,1},{9,5},{13... | collective-permute-start | bytes 1544 | tf_op jit(solution)/shard_map/ppermute | solution.py:37
  108.8 5.2 %collective-permute-start.21 = (f32[1,128]{1,0:T(1,128)S(1)}, f32[1,128]{1,0:T(1,128)S(1)}, u32[]{:S(2)}, u32[]{:S(2)}) collective-permute-start(f32[1,128]{1,0:T(1,128)S(1)} %get-tuple-element.110), channel_id=1, source_target_pairs={{0,4},{4,8},{8,12},{12,16},{16,20},{20,24},{24,28},{1,5},{5,9},{9,... | collective-permute-start | bytes 1544 | tf_op jit(solution)/shard_map/ppermute | solution.py:36
  114.1 7.5 %collective-permute-start.22 = (f32[66,1]{1,0:T(8,128)S(1)}, f32[66,1]{1,0:T(8,128)S(1)}, u32[]{:S(2)}, u32[]{:S(2)}) collective-permute-start(f32[66,1]{1,0:T(8,128)S(1)} %get-tuple-element.98), channel_id=1, source_target_pairs={{1,0},{2,1},{3,2},{5,4},{6,5},{7,6},{9,8},{10,9},{11,10},{13,12},{... | collective-permute-start | bytes 800 | tf_op jit(solution)/shard_map/ppermute | solution.py:37
  116.0 6.6 %collective-permute-start.23 = (f32[66,1]{1,0:T(8,128)S(1)}, f32[66,1]{1,0:T(8,128)S(1)}, u32[]{:S(2)}, u32[]{:S(2)}) collective-permute-start(f32[66,1]{1,0:T(8,128)S(1)} %get-tuple-element.99), channel_id=1, source_target_pairs={{0,1},{1,2},{2,3},{4,5},{5,6},{6,7},{8,9},{9,10},{10,11},{12,13},{... | collective-permute-start | bytes 800 | tf_op jit(solution)/shard_map/ppermute | solution.py:36
  (11 other events, 27.8 us)
where the time goes:
time: 125 us; the launch traced here: 124 us
  starting transfers between devices  75.2 us (60%)
  waiting for transfers between devices  29.3 us (23%)
  local copies, waits for them, and re-layouts  7.25 us (6%)
  matrix products  5.88 us (5%)
  other arithmetic  4.35 us (3%)
  between operations  1.58 us (1%)
    ppermute x12, starting transfers between devices, with_halo(): before = lax.ppermute(last, axis, up)  47.1 us
    ppermute x12, starting transfers between devices, with_halo(): after = lax.ppermute(first, axis, down)  28 us
    ppermute x12, waiting for transfers between devices, with_halo(): before = lax.ppermute(last, axis, up)  19.1 us
    ppermute x12, waiting for transfers between devices, with_halo(): after = lax.ppermute(first, axis, down)  10.3 us
    unnamed x31, local copies, waits for them, and re-layouts  3.71 us
  transfers between devices with their start and end apart: 24, of which 15 were waited for; matrix products, arithmetic and copies ran while one was open for 2% of the time, Pallas kernels for 0%

commit v1 on v0

v1 whole, which is shorter than its diff:
```python
import functools

import jax
import jax.numpy as jnp
from jax import lax
from jax.experimental import pallas as pl
from jax.experimental.pallas import tpu as pltpu
from jax.sharding import PartitionSpec as P

RADIUS = 8
CX, CY = 64, 128
WIDE, NEAR = 20, 11
PAD = 24
ROWS = CX + 2 * PAD
OFF = 8
HELD = ROWS + 2 * OFF
LANES = 128
SLAB = 224
K_STIFF = (1.0, 1.0, 0.0, 0.5, 0.5, 0.2)
VISCOUS = 0.2
KEEP = 0.95
DT = 0.4
ALONG = ((2, 3, 1.0, 0.8), (1, 5, 1.0, 0.3))
ACROSS = ((2, 4, 1.0, 0.8), (0, 5, -1.0, 0.3))
STEP_ROWS = ((0, 112, 8, 104, 8, 104), (8, 104, 16, 96, 24, 88))
F32, BF16 = jnp.float32, jnp.bfloat16


def halo_of(field):
    return WIDE if field < 6 else NEAR


def slab_start(field):
    return WIDE * field if field < 6 else 6 * WIDE + NEAR * (field - 6)


def swap(block, axis):
    count = lax.axis_size(axis)
    out = []
    for first, part in zip((0, 1), block):
        pairs = []
        for i in range(first, count - 1, 2):
            pairs += [(i, i + 1), (i + 1, i)]
        out.append(lax.ppermute(part, axis, pairs))
    return out


def pack_kernel(flaw, disp, vel, dam, stren, con, out_a, out_b, lim):
    node = lax.broadcasted_iota(jnp.int32, (CX, CY), 0) * CY + lax.broadcasted_iota(
        jnp.int32, (CX, CY), 1
    )
    mark = node == flaw[0, 0, 0]
    for j in range(1, flaw.shape[2]):
        mark = mark | (node == flaw[0, 0, j])
    lim[...] = stren[...] * jnp.where(mark, 0.4, 1.0)

    def field(k, rows):
        if k < 6:
            return disp[k, rows, :]
        if k < 12:
            return vel[k - 6, rows, :]
        if k == 12:
            return dam[rows, :]
        if k == 13:
            return lim[rows, :]
        return con[rows, :].astype(F32)

    def fill(out, top):
        for k in range(15):
            width = halo_of(k)
            rows = slice(0, width) if top else slice(CX - width, CX)
            start = slab_start(k)
            out[start : start + width, :] = field(k, rows)
        out[219:SLAB, :] = jnp.zeros((SLAB - 219, LANES), F32)

    even = lax.rem(lax.axis_index("transit"), 2) == 0

    @pl.when(even)
    def _():
        fill(out_a, False)
        fill(out_b, True)

    @pl.when(jnp.logical_not(even))
    def _():
        fill(out_a, True)
        fill(out_b, False)


def assemble(ext, disp, vel, dam, lim, con, got_a, got_b):
    even = lax.rem(lax.axis_index("transit"), 2) == 0
    for k in range(15):
        width, start = halo_of(k), slab_start(k)
        part_a = got_a[start : start + width, :]
        part_b = got_b[start : start + width, :]
        if k < 6:
            own = disp[k]
        elif k < 12:
            own = vel[k - 6]
        else:
            own = (dam, lim, con)[k - 12][...].astype(F32)
        low, high = OFF + PAD, OFF + PAD + CX
        ext[k, 0 : low - width, :] = jnp.zeros((low - width, LANES), F32)
        ext[k, low - width : low, :] = jnp.where(even, part_b, part_a)
        ext[k, low:high, :] = own
        ext[k, high : high + width, :] = jnp.where(even, part_a, part_b)
        ext[k, high + width : HELD, :] = jnp.zeros((HELD - high - width, LANES), F32)


def edge_kernel(disp, vel, dam, lim, con, got_a, got_b, out_a, out_b, ext):
    assemble(ext, disp, vel, dam, lim, con, got_a, got_b)
    lane = lax.broadcasted_iota(jnp.int32, (ROWS, LANES), 1)
    even = lax.rem(lax.axis_index("lateral"), 2) == 0
    for tile, fields in ((0, range(6)), (1, range(6, 15))):
        right = left = jnp.zeros((ROWS, LANES), F32)
        for n, k in enumerate(fields):
            width = halo_of(k)
            here = (lane >= n * width) & (lane < (n + 1) * width)
            block = ext[k, OFF : OFF + ROWS, :]
            right = jnp.where(here, pltpu.roll(block, (n * width - (CY - width)) % LANES, 1), right)
            left = jnp.where(here, pltpu.roll(block, n * width, 1) if n else block, left)
        cols = slice(tile * LANES, (tile + 1) * LANES)
        out_a[:, cols] = jnp.where(even, right, left)
        out_b[:, cols] = jnp.where(even, left, right)


def split(x):
    high = x.astype(BF16)
    return high, (x - high.astype(F32)).astype(BF16)


def step_kernel(
    disp, vel, dam, lim, con, got_a, got_b, side_a, side_b,
    along_1, along_2, across_hi, across_lo, cover, decay, rate,
    out_u, out_v, out_d,
    ext, ext2, mid, wp, fm, hd, energy, t_hi, t_lo, aver,
):
    assemble(ext.at[0], disp, vel, dam, lim, con, got_a, got_b)
    lane8 = lax.broadcasted_iota(jnp.int32, (8, LANES), 1)
    lane = lax.broadcasted_iota(jnp.int32, (ROWS, LANES), 1)
    even = lax.rem(lax.axis_index("lateral"), 2) == 0
    for tile, fields in ((0, range(6)), (1, range(6, 15))):
        cols = slice(tile * LANES, (tile + 1) * LANES)
        right = jnp.where(even, side_a[:, cols], side_b[:, cols])
        left = jnp.where(even, side_b[:, cols], side_a[:, cols])
        for n, k in enumerate(fields):
            width = halo_of(k)
            from_right = pltpu.roll(right, (-n * width) % LANES, 1) if n else right
            from_left = pltpu.roll(left, (CY - width - n * width) % LANES, 1)
            ext[1, k, 0:OFF, :] = jnp.zeros((OFF, LANES), F32)
            ext[1, k, OFF : OFF + ROWS, :] = jnp.where(lane < 64, from_right, from_left)
            ext[1, k, OFF + ROWS : HELD, :] = jnp.zeros((OFF, LANES), F32)
    for tile in range(2):
        for k in range(12):
            for low in (0, OFF + 104):
                ext2[tile, k, low : low + 16, :] = jnp.zeros((16, LANES), F32)
        for low in (0, HELD - 16):
            hd[tile, low : low + 16, :] = jnp.full((16, LANES), 0.5, F32)

    def after(pair):
        last = lax.broadcasted_iota(jnp.int32, pair[0].shape, 1) == LANES - 1
        r0, r1 = (pltpu.roll(x, LANES - 1, 1) for x in pair)
        return jnp.where(last, r1, r0), jnp.where(last, r0, r1)

    def before(pair):
        first = lax.broadcasted_iota(jnp.int32, pair[0].shape, 1) == 0
        r0, r1 = (pltpu.roll(x, 1, 1) for x in pair)
        return jnp.where(first, r1, r0), jnp.where(first, r0, r1)

    state, after_state = ext, ext2
    for step, (e0, e1, d0, d1, f0, f1) in enumerate(STEP_ROWS):
        last_step = step == 1
        span = e1 - e0
        for b in range(e0, e1, 16):
            def rows(k, shift=0):
                return tuple(state[tile, k, OFF + b + shift : OFF + b + shift + 16, :] for tile in range(2))
            here = [rows(k) for k in range(6)]
            dx = [tuple(p - m for p, m in zip(rows(k, 1), rows(k, -1))) for k in range(5)]
            dy = [tuple(p - m for p, m in zip(after(here[k]), before(here[k]))) for k in range(5)]
            for tile in range(2):
                x = [v[tile] for v in dx]
                y = [v[tile] for v in dy]
                c = [v[tile] for v in here]
                plane = (x[0], y[1], y[0] + x[1])
                bend = (x[3], y[4], y[3] + x[4])
                e7 = x[2] - 2.0 * c[3]
                e8 = y[2] - 2.0 * c[4]
                e9 = 0.5 * (x[1] - y[0]) - 2.0 * c[5]
                prods = []
                for p, q in zip(plane, bend):
                    prods += [p * p, p * q, q * q]
                prods += [e7 * e7, e8 * e8, e9 * e9]
                for ch, value in enumerate(prods):
                    high, low = split(value)
                    cols = slice(tile * LANES, (tile + 1) * LANES)
                    energy[ch, b - e0 : b - e0 + 16, cols] = high
                    energy[ch, span + b - e0 : span + b - e0 + 16, cols] = low
        band = along_2 if last_step else along_1
        n_out = d1 - d0
        for ch in range(12):
            both = jnp.dot(band[...], energy[ch, 0 : 2 * span, :], preferred_element_type=F32)
            high, low = split(both[:n_out] + both[n_out:])
            t_hi[ch * n_out : (ch + 1) * n_out, :] = high
            t_lo[ch * n_out : (ch + 1) * n_out, :] = low
        total = 12 * n_out
        aver[0:total, :] = (
            jnp.dot(t_hi[0:total, :], across_hi[...], preferred_element_type=F32)
            + jnp.dot(t_lo[0:total, :], across_hi[...], preferred_element_type=F32)
            + jnp.dot(t_hi[0:total, :], across_lo[...], preferred_element_type=F32)
        )
        for b in range(d0, d1, 8):
            for tile in range(2):
                cols = slice(tile * LANES, (tile + 1) * LANES)
                at = slice(OFF + b, OFF + b + 8)
                def mean(ch):
                    start = ch * n_out + b - d0
                    return aver[start : start + 8, cols]
                level = state[tile, 13, at, :] if step == 0 else ext[tile, 13, at, :]
                level = level * cover[b : b + 8, cols]
                driving = jnp.zeros((8, LANES), F32)
                for comp, threshold in enumerate((0.6, 0.6, 1.2)):
                    p, q, r = (mean(3 * comp + n) for n in range(3))
                    base = p - threshold * level
                    for depth in (0.75, 0.25):
                        centre = base + (depth * depth) * r
                        swing = (2.0 * depth) * q
                        driving += jnp.maximum(centre + swing, 0.0) + jnp.maximum(centre - swing, 0.0)
                    if comp == 2:
                        driving += jnp.maximum(r - level, 0.0)
                for ch, threshold in ((9, 1.5), (10, 1.5), (11, 1.2)):
                    driving += jnp.maximum(mean(ch) - threshold * level, 0.0)
                new = jnp.maximum(
                    ext[tile, 12, at, :], 1.0 - jnp.exp(driving * decay[b : b + 8, cols])
                )
                ext[tile, 12, at, :] = new
                hd[tile, at, :] = 0.5 - 0.5 * new
                if last_step and tile == 0 and PAD <= b < PAD + CX:
                    out_d[b - PAD : b - PAD + 8, :] = new
        for b in range(f0 - 8, f1 + 8, 8):
            at = slice(OFF + b, OFF + b + 8)
            for tile in range(2):
                u = [state[tile, k, at, :] for k in range(6)]
                v = [state[tile, 6 + k, at, :] for k in range(6)]
                for k in range(6):
                    value = VISCOUS * v[k]
                    if K_STIFF[k] == 1.0:
                        value = u[k] + value
                    elif K_STIFF[k]:
                        value = K_STIFF[k] * u[k] + value
                    wp[tile, k, at, :] = value
                for n, (lead, turn, sign, _) in enumerate(ALONG):
                    wp[tile, 6 + n, at, :] = sign * u[lead] - 0.5 * u[turn]
        for b in range(f0 - 8, f1, 8):
            at = slice(OFF + b, OFF + b + 8)
            nxt = slice(OFF + b + 1, OFF + b + 9)
            prv = slice(OFF + b - 1, OFF + b + 7)

            def fluxes(base, gammas, s, pairs):
                plus, minus = list(base), list(base)
                for gamma, (lead, turn, sign, stiff) in zip(gammas, pairs):
                    plus[lead] = minus[lead] = base[lead] + (sign * stiff) * gamma
                    half = (0.5 * stiff) * gamma
                    plus[turn], minus[turn] = base[turn] + half, base[turn] - half
                out_p = [s * x for x in plus]
                out_m = [out_p[k] if plus[k] is minus[k] else s * minus[k] for k in range(6)]
                return out_p, out_m

            force = [None, None]
            for tile in range(2):
                if last_step and tile == 1:
                    continue
                u = {k: state[tile, k, at, :] for k in (1, 2, 3, 5)}
                base = [wp[tile, k, nxt, :] - wp[tile, k, at, :] for k in range(6)]
                gammas = [
                    wp[tile, 6 + n, nxt, :] - (sign * u[lead] + 0.5 * u[turn])
                    for n, (lead, turn, sign, _) in enumerate(ALONG)
                ]
                s = hd[tile, at, :] + hd[tile, nxt, :]
                plus, minus = fluxes(base, gammas, s, ALONG)
                for k in range(6):
                    fm[tile, k, at, :] = minus[k]
                if b >= f0:
                    force[tile] = [plus[k] - fm[tile, k, prv, :] for k in range(6)]
            if b < f0:
                continue
            u = [[state[tile, k, at, :] for k in range(6)] for tile in range(2)]
            w = [[wp[tile, k, at, :] for k in range(6)] for tile in range(2)]
            w_next = [after((w[0][k], w[1][k])) for k in range(6)]
            p_next = [
                after(tuple(sign * u[tile][lead] - 0.5 * u[tile][turn] for tile in range(2)))
                for lead, turn, sign, _ in ACROSS
            ]
            h = tuple(hd[tile, at, :] for tile in range(2))
            h_next = after(h)
            plus, minus = [], []
            for tile in range(2):
                base = [w_next[k][tile] - w[tile][k] for k in range(6)]
                gammas = [
                    p_next[n][tile] - (sign * u[tile][lead] + 0.5 * u[tile][turn])
                    for n, (lead, turn, sign, _) in enumerate(ACROSS)
                ]
                one_p, one_m = fluxes(base, gammas, h[tile] + h_next[tile], ACROSS)
                plus.append(one_p)
                minus.append(one_m)
            minus_prev = [before((minus[0][k], minus[1][k])) for k in range(6)]
            for tile in range(2):
                if last_step and tile == 1:
                    continue
                cols = slice(tile * LANES, (tile + 1) * LANES)
                dt = rate[b : b + 8, cols]
                total = [force[tile][k] + plus[tile][k] - minus_prev[k][tile] for k in range(6)]
                grip = 2.0 * ext[tile, 14, at, :]
                total[0] = total[0] + grip * (1.5 - u[tile][0])
                total[2] = total[2] + grip * (-0.5 - u[tile][2])
                for k in range(6):
                    v_new = KEEP * state[tile, 6 + k, at, :] + dt * total[k]
                    u_new = u[tile][k] + dt * v_new
                    if last_step:
                        out_v[k, b - PAD : b - PAD + 8, :] = v_new
                        out_u[k, b - PAD : b - PAD + 8, :] = u_new
                    else:
                        after_state[tile, 6 + k, at, :] = v_new
                        after_state[tile, k, at, :] = u_new
        state = ext2


def tables(count_x, count_y):
    pos_x = jnp.arange(ROWS) + lax.axis_index("transit") * CX - PAD
    in_x = (pos_x >= 0) & (pos_x < count_x)
    ring = jnp.arange(2 * LANES)
    pos_y = lax.axis_index("lateral") * CY + jnp.where(ring < 192, ring, ring - 2 * LANES)
    in_y = (pos_y >= 0) & (pos_y < count_y)

    def weight(offset, inside):
        dist = offset.astype(F32)
        return jnp.where((jnp.abs(offset) <= RADIUS) & inside, jnp.exp(-dist * dist / 32.0), 0.0)

    row = jnp.arange(ROWS)
    along = weight(row[None, :] - row[:, None], in_x[None, :])
    across = weight((ring[:, None] - ring[None, :] + LANES) % (2 * LANES) - LANES, in_y[:, None])
    cover = jnp.sum(along, 1)[:, None] * jnp.sum(across, 0)[None, :]
    inside = in_x[:, None] & in_y[None, :]
    cover = jnp.where(inside, cover, 1.0)
    decay = jnp.where(inside, -1.0 / (24.0 * cover), 0.0)
    rate = jnp.where(inside, DT, 0.0)

    def parts(x):
        high = lax.reduce_precision(x, 8, 7)
        return high.astype(BF16), (x - high).astype(BF16)

    bands = []
    for e0, e1, d0, d1, _, _ in STEP_ROWS:
        high, low = parts(along[d0:d1, e0:e1])
        bands.append(jnp.concatenate([jnp.concatenate([high, high], 1), jnp.concatenate([low, low], 1)], 0))
    high, low = parts(across)
    return bands + [high, low, 4.0 * cover, decay, rate]


def vmem(n):
    return [pl.BlockSpec(memory_space=pltpu.VMEM)] * n


def on_device(displacement, velocity, damage, strength, contact, flaw_cells):
    params = pltpu.CompilerParams(vmem_limit_bytes=48 * 1024 * 1024)
    shape = jax.ShapeDtypeStruct
    send_a, send_b, limit = pl.pallas_call(
        pack_kernel,
        out_shape=[shape((SLAB, LANES), F32)] * 2 + [shape((CX, CY), F32)],
        in_specs=[pl.BlockSpec(memory_space=pltpu.SMEM)] + vmem(5),
        out_specs=vmem(3),
        compiler_params=params,
        name="pack_rows",
    )(flaw_cells, displacement, velocity, damage, strength, contact)
    got = swap((send_a, send_b), "transit")
    own = (displacement, velocity, damage, limit, contact)
    side = pl.pallas_call(
        edge_kernel,
        out_shape=[shape((ROWS, 2 * LANES), F32)] * 2,
        in_specs=vmem(7),
        out_specs=vmem(2),
        scratch_shapes=[pltpu.VMEM((15, HELD, LANES), F32)],
        compiler_params=params,
        name="pack_columns",
    )(*own, *got)
    side = swap(side, "lateral")
    table = tables(CX * lax.axis_size("transit"), CY * lax.axis_size("lateral"))
    out = pl.pallas_call(
        step_kernel,
        out_shape=[shape((6, CX, CY), F32)] * 2 + [shape((CX, CY), F32)],
        in_specs=vmem(16),
        out_specs=vmem(3),
        scratch_shapes=[
            pltpu.VMEM((2, 15, HELD, LANES), F32),
            pltpu.VMEM((2, 12, HELD, LANES), F32),
            pltpu.VMEM((8, LANES), F32),
            pltpu.VMEM((2, 8, HELD, LANES), F32),
            pltpu.VMEM((2, 6, HELD, LANES), F32),
            pltpu.VMEM((2, HELD, LANES), F32),
            pltpu.VMEM((12, 2 * ROWS, 2 * LANES), BF16),
            pltpu.VMEM((12 * 96, 2 * LANES), BF16),
            pltpu.VMEM((12 * 96, 2 * LANES), BF16),
            pltpu.VMEM((12 * 96, 2 * LANES), F32),
        ],
        compiler_params=params,
        name="two_steps",
    )(*own, *got, *side, *table)
    return tuple(out)


def solution(mesh):
    return jax.shard_map(
        on_device,
        mesh=mesh,
        in_specs=(
            P(None, "transit", "lateral"),
            P(None, "transit", "lateral"),
            P("transit", "lateral"),
            P("transit", "lateral"),
            P("transit", "lateral"),
            P("transit", "lateral", None),
        ),
        out_specs=(
            P(None, "transit", "lateral"),
            P(None, "transit", "lateral"),
            P("transit", "lateral"),
        ),
        check_vma=False,
    )
```

time: 125 us -> 28 us (0.22)
  starting transfers between devices: 75.2 us -> 8.5 us
  waiting for transfers between devices: 29.3 us -> 6.56 us
  Pallas kernels: 0 us -> 6.17 us
  matrix products: 5.88 us -> 0 us
  other arithmetic: 4.35 us -> 0.81 us
  local copies, waits for them, and re-layouts: 7.25 us -> 4.8 us
    ppermute x24 -> x4, starting transfers between devices: 75.2 us -> 8.5 us  [swap(): out.append(lax.ppermute(part, axis, pairs))]
    ppermute x24 -> x4, waiting for transfers between devices: 29.3 us -> 6.56 us  [swap(): out.append(lax.ppermute(part, axis, pairs))]
    pallas_call x0 -> x3, Pallas kernels: none -> 6.17 us  [the longest x1 5.01 us: on_device(): pl.pallas_call(step_kernel, out_shape=[shape((6, CX, CY), F32)] * 2 + [sh...]
    dot_general x8 -> x0, matrix products: 5.88 us -> none  [the longest x2 2.29 us: across_product(): jnp.einsum('kinj,mj->kinm', windows, band, precision=lax.Precision.HIGHEST)]
    slice x15 -> x0, local copies, waits for them, and re-layouts: 1.76 us -> none  [the longest x6 0.92 us: with_halo(): first = lax.slice_in_dim(shard, 0, width, axis=dim)]
    unnamed x31 -> x20, local copies, waits for them, and re-layouts: 3.71 us -> 4.8 us
  transfers between devices with their start and end apart: 24 -> 4, of which waited for: 15 -> 2; matrix products, arithmetic and copies ran while one was open for 2% -> 3% of each run, Pallas kernels for 0% -> 0%
where the time goes in v1:
time: 28 us; the launch traced here: 27.6 us
  starting transfers between devices  8.5 us (30%)
  waiting for transfers between devices  6.56 us (23%)
  Pallas kernels  6.17 us (22%)
  local copies, waits for them, and re-layouts  4.8 us (17%)
  other arithmetic  0.81 us (3%)
  between operations  0.8 us (3%)
    ppermute x4, starting transfers between devices, swap(): out.append(lax.ppermute(part, axis, pairs))  8.5 us
    ppermute x4, waiting for transfers between devices, swap(): out.append(lax.ppermute(part, axis, pairs))  6.56 us
    pallas_call x1, Pallas kernels, on_device(): pl.pallas_call(step_kernel, out_shape=[shape((6, CX, CY), F32)] * 2 + [sh...  5.01 us
    unnamed x20, local copies, waits for them, and re-layouts  4.8 us
    pallas_call x1, Pallas kernels, on_device(): pl.pallas_call(pack_kernel, out_shape=[shape((SLAB, LANES), F32)] * 2 + [...  0.68 us
  transfers between devices with their start and end apart: 4, of which 2 were waited for; matrix products, arithmetic and copies ran while one was open for 3% of the time, Pallas kernels for 0%

profile of v1, /device:TPU:25, one launch (start us, length us, event | category | flops | bytes accessed | tf_op | source)
XLA Modules:
  0.0 27.6 jit_solution(6674835489991139009)
XLA Ops:
  0.6 0.0 copy-start
  0.6 0.9 %copy-done = f32[6,64,128]{2,1,0:T(8,128)S(1)} copy-done((f32[6,64,128]{2,1,0:T(8,128)S(1)}, f32[6,64,128]{2,1,0:T(8,128)}, u32[]{:S(2)}) %copy-start) | copy-done | bytes 196632
  1.6 0.9 %copy-done.2 = f32[6,64,128]{2,1,0:T(8,128)S(1)} copy-done((f32[6,64,128]{2,1,0:T(8,128)S(1)}, f32[6,64,128]{2,1,0:T(8,128)}, u32[]{:S(2)}) %copy-start.2) | copy-done | bytes 196632
  2.5 0.8 %copy-done.4 = f32[64,128]{1,0:T(8,128)S(1)} copy-done((f32[64,128]{1,0:T(8,128)S(1)}, f32[64,128]{1,0:T(8,128)}, u32[]{:S(2)}) %copy-start.4) | copy-done | bytes 32792
  3.2 0.8 %copy-done.6 = s32[64,128]{1,0:T(8,128)S(1)} copy-done((s32[64,128]{1,0:T(8,128)S(1)}, s32[64,128]{1,0:T(8,128)}, u32[]{:S(2)}) %copy-start.6) | copy-done | bytes 32792
  4.0 0.8 %copy-done.8 = f32[64,128]{1,0:T(8,128)S(1)} copy-done((f32[64,128]{1,0:T(8,128)S(1)}, f32[64,128]{1,0:T(8,128)}, u32[]{:S(2)}) %copy-start.8) | copy-done | bytes 32792
  4.8 0.7 %copy-done.9 = s32[1,1,32]{2,1,0:T(1,128)S(1)} copy-done((s32[1,1,32]{2,1,0:T(1,128)S(1)}, s32[1,1,32]{2,1,0:T(1,128)}, u32[]{:S(2)}) %copy-start.9) | copy-done | bytes 152
  5.4 0.7 %pack_rows.1 = (f32[224,128]{1,0:T(8,128)S(1)}, f32[224,128]{1,0:T(8,128)S(1)}, f32[64,128]{1,0:T(8,128)S(1)}) custom-call(s32[1,1,32]{2,1,0:T(1,128)S(1)} %copy-done.9, f32[6,64,128]{2,1,0:T(8,128)S(1)} %copy-done, f32[6,64,128]{2,1,0:T(8,128)S(1)} %copy-done.2, f32[64,128]{1,0:T(8,128)S(1)} %copy-done.4, f32[64,128]{1,0:T(8,128)S(1)} %copy-done.8, ...), custom_call_target="tpu_custom_call" | custom-call | tf_op jit(solution)/shard_map/pack_rows/pallas_call | solution.py:365
  6.1 1.3 %collective-permute-start = (f32[224,128]{1,0:T(8,128)S(1)}, f32[224,128]{1,0:T(8,128)S(1)}, u32[]{:S(2)}, u32[]{:S(2)}) collective-permute-start(f32[224,128]{1,0:T(8,128)S(1)} %get-tuple-element.9), channel_id=1, source_target_pairs={{0,4},{4,0},{8,12},{12,8},{16,20},{20,16},{24,28},{28,24},{1,5},{5... | collective-permute-start | bytes 344072 | tf_op jit(solution)/shard_map/ppermute | solution.py:44
  7.4 2.0 %collective-permute-start.1 = (f32[224,128]{1,0:T(8,128)S(1)}, f32[224,128]{1,0:T(8,128)S(1)}, u32[]{:S(2)}, u32[]{:S(2)}) collective-permute-start(f32[224,128]{1,0:T(8,128)S(1)} %get-tuple-element.10), channel_id=1, source_target_pairs={{4,8},{8,4},{12,16},{16,12},{20,24},{24,20},{5,9},{9,5},{13,17},{1... | collective-permute-start | bytes 344072 | tf_op jit(solution)/shard_map/ppermute | solution.py:44
  9.5 0.1 fusion.15
  9.6 0.3 fusion.7
  9.9 0.0 copy-start.3
  9.9 0.1 and_select_fusion.1
  10.0 0.1 reduce-precision_convert_fusion.2
  10.1 0.0 copy-start.7
  10.1 0.1 maximum_maximum_fusion.1.along_2
  10.3 3.6 %collective-permute-done.1.got_b = f32[224,128]{1,0:T(8,128)S(1)} collective-permute-done((f32[224,128]{1,0:T(8,128)S(1)}, f32[224,128]{1,0:T(8,128)S(1)}, u32[]{:S(2)}, u32[]{:S(2)}) %collective-permute-start.1) | collective-permute-done | bytes 114720 | tf_op jit(solution)/shard_map/ppermute | solution.py:44
  13.9 0.5 %pack_columns.1 = (f32[112,256]{1,0:T(8,128)S(1)}, f32[112,256]{1,0:T(8,128)S(1)}) custom-call(f32[6,64,128]{2,1,0:T(8,128)S(1)} %copy-done.1, f32[6,64,128]{2,1,0:T(8,128)S(1)} %copy-done.3, f32[64,128]{1,0:T(8,128)S(1)} %copy-done.5, f32[64,128]{1,0:T(8,128)S(1)} %get-tuple-element.8.lim, s32[64,128]{1,0:T(8,128)S(1)} %copy-done.7, ...), custom_call_target="tpu_custom_call" | custom-call | tf_op jit(solution)/shard_map/pack_columns/pallas_call | solution.py:375
  14.4 2.2 %collective-permute-start.2 = (f32[112,256]{1,0:T(8,128)S(1)}, f32[112,256]{1,0:T(8,128)S(1)}, u32[]{:S(2)}, u32[]{:S(2)}) collective-permute-start(f32[112,256]{1,0:T(8,128)S(1)} %get-tuple-element.11), channel_id=1, source_target_pairs={{0,1},{1,0},{2,3},{3,2},{4,5},{5,4},{6,7},{7,6},{8,9},{9,8},{10,11... | collective-permute-start | bytes 344072 | tf_op jit(solution)/shard_map/ppermute | solution.py:44
  16.5 3.0 %collective-permute-start.3 = (f32[112,256]{1,0:T(8,128)S(1)}, f32[112,256]{1,0:T(8,128)S(1)}, u32[]{:S(2)}, u32[]{:S(2)}) collective-permute-start(f32[112,256]{1,0:T(8,128)S(1)} %get-tuple-element.12), channel_id=1, source_target_pairs={{1,2},{2,1},{5,6},{6,5},{9,10},{10,9},{13,14},{14,13},{17,18},{18,... | collective-permute-start | bytes 344072 | tf_op jit(solution)/shard_map/ppermute | solution.py:44
  19.6 0.1 maximum_maximum_fusion.along_1
  19.7 3.0 %collective-permute-done.3.side_b = f32[112,256]{1,0:T(8,128)S(1)} collective-permute-done((f32[112,256]{1,0:T(8,128)S(1)}, f32[112,256]{1,0:T(8,128)S(1)}, u32[]{:S(2)}, u32[]{:S(2)}) %collective-permute-start.3) | collective-permute-done | bytes 114720 | tf_op jit(solution)/shard_map/ppermute | solution.py:44
  22.6 5.0 %two_steps.1 = (f32[6,64,128]{2,1,0:T(8,128)}, f32[6,64,128]{2,1,0:T(8,128)}, f32[64,128]{1,0:T(8,128)}) custom-call(f32[6,64,128]{2,1,0:T(8,128)S(1)} %copy-done.1, f32[6,64,128]{2,1,0:T(8,128)S(1)} %copy-done.3, f32[64,128]{1,0:T(8,128)S(1)} %copy-done.5, f32[64,128]{1,0:T(8,128)S(1)} %get-tuple-element.8.lim, s32[64,128]{1,0:T(8,128)S(1)} %copy-done.7, ...), custom_call_target="tpu_custom_call" | custom-call | tf_op jit(solution)/shard_map/two_steps/pallas_call | solution.py:386
  (16 shorter events, 0.1 us)
Async XLA Ops:
  0.6 0.9 %copy-start = (f32[6,64,128]{2,1,0:T(8,128)S(1)}, f32[6,64,128]{2,1,0:T(8,128)}, u32[]{:S(2)}) copy-start(f32[6,64,128]{2,1,0:T(8,128)} %disp.5) | copy-start | bytes 589828
  1.6 0.9 %copy-start.2 = (f32[6,64,128]{2,1,0:T(8,128)S(1)}, f32[6,64,128]{2,1,0:T(8,128)}, u32[]{:S(2)}) copy-start(f32[6,64,128]{2,1,0:T(8,128)} %vel.5) | copy-start | bytes 589828
  2.5 0.8 %copy-start.4 = (f32[64,128]{1,0:T(8,128)S(1)}, f32[64,128]{1,0:T(8,128)}, u32[]{:S(2)}) copy-start(f32[64,128]{1,0:T(8,128)} %dam.5) | copy-start | bytes 98308
  3.2 0.8 %copy-start.6 = (s32[64,128]{1,0:T(8,128)S(1)}, s32[64,128]{1,0:T(8,128)}, u32[]{:S(2)}) copy-start(s32[64,128]{1,0:T(8,128)} %con.5) | copy-start | bytes 98308
  4.0 0.8 %copy-start.8 = (f32[64,128]{1,0:T(8,128)S(1)}, f32[64,128]{1,0:T(8,128)}, u32[]{:S(2)}) copy-start(f32[64,128]{1,0:T(8,128)} %stren.1) | copy-start | bytes 98308
  4.8 0.7 %copy-start.9 = (s32[1,1,32]{2,1,0:T(1,128)S(1)}, s32[1,1,32]{2,1,0:T(1,128)}, u32[]{:S(2)}) copy-start(s32[1,1,32]{2,1,0:T(1,128)} %flaw.1) | copy-start | bytes 388
  6.1 4.1 %collective-permute-start = (f32[224,128]{1,0:T(8,128)S(1)}, f32[224,128]{1,0:T(8,128)S(1)}, u32[]{:S(2)}, u32[]{:S(2)}) collective-permute-start(f32[224,128]{1,0:T(8,128)S(1)} %get-tuple-element.9), channel_id=1, source_target_pairs={{0,4},{4,0},{8,12},{12,8},{16,20},{20,16},{24,28},{28,24},{1,5},{5... | collective-permute-start | bytes 344072 | tf_op jit(solution)/shard_map/ppermute | solution.py:44
  7.4 6.4 %collective-permute-start.1 = (f32[224,128]{1,0:T(8,128)S(1)}, f32[224,128]{1,0:T(8,128)S(1)}, u32[]{:S(2)}, u32[]{:S(2)}) collective-permute-start(f32[224,128]{1,0:T(8,128)S(1)} %get-tuple-element.10), channel_id=1, source_target_pairs={{4,8},{8,4},{12,16},{16,12},{20,24},{24,20},{5,9},{9,5},{13,17},{1... | collective-permute-start | bytes 344072 | tf_op jit(solution)/shard_map/ppermute | solution.py:44
  9.9 4.0 %copy-start.1 = (f32[6,64,128]{2,1,0:T(8,128)S(1)}, f32[6,64,128]{2,1,0:T(8,128)}, u32[]{:S(2)}) copy-start(f32[6,64,128]{2,1,0:T(8,128)} %disp.5) | copy-start | bytes 589828
  9.9 4.0 %copy-start.3 = (f32[6,64,128]{2,1,0:T(8,128)S(1)}, f32[6,64,128]{2,1,0:T(8,128)}, u32[]{:S(2)}) copy-start(f32[6,64,128]{2,1,0:T(8,128)} %vel.5) | copy-start | bytes 589828
  10.1 3.7 %copy-start.5 = (f32[64,128]{1,0:T(8,128)S(1)}, f32[64,128]{1,0:T(8,128)}, u32[]{:S(2)}) copy-start(f32[64,128]{1,0:T(8,128)} %dam.5) | copy-start | bytes 98308
  10.1 3.7 %copy-start.7 = (s32[64,128]{1,0:T(8,128)S(1)}, s32[64,128]{1,0:T(8,128)}, u32[]{:S(2)}) copy-start(s32[64,128]{1,0:T(8,128)} %con.5) | copy-start | bytes 98308
  14.4 5.3 %collective-permute-start.2 = (f32[112,256]{1,0:T(8,128)S(1)}, f32[112,256]{1,0:T(8,128)S(1)}, u32[]{:S(2)}, u32[]{:S(2)}) collective-permute-start(f32[112,256]{1,0:T(8,128)S(1)} %get-tuple-element.11), channel_id=1, source_target_pairs={{0,1},{1,0},{2,3},{3,2},{4,5},{5,4},{6,7},{7,6},{8,9},{9,8},{10,11... | collective-permute-start | bytes 344072 | tf_op jit(solution)/shard_map/ppermute | solution.py:44
  16.5 6.1 %collective-permute-start.3 = (f32[112,256]{1,0:T(8,128)S(1)}, f32[112,256]{1,0:T(8,128)S(1)}, u32[]{:S(2)}, u32[]{:S(2)}) collective-permute-start(f32[112,256]{1,0:T(8,128)S(1)} %get-tuple-element.12), channel_id=1, source_target_pairs={{1,2},{2,1},{5,6},{6,5},{9,10},{10,9},{13,14},{14,13},{17,18},{18,... | collective-permute-start | bytes 344072 | tf_op jit(solution)/shard_map/ppermute | solution.py:44

commit v2 on v1

--- a/solution.py
+++ b/solution.py
@@ -45,7 +45,19 @@
     return out
 
 
-def pack_kernel(flaw, disp, vel, dam, stren, con, out_a, out_b, lim):
+def pack_kernel(
+    flaw_in, disp_in, vel_in, dam_in, stren_in, con_in,
+    out_a, out_b, disp, vel, dam, lim, con, stren, flaw, sems,
+):
+    sources = (flaw_in, disp_in, vel_in, dam_in, stren_in, con_in)
+    copies = [
+        pltpu.make_async_copy(src, dst, sems.at[n])
+        for n, (src, dst) in enumerate(zip(sources, (flaw, disp, vel, dam, stren, con)))
+    ]
+    for copy in copies:
+        copy.start()
+    for copy in copies:
+        copy.wait()
     node = lax.broadcasted_iota(jnp.int32, (CX, CY), 0) * CY + lax.broadcasted_iota(
         jnp.int32, (CX, CY), 1
     )
@@ -362,16 +374,23 @@
 def on_device(displacement, velocity, damage, strength, contact, flaw_cells):
     params = pltpu.CompilerParams(vmem_limit_bytes=48 * 1024 * 1024)
     shape = jax.ShapeDtypeStruct
-    send_a, send_b, limit = pl.pallas_call(
+    tile = shape((CX, CY), F32)
+    send_a, send_b, *own = pl.pallas_call(
         pack_kernel,
-        out_shape=[shape((SLAB, LANES), F32)] * 2 + [shape((CX, CY), F32)],
-        in_specs=[pl.BlockSpec(memory_space=pltpu.SMEM)] + vmem(5),
-        out_specs=vmem(3),
+        out_shape=[shape((SLAB, LANES), F32)] * 2
+        + [shape((6, CX, CY), F32)] * 2
+        + [tile, tile, shape((CX, CY), jnp.int32)],
+        in_specs=[pl.BlockSpec(memory_space=pltpu.HBM)] * 6,
+        out_specs=vmem(7),
+        scratch_shapes=[
+            pltpu.VMEM((CX, CY), F32),
+            pltpu.SMEM(flaw_cells.shape, jnp.int32),
+            pltpu.SemaphoreType.DMA((6,)),
+        ],
         compiler_params=params,
         name="pack_rows",
-    )(flaw_cells, displacement, velocity, damage, strength, contact)
+    )(*(pltpu.with_memory_space_constraint(x, pltpu.HBM) for x in (flaw_cells, displacement, velocity, damage, strength, contact)))
     got = swap((send_a, send_b), "transit")
-    own = (displacement, velocity, damage, limit, contact)
     side = pl.pallas_call(
         edge_kernel,
         out_shape=[shape((ROWS, 2 * LANES), F32)] * 2,

time: 28 us -> 23.6 us (0.84)
  local copies, waits for them, and re-layouts: 4.8 us -> 0 us
  Pallas kernels: 6.17 us -> 6.71 us
    unnamed x20 -> x0, local copies, waits for them, and re-layouts: 4.8 us -> none
    pallas_call x1, Pallas kernels: 0.68 us -> 1.22 us  [on_device(): pl.pallas_call(pack_kernel, out_shape=[shape((SLAB, LANES), F32)] * 2 + [...]
where the time goes in v2:
time: 23.6 us; the launch traced here: 23.4 us
  starting transfers between devices  8.5 us (36%)
  Pallas kernels  6.71 us (28%)
  waiting for transfers between devices  6.61 us (28%)
  other arithmetic  0.8 us (3%)
  between operations  0.74 us (3%)
    ppermute x4, starting transfers between devices, swap(): out.append(lax.ppermute(part, axis, pairs))  8.5 us
    ppermute x4, waiting for transfers between devices, swap(): out.append(lax.ppermute(part, axis, pairs))  6.61 us
    pallas_call x1, Pallas kernels, on_device(): pl.pallas_call(step_kernel, out_shape=[shape((6, CX, CY), F32)] * 2 + [sh...  5.01 us
    pallas_call x1, Pallas kernels, on_device(): pl.pallas_call(pack_kernel, out_shape=[shape((SLAB, LANES), F32)] * 2 + [...  1.22 us
    pallas_call x1, Pallas kernels, on_device(): pl.pallas_call(edge_kernel, out_shape=[shape((ROWS, 2 * LANES), F32)] * 2...  0.48 us
  transfers between devices with their start and end apart: 4, of which 2 were waited for; matrix products, arithmetic and copies ran while one was open for 3% of the time, Pallas kernels for 0%

profile of v2, /device:TPU:25, one launch (start us, length us, event | category | flops | bytes accessed | tf_op | source)
XLA Modules:
  0.0 23.4 jit_solution(18334287710941569737)
XLA Ops:
  0.6 1.2 %pack_rows.1 = (f32[224,128]{1,0:T(8,128)S(1)}, f32[224,128]{1,0:T(8,128)S(1)}, f32[6,64,128]{2,1,0:T(8,128)S(1)}, f32[6,64,128]{2,1,0:T(8,128)S(1)}, f32[64,128...) custom-call(s32[1,1,32]{2,1,0:T(1,128)} %flaw_in.1, f32[6,64,128]{2,1,0:T(8,128)} %disp_in.1, ...), custom_call_target="tpu_custom_call" | custom-call | tf_op jit(solution)/shard_map/pack_rows/pallas_call | solution.py:378
  1.9 1.3 %collective-permute-start = (f32[224,128]{1,0:T(8,128)S(1)}, f32[224,128]{1,0:T(8,128)S(1)}, u32[]{:S(2)}, u32[]{:S(2)}) collective-permute-start(f32[224,128]{1,0:T(8,128)S(1)} %get-tuple-element.17), channel_id=1, source_target_pairs={{0,4},{4,0},{8,12},{12,8},{16,20},{20,16},{24,28},{28,24},{1,5},{5... | collective-permute-start | bytes 344072 | tf_op jit(solution)/shard_map/ppermute | solution.py:44
  3.2 2.0 %collective-permute-start.1 = (f32[224,128]{1,0:T(8,128)S(1)}, f32[224,128]{1,0:T(8,128)S(1)}, u32[]{:S(2)}, u32[]{:S(2)}) collective-permute-start(f32[224,128]{1,0:T(8,128)S(1)} %get-tuple-element.18), channel_id=1, source_target_pairs={{4,8},{8,4},{12,16},{16,12},{20,24},{24,20},{5,9},{9,5},{13,17},{1... | collective-permute-start | bytes 344072 | tf_op jit(solution)/shard_map/ppermute | solution.py:44
  5.2 0.1 fusion.15
  5.4 0.3 %fusion.7 = (f32[256]{0:T(256)S(1)}, bf16[256,256]{1,0:T(8,128)(2,1)S(1)}, bf16[256,256]{1,0:T(8,128)(2,1)S(1)}) fusion(pred[256]{0:T(512)(128)(4,1)S(1)} %compare_and_fusion), kind=kLoop, calls=%fused_computation.17 | loop fusion | flops 1769216 | bytes 263424 | tf_op jit(solution)/shard_map/reduce_sum | solution.py:352
  5.6 0.1 and_select_fusion.1
  5.8 0.1 reduce-precision_convert_fusion.2
  5.8 0.1 maximum_maximum_fusion.1.along_2
  5.9 0.0 collective-permute-done.got_a
  6.0 3.7 %collective-permute-done.1.got_b = f32[224,128]{1,0:T(8,128)S(1)} collective-permute-done((f32[224,128]{1,0:T(8,128)S(1)}, f32[224,128]{1,0:T(8,128)S(1)}, u32[]{:S(2)}, u32[]{:S(2)}) %collective-permute-start.1) | collective-permute-done | bytes 114720 | tf_op jit(solution)/shard_map/ppermute | solution.py:44
  9.6 0.5 %pack_columns.1 = (f32[112,256]{1,0:T(8,128)S(1)}, f32[112,256]{1,0:T(8,128)S(1)}) custom-call(f32[6,64,128]{2,1,0:T(8,128)S(1)} %get-tuple-element.12.disp, f32[6,64,128]{2,1,0:T(8,128)S(1)} %get-tuple-element.13.vel, f32[64,128]{1,0:T(8,128)S(1)} %get-tuple-element.14.dam, f32[64,128]{1,0:T(8,128)S(1)} %get-tuple-element.15.lim, ...), custom_call_target="tpu_custom_call" | custom-call | tf_op jit(solution)/shard_map/pack_columns/pallas_call | solution.py:394
  10.1 2.2 %collective-permute-start.2 = (f32[112,256]{1,0:T(8,128)S(1)}, f32[112,256]{1,0:T(8,128)S(1)}, u32[]{:S(2)}, u32[]{:S(2)}) collective-permute-start(f32[112,256]{1,0:T(8,128)S(1)} %get-tuple-element.19), channel_id=1, source_target_pairs={{0,1},{1,0},{2,3},{3,2},{4,5},{5,4},{6,7},{7,6},{8,9},{9,8},{10,11... | collective-permute-start | bytes 344072 | tf_op jit(solution)/shard_map/ppermute | solution.py:44
  12.3 3.0 %collective-permute-start.3 = (f32[112,256]{1,0:T(8,128)S(1)}, f32[112,256]{1,0:T(8,128)S(1)}, u32[]{:S(2)}, u32[]{:S(2)}) collective-permute-start(f32[112,256]{1,0:T(8,128)S(1)} %get-tuple-element.20), channel_id=1, source_target_pairs={{1,2},{2,1},{5,6},{6,5},{9,10},{10,9},{13,14},{14,13},{17,18},{18,... | collective-permute-start | bytes 344072 | tf_op jit(solution)/shard_map/ppermute | solution.py:44
  15.3 0.1 maximum_maximum_fusion.along_1
  15.4 0.0 collective-permute-done.2.side_a
  15.4 3.0 %collective-permute-done.3.side_b = f32[112,256]{1,0:T(8,128)S(1)} collective-permute-done((f32[112,256]{1,0:T(8,128)S(1)}, f32[112,256]{1,0:T(8,128)S(1)}, u32[]{:S(2)}, u32[]{:S(2)}) %collective-permute-start.3) | collective-permute-done | bytes 114720 | tf_op jit(solution)/shard_map/ppermute | solution.py:44
  18.4 5.0 %two_steps.1 = (f32[6,64,128]{2,1,0:T(8,128)}, f32[6,64,128]{2,1,0:T(8,128)}, f32[64,128]{1,0:T(8,128)}) custom-call(f32[6,64,128]{2,1,0:T(8,128)S(1)} %get-tuple-element.12.disp, f32[6,64,128]{2,1,0:T(8,128)S(1)} %get-tuple-element.13.vel, f32[64,128]{1,0:T(8,128)S(1)} %get-tuple-element.14.dam, f32[64,128]{1,0:T(8,128)S(1)} %get-tuple-element.15.lim, ...), custom_call_target="tpu_custom_call" | custom-call | tf_op jit(solution)/shard_map/two_steps/pallas_call | solution.py:405
  (3 shorter events, 0.0 us)
Async XLA Ops:
  1.9 4.1 %collective-permute-start = (f32[224,128]{1,0:T(8,128)S(1)}, f32[224,128]{1,0:T(8,128)S(1)}, u32[]{:S(2)}, u32[]{:S(2)}) collective-permute-start(f32[224,128]{1,0:T(8,128)S(1)} %get-tuple-element.17), channel_id=1, source_target_pairs={{0,4},{4,0},{8,12},{12,8},{16,20},{20,16},{24,28},{28,24},{1,5},{5... | collective-permute-start | bytes 344072 | tf_op jit(solution)/shard_map/ppermute | solution.py:44
  3.2 6.4 %collective-permute-start.1 = (f32[224,128]{1,0:T(8,128)S(1)}, f32[224,128]{1,0:T(8,128)S(1)}, u32[]{:S(2)}, u32[]{:S(2)}) collective-permute-start(f32[224,128]{1,0:T(8,128)S(1)} %get-tuple-element.18), channel_id=1, source_target_pairs={{4,8},{8,4},{12,16},{16,12},{20,24},{24,20},{5,9},{9,5},{13,17},{1... | collective-permute-start | bytes 344072 | tf_op jit(solution)/shard_map/ppermute | solution.py:44
  10.1 5.3 %collective-permute-start.2 = (f32[112,256]{1,0:T(8,128)S(1)}, f32[112,256]{1,0:T(8,128)S(1)}, u32[]{:S(2)}, u32[]{:S(2)}) collective-permute-start(f32[112,256]{1,0:T(8,128)S(1)} %get-tuple-element.19), channel_id=1, source_target_pairs={{0,1},{1,0},{2,3},{3,2},{4,5},{5,4},{6,7},{7,6},{8,9},{9,8},{10,11... | collective-permute-start | bytes 344072 | tf_op jit(solution)/shard_map/ppermute | solution.py:44
  12.3 6.1 %collective-permute-start.3 = (f32[112,256]{1,0:T(8,128)S(1)}, f32[112,256]{1,0:T(8,128)S(1)}, u32[]{:S(2)}, u32[]{:S(2)}) collective-permute-start(f32[112,256]{1,0:T(8,128)S(1)} %get-tuple-element.20), channel_id=1, source_target_pairs={{1,2},{2,1},{5,6},{6,5},{9,10},{10,9},{13,14},{14,13},{17,18},{18,... | collective-permute-start | bytes 344072 | tf_op jit(solution)/shard_map/ppermute | solution.py:44

commit v3 on v2

--- a/solution.py
+++ b/solution.py
@@ -141,7 +141,7 @@
 
 
 def step_kernel(
-    disp, vel, dam, lim, con, got_a, got_b, side_a, side_b,
+    disp, vel, dam, lim, con, got_a, got_b, side_b, side_a,
     along_1, along_2, across_hi, across_lo, cover, decay, rate,
     out_u, out_v, out_d,
     ext, ext2, mid, wp, fm, hd, energy, t_hi, t_lo, aver,
@@ -421,7 +421,7 @@
         ],
         compiler_params=params,
         name="two_steps",
-    )(*own, *got, *side, *table)
+    )(*own, *got, *side[::-1], *table)
     return tuple(out)
 
 

time: 23.6 us -> 22.9 us (0.970)
  waiting for transfers between devices: 6.61 us -> 5.93 us
    ppermute x4, waiting for transfers between devices: 6.61 us -> 5.93 us  [swap(): out.append(lax.ppermute(part, axis, pairs))]
  transfers between devices with their start and end apart: 4 -> 4, of which waited for: 2 -> 2; matrix products, arithmetic and copies ran while one was open for 3% -> 4% of each run, Pallas kernels for 0% -> 0%
where the time goes in v3:
time: 22.9 us; the launch traced here: 22.7 us
  starting transfers between devices  8.49 us (37%)
  Pallas kernels  6.71 us (29%)
  waiting for transfers between devices  5.93 us (26%)
  other arithmetic  0.8 us (3%)
  between operations  0.74 us (3%)
    ppermute x4, starting transfers between devices, swap(): out.append(lax.ppermute(part, axis, pairs))  8.49 us
    ppermute x4, waiting for transfers between devices, swap(): out.append(lax.ppermute(part, axis, pairs))  5.93 us
    pallas_call x1, Pallas kernels, on_device(): pl.pallas_call(step_kernel, out_shape=[shape((6, CX, CY), F32)] * 2 + [sh...  5.01 us
    pallas_call x1, Pallas kernels, on_device(): pl.pallas_call(pack_kernel, out_shape=[shape((SLAB, LANES), F32)] * 2 + [...  1.22 us
    pallas_call x1, Pallas kernels, on_device(): pl.pallas_call(edge_kernel, out_shape=[shape((ROWS, 2 * LANES), F32)] * 2...  0.48 us
  transfers between devices with their start and end apart: 4, of which 2 were waited for; matrix products, arithmetic and copies ran while one was open for 4% of the time, Pallas kernels for 0%

profile of v3, /device:TPU:25, one launch (start us, length us, event | category | flops | bytes accessed | tf_op | source)
XLA Modules:
  0.0 22.7 jit_solution(16671982193303400088)
XLA Ops:
  0.6 1.2 %pack_rows.1 = (f32[224,128]{1,0:T(8,128)S(1)}, f32[224,128]{1,0:T(8,128)S(1)}, f32[6,64,128]{2,1,0:T(8,128)S(1)}, f32[6,64,128]{2,1,0:T(8,128)S(1)}, f32[64,128...) custom-call(s32[1,1,32]{2,1,0:T(1,128)} %flaw_in.1, f32[6,64,128]{2,1,0:T(8,128)} %disp_in.1, ...), custom_call_target="tpu_custom_call" | custom-call | tf_op jit(solution)/shard_map/pack_rows/pallas_call | solution.py:378
  1.9 1.3 %collective-permute-start = (f32[224,128]{1,0:T(8,128)S(1)}, f32[224,128]{1,0:T(8,128)S(1)}, u32[]{:S(2)}, u32[]{:S(2)}) collective-permute-start(f32[224,128]{1,0:T(8,128)S(1)} %get-tuple-element.17), channel_id=1, source_target_pairs={{0,4},{4,0},{8,12},{12,8},{16,20},{20,16},{24,28},{28,24},{1,5},{5... | collective-permute-start | bytes 344072 | tf_op jit(solution)/shard_map/ppermute | solution.py:44
  3.2 2.0 %collective-permute-start.1 = (f32[224,128]{1,0:T(8,128)S(1)}, f32[224,128]{1,0:T(8,128)S(1)}, u32[]{:S(2)}, u32[]{:S(2)}) collective-permute-start(f32[224,128]{1,0:T(8,128)S(1)} %get-tuple-element.18), channel_id=1, source_target_pairs={{4,8},{8,4},{12,16},{16,12},{20,24},{24,20},{5,9},{9,5},{13,17},{1... | collective-permute-start | bytes 344072 | tf_op jit(solution)/shard_map/ppermute | solution.py:44
  5.2 0.1 fusion.15
  5.4 0.3 %fusion.7 = (f32[256]{0:T(256)S(1)}, bf16[256,256]{1,0:T(8,128)(2,1)S(1)}, bf16[256,256]{1,0:T(8,128)(2,1)S(1)}) fusion(pred[256]{0:T(512)(128)(4,1)S(1)} %compare_and_fusion), kind=kLoop, calls=%fused_computation.17 | loop fusion | flops 1769216 | bytes 263424 | tf_op jit(solution)/shard_map/reduce_sum | solution.py:352
  5.6 0.1 and_select_fusion.1
  5.8 0.1 reduce-precision_convert_fusion.2
  5.8 0.1 maximum_maximum_fusion.1.along_2
  5.9 0.0 collective-permute-done.got_a
  6.0 3.7 %collective-permute-done.1.got_b = f32[224,128]{1,0:T(8,128)S(1)} collective-permute-done((f32[224,128]{1,0:T(8,128)S(1)}, f32[224,128]{1,0:T(8,128)S(1)}, u32[]{:S(2)}, u32[]{:S(2)}) %collective-permute-start.1) | collective-permute-done | bytes 114720 | tf_op jit(solution)/shard_map/ppermute | solution.py:44
  9.6 0.5 %pack_columns.1 = (f32[112,256]{1,0:T(8,128)S(1)}, f32[112,256]{1,0:T(8,128)S(1)}) custom-call(f32[6,64,128]{2,1,0:T(8,128)S(1)} %get-tuple-element.12.disp, f32[6,64,128]{2,1,0:T(8,128)S(1)} %get-tuple-element.13.vel, f32[64,128]{1,0:T(8,128)S(1)} %get-tuple-element.14.dam, f32[64,128]{1,0:T(8,128)S(1)} %get-tuple-element.15.lim, ...), custom_call_target="tpu_custom_call" | custom-call | tf_op jit(solution)/shard_map/pack_columns/pallas_call | solution.py:394
  10.1 5.1 %collective-permute-start.2 = (f32[112,256]{1,0:T(8,128)S(1)}, f32[112,256]{1,0:T(8,128)S(1)}, u32[]{:S(2)}, u32[]{:S(2)}) collective-permute-start(f32[112,256]{1,0:T(8,128)S(1)} %get-tuple-element.19), channel_id=1, source_target_pairs={{1,2},{2,1},{5,6},{6,5},{9,10},{10,9},{13,14},{14,13},{17,18},{18,... | collective-permute-start | bytes 344072 | tf_op jit(solution)/shard_map/ppermute | solution.py:44
  15.2 0.1 collective-permute-start.3
  15.3 0.1 maximum_maximum_fusion.along_1
  15.4 2.3 %collective-permute-done.2.side_b = f32[112,256]{1,0:T(8,128)S(1)} collective-permute-done((f32[112,256]{1,0:T(8,128)S(1)}, f32[112,256]{1,0:T(8,128)S(1)}, u32[]{:S(2)}, u32[]{:S(2)}) %collective-permute-start.2) | collective-permute-done | bytes 114720 | tf_op jit(solution)/shard_map/ppermute | solution.py:44
  17.7 0.0 collective-permute-done.3.side_a
  17.7 5.0 %two_steps.1 = (f32[6,64,128]{2,1,0:T(8,128)}, f32[6,64,128]{2,1,0:T(8,128)}, f32[64,128]{1,0:T(8,128)}) custom-call(f32[6,64,128]{2,1,0:T(8,128)S(1)} %get-tuple-element.12.disp, f32[6,64,128]{2,1,0:T(8,128)S(1)} %get-tuple-element.13.vel, f32[64,128]{1,0:T(8,128)S(1)} %get-tuple-element.14.dam, f32[64,128]{1,0:T(8,128)S(1)} %get-tuple-element.15.lim, ...), custom_call_target="tpu_custom_call" | custom-call | tf_op jit(solution)/shard_map/two_steps/pallas_call | solution.py:405
  (3 shorter events, 0.0 us)
Async XLA Ops:
  1.9 4.1 %collective-permute-start = (f32[224,128]{1,0:T(8,128)S(1)}, f32[224,128]{1,0:T(8,128)S(1)}, u32[]{:S(2)}, u32[]{:S(2)}) collective-permute-start(f32[224,128]{1,0:T(8,128)S(1)} %get-tuple-element.17), channel_id=1, source_target_pairs={{0,4},{4,0},{8,12},{12,8},{16,20},{20,16},{24,28},{28,24},{1,5},{5... | collective-permute-start | bytes 344072 | tf_op jit(solution)/shard_map/ppermute | solution.py:44
  3.2 6.4 %collective-permute-start.1 = (f32[224,128]{1,0:T(8,128)S(1)}, f32[224,128]{1,0:T(8,128)S(1)}, u32[]{:S(2)}, u32[]{:S(2)}) collective-permute-start(f32[224,128]{1,0:T(8,128)S(1)} %get-tuple-element.18), channel_id=1, source_target_pairs={{4,8},{8,4},{12,16},{16,12},{20,24},{24,20},{5,9},{9,5},{13,17},{1... | collective-permute-start | bytes 344072 | tf_op jit(solution)/shard_map/ppermute | solution.py:44
  10.1 7.6 %collective-permute-start.2 = (f32[112,256]{1,0:T(8,128)S(1)}, f32[112,256]{1,0:T(8,128)S(1)}, u32[]{:S(2)}, u32[]{:S(2)}) collective-permute-start(f32[112,256]{1,0:T(8,128)S(1)} %get-tuple-element.19), channel_id=1, source_target_pairs={{1,2},{2,1},{5,6},{6,5},{9,10},{10,9},{13,14},{14,13},{17,18},{18,... | collective-permute-start | bytes 344072 | tf_op jit(solution)/shard_map/ppermute | solution.py:44
  15.2 2.5 %collective-permute-start.3 = (f32[112,256]{1,0:T(8,128)S(1)}, f32[112,256]{1,0:T(8,128)S(1)}, u32[]{:S(2)}, u32[]{:S(2)}) collective-permute-start(f32[112,256]{1,0:T(8,128)S(1)} %get-tuple-element.20), channel_id=1, source_target_pairs={{0,1},{1,0},{2,3},{3,2},{4,5},{5,4},{6,7},{7,6},{8,9},{9,8},{10,11... | collective-permute-start | bytes 344072 | tf_op jit(solution)/shard_map/ppermute | solution.py:44

commit v4 on v3

v4 whole, which is shorter than its diff:
```python
import functools

import jax
import jax.numpy as jnp
from jax import lax
from jax.experimental import pallas as pl
from jax.experimental.pallas import tpu as pltpu
from jax.sharding import PartitionSpec as P

RADIUS = 8
CX, CY = 64, 128
WIDE, NEAR = 20, 11
PAD = 24
EDGE = 32
SPAN = CY + 2 * EDGE
OFF = EDGE + 8
HELD = CY + 2 * OFF
LANES = 128
SLAB = 224
K_STIFF = (1.0, 1.0, 0.0, 0.5, 0.5, 0.2)
VISCOUS = 0.2
KEEP = 0.95
DT = 0.4
ALONG = ((2, 3, 1.0, 0.8), (1, 5, 1.0, 0.3))
ACROSS = ((2, 4, 1.0, 0.8), (0, 5, -1.0, 0.3))
F32, BF16 = jnp.float32, jnp.bfloat16


def halo_of(field):
    return WIDE if field < 6 else NEAR


def slab_start(field):
    return WIDE * field if field < 6 else 6 * WIDE + NEAR * (field - 6)


def swap(block, axis):
    count = lax.axis_size(axis)
    out = []
    for first, part in zip((0, 1), block):
        pairs = []
        for i in range(first, count - 1, 2):
            pairs += [(i, i + 1), (i + 1, i)]
        out.append(lax.ppermute(part, axis, pairs))
    return out


def pack_kernel(
    flaw_in, disp_in, vel_in, dam_in, stren_in, con_in,
    out_a, out_b, disp, vel, dam, lim, con, stren, flaw, sems,
):
    sources = (flaw_in, disp_in, vel_in, dam_in, stren_in, con_in)
    copies = [
        pltpu.make_async_copy(src, dst, sems.at[n])
        for n, (src, dst) in enumerate(zip(sources, (flaw, disp, vel, dam, stren, con)))
    ]
    for copy in copies:
        copy.start()
    for copy in copies:
        copy.wait()
    node = lax.broadcasted_iota(jnp.int32, (CX, CY), 0) * CY + lax.broadcasted_iota(
        jnp.int32, (CX, CY), 1
    )
    mark = node == flaw[0, 0, 0]
    for j in range(1, flaw.shape[2]):
        mark = mark | (node == flaw[0, 0, j])
    lim[...] = stren[...] * jnp.where(mark, 0.4, 1.0)

    def field(k, rows):
        if k < 6:
            return disp[k, rows, :]
        if k < 12:
            return vel[k - 6, rows, :]
        if k == 12:
            return dam[rows, :]
        if k == 13:
            return lim[rows, :]
        return con[rows, :].astype(F32)

    def fill(out, top):
        for k in range(15):
            width = halo_of(k)
            rows = slice(0, width) if top else slice(CX - width, CX)
            start = slab_start(k)
            out[start : start + width, :] = field(k, rows)
        out[219:SLAB, :] = jnp.zeros((SLAB - 219, LANES), F32)

    even = lax.rem(lax.axis_index("transit"), 2) == 0

    @pl.when(even)
    def _():
        fill(out_a, False)
        fill(out_b, True)

    @pl.when(jnp.logical_not(even))
    def _():
        fill(out_a, True)
        fill(out_b, False)


def edge_kernel(disp, vel, dam, lim, con, got_a, got_b, out_a, out_b, flat, ext):
    even = lax.rem(lax.axis_index("transit"), 2) == 0
    even_l = lax.rem(lax.axis_index("lateral"), 2) == 0
    for k in range(15):
        width, start = halo_of(k), slab_start(k)
        part_a = got_a[start : start + width, :]
        part_b = got_b[start : start + width, :]
        if k < 6:
            own = disp[k]
        elif k < 12:
            own = vel[k - 6]
        else:
            own = (dam, lim, con)[k - 12][...].astype(F32)
        low, high = PAD, PAD + CX
        ext[k, 0 : low - width, :] = jnp.zeros((low - width, LANES), F32)
        ext[k, low - width : low, :] = jnp.where(even, part_b, part_a)
        ext[k, low:high, :] = own
        ext[k, high : high + width, :] = jnp.where(even, part_a, part_b)
        ext[k, high + width : LANES, :] = jnp.zeros((LANES - high - width, LANES), F32)
        turned = ext[k].T
        flat[k, 8 : 8 + CY, :] = turned
        flat[k, 0:8, :] = jnp.zeros((8, LANES), F32)
        flat[k, 8 + CY : 16 + CY, :] = jnp.zeros((8, LANES), F32)
        right, left = turned[CY - width :, :], turned[:width, :]
        out_a[start : start + width, :] = jnp.where(even_l, right, left)
        out_b[start : start + width, :] = jnp.where(even_l, left, right)
    for out in (out_a, out_b):
        out[219:SLAB, :] = jnp.zeros((SLAB - 219, LANES), F32)


def split(x):
    high = x.astype(BF16)
    return high, (x - high.astype(F32)).astype(BF16)


def next_lane(x):
    return pltpu.roll(x, LANES - 1, 1)


def prev_lane(x):
    return pltpu.roll(x, 1, 1)


def products(get, put):
    c = [get(k, 0) for k in range(6)]
    x = [next_lane(c[k]) - prev_lane(c[k]) for k in range(5)]
    y = [get(k, 1) - get(k, -1) for k in range(5)]
    plane = (x[0], y[1], y[0] + x[1])
    bend = (x[3], y[4], y[3] + x[4])
    e7 = x[2] - 2.0 * c[3]
    e8 = y[2] - 2.0 * c[4]
    e9 = 0.5 * (x[1] - y[0]) - 2.0 * c[5]
    values = []
    for p, q in zip(plane, bend):
        values += [p * p, p * q, q * q]
    for ch, value in enumerate(values + [e7 * e7, e8 * e8, e9 * e9]):
        high, low = split(value)
        put(ch, slice(0, LANES), high)
        put(ch, slice(LANES, 2 * LANES), low)


def lane_sums(energy, turned, rows, band):
    for ch in range(12):
        both = jnp.dot(energy[ch, 0:rows, :], band[...], preferred_element_type=F32)
        high, low = split(both[:, :LANES] + both[:, LANES:])
        cols = slice(ch % 2 * LANES, (ch % 2 + 1) * LANES)
        turned[ch // 2, 0:rows, cols] = high
        turned[ch // 2, rows : 2 * rows, cols] = low


def row_sums(turned, pair, rows, first, second):
    return jnp.dot(first[...], turned[pair, 0 : 2 * rows, :], preferred_element_type=F32) + jnp.dot(
        second[...], turned[pair, 0:rows, :], preferred_element_type=F32
    )


def inner_kernel(flat, band, first, second, partial, energy, turned):
    for b in range(0, CY, 16):
        def get(k, shift):
            return flat[k, 8 + b + shift : 24 + b + shift, :]

        def put(ch, cols, value):
            energy[ch, b : b + 16, cols] = value

        products(get, put)
    lane_sums(energy, turned, CY, band)
    for pair in range(6):
        partial[pair] = row_sums(turned, pair, CY, first, second)


def step_kernel(
    flat, partial, side_b, side_a, band, rim_1, rim_2, all_1, all_2, cover, decay, rate,
    out_u, out_v, out_d,
    ext, ext2, wp, fm, hd, energy, turned, aver, final,
):
    even = lax.rem(lax.axis_index("lateral"), 2) == 0
    for k in range(15):
        width, start = halo_of(k), slab_start(k)
        part_a = side_a[start : start + width, :]
        part_b = side_b[start : start + width, :]
        ext[k, 0 : OFF - width, :] = jnp.zeros((OFF - width, LANES), F32)
        ext[k, OFF - width : OFF, :] = jnp.where(even, part_b, part_a)
        ext[k, OFF : OFF + CY, :] = flat[k, 8 : 8 + CY, :]
        ext[k, OFF + CY : OFF + CY + width, :] = jnp.where(even, part_a, part_b)
        ext[k, OFF + CY + width : HELD, :] = jnp.zeros((OFF - width, LANES), F32)
    for low in (-24, 144):
        for k in range(12):
            ext2[k, OFF + low : OFF + low + 8, :] = jnp.zeros((8, LANES), F32)
        hd[OFF + low : OFF + low + 8, :] = jnp.full((8, LANES), 0.5, F32)

    state = ext
    for last_step in (False, True):
        if last_step:
            starts, n_in, d0, d1, f0, f1 = range(-16, 144, 16), 160, -8, 136, 0, CY
        else:
            starts, n_in, d0, d1, f0, f1 = (-32, -16, 0, 112, 128, 144), 96, -16, 144, -16, 144
        for n, b in enumerate(starts):
            def get(k, shift):
                return state[k, OFF + b + shift : OFF + b + shift + 16, :]

            def put(ch, cols, value):
                energy[ch, 16 * n : 16 * n + 16, cols] = value

            products(get, put)
        lane_sums(energy, turned, n_in, band)
        n_out = d1 - d0
        for pair in range(6):
            if last_step:
                aver[pair, 0:n_out, :] = row_sums(turned, pair, n_in, all_1, all_2)
            else:
                aver[pair, 0:n_out, :] = partial[pair] + row_sums(turned, pair, n_in, rim_1, rim_2)
        for b in range(d0, d1, 8):
            at = slice(OFF + b, OFF + b + 8)
            tab = slice(EDGE + b, EDGE + b + 8)

            def mean(ch):
                cols = slice(ch % 2 * LANES, (ch % 2 + 1) * LANES)
                return aver[ch // 2, b - d0 : b - d0 + 8, cols]

            level = ext[13, at, :] * cover[tab, :]
            driving = jnp.zeros((8, LANES), F32)
            for comp, threshold in enumerate((0.6, 0.6, 1.2)):
                p, q, r = (mean(3 * comp + n) for n in range(3))
                base = p - threshold * level
                for depth in (0.75, 0.25):
                    centre = base + (depth * depth) * r
                    swing = (2.0 * depth) * q
                    driving += jnp.maximum(centre + swing, 0.0) + jnp.maximum(centre - swing, 0.0)
                if comp == 2:
                    driving += jnp.maximum(r - level, 0.0)
            for ch, threshold in ((9, 1.5), (10, 1.5), (11, 1.2)):
                driving += jnp.maximum(mean(ch) - threshold * level, 0.0)
            new = jnp.maximum(ext[12, at, :], 1.0 - jnp.exp(driving * decay[tab, :]))
            ext[12, at, :] = new
            hd[at, :] = 0.5 - 0.5 * new
        for b in range(f0 - 8, f1 + 8, 8):
            at = slice(OFF + b, OFF + b + 8)
            u = [state[k, at, :] for k in range(6)]
            for k in range(6):
                value = VISCOUS * state[6 + k, at, :]
                if K_STIFF[k] == 1.0:
                    value = u[k] + value
                elif K_STIFF[k]:
                    value = K_STIFF[k] * u[k] + value
                wp[k, at, :] = value
            for n, (lead, turn, sign, _) in enumerate(ACROSS):
                wp[6 + n, at, :] = sign * u[lead] - 0.5 * u[turn]
        for b in range(f0 - 8, f1, 8):
            at = slice(OFF + b, OFF + b + 8)
            nxt = slice(OFF + b + 1, OFF + b + 9)
            prv = slice(OFF + b - 1, OFF + b + 7)

            def fluxes(base, gammas, s, pairs):
                plus, minus = list(base), list(base)
                for gamma, (lead, turn, sign, stiff) in zip(gammas, pairs):
                    plus[lead] = minus[lead] = base[lead] + (sign * stiff) * gamma
                    half = (0.5 * stiff) * gamma
                    plus[turn], minus[turn] = base[turn] + half, base[turn] - half
                out_p = [s * x for x in plus]
                return out_p, [out_p[k] if plus[k] is minus[k] else s * minus[k] for k in range(6)]

            u = [state[k, at, :] for k in range(6)]
            w = [wp[k, at, :] for k in range(6)]
            h = hd[at, :]
            base = [wp[k, nxt, :] - w[k] for k in range(6)]
            gammas = [
                wp[6 + n, nxt, :] - (sign * u[lead] + 0.5 * u[turn])
                for n, (lead, turn, sign, _) in enumerate(ACROSS)
            ]
            plus, minus = fluxes(base, gammas, h + hd[nxt, :], ACROSS)
            for k in range(6):
                fm[k, at, :] = minus[k]
            if b < f0:
                continue
            total = [plus[k] - fm[k, prv, :] for k in range(6)]
            base = [next_lane(w[k]) - w[k] for k in range(6)]
            gammas = [
                next_lane(sign * u[lead] - 0.5 * u[turn]) - (sign * u[lead] + 0.5 * u[turn])
                for lead, turn, sign, _ in ALONG
            ]
            plus, minus = fluxes(base, gammas, h + next_lane(h), ALONG)
            total = [total[k] + plus[k] - prev_lane(minus[k]) for k in range(6)]
            dt = rate[EDGE + b : EDGE + b + 8, :]
            grip = 2.0 * ext[14, at, :]
            total[0] = total[0] + grip * (1.5 - u[0])
            total[2] = total[2] + grip * (-0.5 - u[2])
            for k in range(6):
                v_new = KEEP * state[6 + k, at, :] + dt * total[k]
                u_new = u[k] + dt * v_new
                if last_step:
                    final[6 + k, b : b + 8, :] = v_new
                    final[k, b : b + 8, :] = u_new
                else:
                    ext2[6 + k, at, :] = v_new
                    ext2[k, at, :] = u_new
        state = ext2
    for k in range(6):
        out_u[k] = final[k].T[PAD : PAD + CX, :]
        out_v[k] = final[6 + k].T[PAD : PAD + CX, :]
    out_d[...] = ext[12, OFF : OFF + CY, :].T[PAD : PAD + CX, :]


def tables(count_x, count_y):
    lane, row = jnp.arange(LANES), jnp.arange(SPAN)
    pos_x = lane + lax.axis_index("transit") * CX - PAD
    pos_y = row + lax.axis_index("lateral") * CY - EDGE
    in_x = (pos_x >= 0) & (pos_x < count_x)
    in_y = (pos_y >= 0) & (pos_y < count_y)

    def weight(offset, inside):
        dist = offset.astype(F32)
        return jnp.where((jnp.abs(offset) <= RADIUS) & inside, jnp.exp(-dist * dist / 32.0), 0.0)

    def parts(x):
        high = lax.reduce_precision(x, 8, 7)
        return high.astype(BF16), (x - high).astype(BF16)

    def beside(x, y):
        return jnp.concatenate([x, y], 1)

    along = weight(lane[:, None] - lane[None, :], in_x[:, None])
    across = weight(row[None, :] - row[:, None], in_y[None, :])
    cover = jnp.sum(across, 1)[:, None] * jnp.sum(along, 0)[None, :]
    inside = in_y[:, None] & in_x[None, :]
    cover = jnp.where(inside, cover, 1.0)
    decay = jnp.where(inside, -1.0 / (24.0 * cover), 0.0)
    rate = jnp.where(inside, DT, 0.0)
    high, low = parts(along)
    band = beside(high, low)
    band = jnp.concatenate([band, band], 0)
    own = (row > EDGE) & (row < EDGE + CY - 1)
    high, low = parts(jnp.where(own[None, :], across, 0.0)[16:176, EDGE : EDGE + CY])
    own_1, own_2 = beside(high, high), low
    outer = jnp.where(own[None, :], 0.0, across)[16:176]
    high, low = parts(beside(outer[:, 0:48], outer[:, 144:192]))
    rim_1, rim_2 = beside(high, high), low
    high, low = parts(across[24:168, 16:176])
    all_1, all_2 = beside(high, high), low
    return band, (own_1, own_2), (rim_1, rim_2, all_1, all_2, 4.0 * cover, decay, rate)


def vmem(n):
    return [pl.BlockSpec(memory_space=pltpu.VMEM)] * n


def on_device(displacement, velocity, damage, strength, contact, flaw_cells):
    params = pltpu.CompilerParams(vmem_limit_bytes=48 * 1024 * 1024)
    shape = jax.ShapeDtypeStruct
    tile = shape((CX, CY), F32)
    send_a, send_b, *own = pl.pallas_call(
        pack_kernel,
        out_shape=[shape((SLAB, LANES), F32)] * 2
        + [shape((6, CX, CY), F32)] * 2
        + [tile, tile, shape((CX, CY), jnp.int32)],
        in_specs=[pl.BlockSpec(memory_space=pltpu.HBM)] * 6,
        out_specs=vmem(7),
        scratch_shapes=[
            pltpu.VMEM((CX, CY), F32),
            pltpu.SMEM(flaw_cells.shape, jnp.int32),
            pltpu.SemaphoreType.DMA((6,)),
        ],
        compiler_params=params,
        name="pack_rows",
    )(*(pltpu.with_memory_space_constraint(x, pltpu.HBM) for x in (flaw_cells, displacement, velocity, damage, strength, contact)))
    got = swap((send_a, send_b), "transit")
    side_a, side_b, flat = pl.pallas_call(
        edge_kernel,
        out_shape=[shape((SLAB, LANES), F32)] * 2 + [shape((15, 16 + CY, LANES), F32)],
        in_specs=vmem(7),
        out_specs=vmem(3),
        scratch_shapes=[pltpu.VMEM((15, LANES, LANES), F32)],
        compiler_params=params,
        name="turn_and_cut",
    )(*own, *got)
    side = swap((side_a, side_b), "lateral")
    band, of_own, table = tables(CX * lax.axis_size("transit"), CY * lax.axis_size("lateral"))
    partial = pl.pallas_call(
        inner_kernel,
        out_shape=shape((6, 160, 2 * LANES), F32),
        in_specs=vmem(4),
        out_specs=vmem(1)[0],
        scratch_shapes=[
            pltpu.VMEM((12, CY, 2 * LANES), BF16),
            pltpu.VMEM((6, 2 * CY, 2 * LANES), BF16),
        ],
        compiler_params=params,
        cost_estimate=pl.CostEstimate(flops=800_000_000, bytes_accessed=2_000_000, transcendentals=0),
        name="own_rows",
    )(flat, band, *of_own)
    out = pl.pallas_call(
        step_kernel,
        out_shape=[shape((6, CX, CY), F32)] * 2 + [shape((CX, CY), F32)],
        in_specs=vmem(12),
        out_specs=vmem(3),
        scratch_shapes=[
            pltpu.VMEM((15, HELD, LANES), F32),
            pltpu.VMEM((12, HELD, LANES), F32),
            pltpu.VMEM((8, HELD, LANES), F32),
            pltpu.VMEM((6, HELD, LANES), F32),
            pltpu.VMEM((HELD, LANES), F32),
            pltpu.VMEM((12, 160, 2 * LANES), BF16),
            pltpu.VMEM((6, 320, 2 * LANES), BF16),
            pltpu.VMEM((6, 160, 2 * LANES), F32),
            pltpu.VMEM((12, CY, LANES), F32),
        ],
        compiler_params=params,
        name="two_steps",
    )(flat, partial, *side[::-1], band, *table)
    return tuple(out)


def solution(mesh):
    return jax.shard_map(
        on_device,
        mesh=mesh,
        in_specs=(
            P(None, "transit", "lateral"),
            P(None, "transit", "lateral"),
            P("transit", "lateral"),
            P("transit", "lateral"),
            P("transit", "lateral"),
            P("transit", "lateral", None),
        ),
        out_specs=(
            P(None, "transit", "lateral"),
            P(None, "transit", "lateral"),
            P("transit", "lateral"),
        ),
        check_vma=False,
    )
```

time: 22.9 us -> 21.3 us (0.930)
  waiting for transfers between devices: 5.93 us -> 4.92 us
  Pallas kernels: 6.71 us -> 5.85 us
    pallas_call x1, Pallas kernels: 5.01 us -> 3.53 us  [on_device(): pl.pallas_call(step_kernel, out_shape=[shape((6, CX, CY), F32)] * 2 + [sh...]
    ppermute x4, waiting for transfers between devices: 5.93 us -> 4.92 us  [swap(): out.append(lax.ppermute(part, axis, pairs))]
    pallas_call x1 -> x2, Pallas kernels: 0.48 us -> 1.1 us  [the longest x1 0.73 us: on_device(): pl.pallas_call(inner_kernel, out_shape=shape((6, 160, 2 * LANES), F32), i...]
  transfers between devices with their start and end apart: 4 -> 4, of which waited for: 2 -> 2; matrix products, arithmetic and copies ran while one was open for 4% -> 5% of each run, Pallas kernels for 0% -> 3%
where the time goes in v4:
time: 21.3 us; the launch traced here: 21.1 us
  starting transfers between devices  8.49 us (40%)
  Pallas kernels  5.85 us (27%)
  waiting for transfers between devices  4.92 us (23%)
  other arithmetic  0.89 us (4%)
  between operations  0.77 us (4%)
    ppermute x4, starting transfers between devices, swap(): out.append(lax.ppermute(part, axis, pairs))  8.49 us
    ppermute x4, waiting for transfers between devices, swap(): out.append(lax.ppermute(part, axis, pairs))  4.92 us
    pallas_call x1, Pallas kernels, on_device(): pl.pallas_call(step_kernel, out_shape=[shape((6, CX, CY), F32)] * 2 + [sh...  3.53 us
    pallas_call x1, Pallas kernels, on_device(): pl.pallas_call(pack_kernel, out_shape=[shape((SLAB, LANES), F32)] * 2 + [...  1.22 us
    pallas_call x1, Pallas kernels, on_device(): pl.pallas_call(inner_kernel, out_shape=shape((6, 160, 2 * LANES), F32), i...  0.73 us
  transfers between devices with their start and end apart: 4, of which 2 were waited for; matrix products, arithmetic and copies ran while one was open for 5% of the time, Pallas kernels for 3%

profile of v4, /device:TPU:25, one launch (start us, length us, event | category | flops | bytes accessed | tf_op | source)
XLA Modules:
  0.0 21.1 jit_solution(15089795289168036984)
XLA Ops:
  0.6 1.2 %pack_rows.1 = (f32[224,128]{1,0:T(8,128)S(1)}, f32[224,128]{1,0:T(8,128)S(1)}, f32[6,64,128]{2,1,0:T(8,128)S(1)}, f32[6,64,128]{2,1,0:T(8,128)S(1)}, f32[64,128...) custom-call(s32[1,1,32]{2,1,0:T(1,128)} %flaw_in.1, f32[6,64,128]{2,1,0:T(8,128)} %disp_in.1, ...), custom_call_target="tpu_custom_call" | custom-call | tf_op jit(solution)/shard_map/pack_rows/pallas_call | solution.py:370
  1.9 1.3 %collective-permute-start = (f32[224,128]{1,0:T(8,128)S(1)}, f32[224,128]{1,0:T(8,128)S(1)}, u32[]{:S(2)}, u32[]{:S(2)}) collective-permute-start(f32[224,128]{1,0:T(8,128)S(1)} %get-tuple-element.18), channel_id=1, source_target_pairs={{0,4},{4,0},{8,12},{12,8},{16,20},{20,16},{24,28},{28,24},{1,5},{5... | collective-permute-start | bytes 344072 | tf_op jit(solution)/shard_map/ppermute | solution.py:44
  3.2 2.0 %collective-permute-start.1 = (f32[224,128]{1,0:T(8,128)S(1)}, f32[224,128]{1,0:T(8,128)S(1)}, u32[]{:S(2)}, u32[]{:S(2)}) collective-permute-start(f32[224,128]{1,0:T(8,128)S(1)} %get-tuple-element.19), channel_id=1, source_target_pairs={{4,8},{8,4},{12,16},{16,12},{20,24},{24,20},{5,9},{9,5},{13,17},{1... | collective-permute-start | bytes 344072 | tf_op jit(solution)/shard_map/ppermute | solution.py:44
  5.2 0.1 slice.19
  5.3 0.1 fusion.13
  5.4 0.1 fusion.6
  5.6 0.1 fusion.4
  5.7 0.1 fusion.7
  5.8 0.1 fusion.15
  5.9 0.1 fusion.8
  6.0 0.1 and_select_fusion.1
  6.1 0.1 pad_maximum_fusion.all_1
  6.2 0.0 collective-permute-done.got_a
  6.2 3.4 %collective-permute-done.1.got_b = f32[224,128]{1,0:T(8,128)S(1)} collective-permute-done((f32[224,128]{1,0:T(8,128)S(1)}, f32[224,128]{1,0:T(8,128)S(1)}, u32[]{:S(2)}, u32[]{:S(2)}) %collective-permute-start.1) | collective-permute-done | bytes 114720 | tf_op jit(solution)/shard_map/ppermute | solution.py:44
  9.6 0.4 %turn_and_cut.1 = (f32[224,128]{1,0:T(8,128)S(1)}, f32[224,128]{1,0:T(8,128)S(1)}, f32[15,144,128]{2,1,0:T(8,128)S(1)}) custom-call(f32[6,64,128]{2,1,0:T(8,128)S(1)} %get-tuple-element.13.disp, f32[6,64,128]{2,1,0:T(8,128)S(1)} %get-tuple-element.14.vel, f32[64,128]{1,0:T(8,128)S(1)} %get-tuple-element.15.dam, f32[64,128]{1,0:T(8,128)S(1)} %get-tuple-element.16.lim, ...), custom_call_target="tpu_custom_call" | custom-call | tf_op jit(solution)/shard_map/turn_and_cut/pallas_call | solution.py:386
  10.0 5.1 %collective-permute-start.2 = (f32[224,128]{1,0:T(8,128)S(1)}, f32[224,128]{1,0:T(8,128)S(1)}, u32[]{:S(2)}, u32[]{:S(2)}) collective-permute-start(f32[224,128]{1,0:T(8,128)S(1)} %get-tuple-element.21), channel_id=1, source_target_pairs={{1,2},{2,1},{5,6},{6,5},{9,10},{10,9},{13,14},{14,13},{17,18},{18,... | collective-permute-start | bytes 344072 | tf_op jit(solution)/shard_map/ppermute | solution.py:44
  15.1 0.1 collective-permute-start.3
  15.2 0.1 pad_maximum_fusion.3.rim_1
  15.3 0.7 %own_rows.1.partial = f32[6,160,256]{2,1,0:T(8,128)S(1)} custom-call(f32[15,144,128]{2,1,0:T(8,128)S(1)} %get-tuple-element.20.flat, bf16[256,256]{1,0:T(8,128)(2,1)S(1)} %maximum_maximum_fusion.band, bf16[160,256]{1,0:T(8,128)(2,1)S(1)} %pad_maximum_fusion.1.first, bf16[160,128]{1,0:T(8,128)(2,1)S(1)} %get-tuple-element.23.second), custom_call_target="tpu_custom_call" | custom-call | flops 800000000 | bytes 2000000 | tf_op jit(solution)/shard_map/own_rows/pallas_call | solution.py:397
  16.0 1.5 %collective-permute-done.2.side_b = f32[224,128]{1,0:T(8,128)S(1)} collective-permute-done((f32[224,128]{1,0:T(8,128)S(1)}, f32[224,128]{1,0:T(8,128)S(1)}, u32[]{:S(2)}, u32[]{:S(2)}) %collective-permute-start.2) | collective-permute-done | bytes 114720 | tf_op jit(solution)/shard_map/ppermute | solution.py:44
  17.6 0.0 collective-permute-done.3.side_a
  17.6 3.5 %two_steps.1 = (f32[6,64,128]{2,1,0:T(8,128)}, f32[6,64,128]{2,1,0:T(8,128)}, f32[64,128]{1,0:T(8,128)}) custom-call(f32[15,144,128]{2,1,0:T(8,128)S(1)} %get-tuple-element.20.flat, f32[6,160,256]{2,1,0:T(8,128)S(1)} %own_rows.1.partial, f32[224,128]{1,0:T(8,128)S(1)} %collective-permute-done.2.side_b, f32[224,128]{1,0:T(8,128)S(1)} %collective-permute-done.3.side_a, ...), custom_call_target="tpu_custom_call" | custom-call | tf_op jit(solution)/shard_map/two_steps/pallas_call | solution.py:410
  (4 shorter events, 0.0 us)
Async XLA Ops:
  1.9 4.4 %collective-permute-start = (f32[224,128]{1,0:T(8,128)S(1)}, f32[224,128]{1,0:T(8,128)S(1)}, u32[]{:S(2)}, u32[]{:S(2)}) collective-permute-start(f32[224,128]{1,0:T(8,128)S(1)} %get-tuple-element.18), channel_id=1, source_target_pairs={{0,4},{4,0},{8,12},{12,8},{16,20},{20,16},{24,28},{28,24},{1,5},{5... | collective-permute-start | bytes 344072 | tf_op jit(solution)/shard_map/ppermute | solution.py:44
  3.2 6.4 %collective-permute-start.1 = (f32[224,128]{1,0:T(8,128)S(1)}, f32[224,128]{1,0:T(8,128)S(1)}, u32[]{:S(2)}, u32[]{:S(2)}) collective-permute-start(f32[224,128]{1,0:T(8,128)S(1)} %get-tuple-element.19), channel_id=1, source_target_pairs={{4,8},{8,4},{12,16},{16,12},{20,24},{24,20},{5,9},{9,5},{13,17},{1... | collective-permute-start | bytes 344072 | tf_op jit(solution)/shard_map/ppermute | solution.py:44
  10.0 7.6 %collective-permute-start.2 = (f32[224,128]{1,0:T(8,128)S(1)}, f32[224,128]{1,0:T(8,128)S(1)}, u32[]{:S(2)}, u32[]{:S(2)}) collective-permute-start(f32[224,128]{1,0:T(8,128)S(1)} %get-tuple-element.21), channel_id=1, source_target_pairs={{1,2},{2,1},{5,6},{6,5},{9,10},{10,9},{13,14},{14,13},{17,18},{18,... | collective-permute-start | bytes 344072 | tf_op jit(solution)/shard_map/ppermute | solution.py:44
  15.1 2.5 %collective-permute-start.3 = (f32[224,128]{1,0:T(8,128)S(1)}, f32[224,128]{1,0:T(8,128)S(1)}, u32[]{:S(2)}, u32[]{:S(2)}) collective-permute-start(f32[224,128]{1,0:T(8,128)S(1)} %get-tuple-element.22), channel_id=1, source_target_pairs={{0,1},{1,0},{2,3},{3,2},{4,5},{5,4},{6,7},{7,6},{8,9},{9,8},{10,11... | collective-permute-start | bytes 344072 | tf_op jit(solution)/shard_map/ppermute | solution.py:44

commit v5 on v4

v5 whole, which is shorter than its diff:
```python
import functools

import jax
import jax.numpy as jnp
from jax import lax
from jax.experimental import pallas as pl
from jax.experimental.pallas import tpu as pltpu
from jax.sharding import PartitionSpec as P

RADIUS = 8
CX, CY = 64, 128
WIDE, NEAR = 20, 11
PAD = 24
EDGE = 32
SPAN = CY + 2 * EDGE
OFF = EDGE + 8
HELD = CY + 2 * OFF
LANES = 128
SLAB = 224
K_STIFF = (1.0, 1.0, 0.0, 0.5, 0.5, 0.2)
VISCOUS = 0.2
KEEP = 0.95
DT = 0.4
ALONG = ((2, 3, 1.0, 0.8), (1, 5, 1.0, 0.3))
ACROSS = ((2, 4, 1.0, 0.8), (0, 5, -1.0, 0.3))
F32, BF16 = jnp.float32, jnp.bfloat16


def halo_of(field):
    return WIDE if field < 6 else NEAR


def slab_start(field):
    return WIDE * field if field < 6 else 6 * WIDE + NEAR * (field - 6)


def swap(block, axis):
    count = lax.axis_size(axis)
    out = []
    for first, part in zip((0, 1), block):
        pairs = []
        for i in range(first, count - 1, 2):
            pairs += [(i, i + 1), (i + 1, i)]
        out.append(lax.ppermute(part, axis, pairs))
    return out


def weakness(rows, flaw, first_row):
    node = lax.broadcasted_iota(jnp.int32, (rows, CY), 0) * CY + lax.broadcasted_iota(
        jnp.int32, (rows, CY), 1
    )
    mark = node == flaw[0, 0, 0] - first_row * CY
    for j in range(1, flaw.shape[2]):
        mark = mark | (node == flaw[0, 0, j] - first_row * CY)
    return jnp.where(mark, 0.4, 1.0)


def run_copies(pairs, sems):
    copies = [pltpu.make_async_copy(src, dst, sems.at[n]) for n, (src, dst) in enumerate(pairs)]
    for copy in copies:
        copy.start()
    copies[0].wait()
    return copies[1:]


def pack_kernel(flaw_in, disp_in, vel_in, dam_in, stren_in, con_in, out_a, out_b, disp, vel, dam, stren, con, flaw, sems):
    pairs = [(flaw_in, flaw)]
    for side in range(2):
        wide = pl.ds(side * (CX - 24), 24)
        near = pl.ds(side * (CX - 16), 16)
        pairs.append((disp_in.at[:, wide, :], disp.at[side]))
        pairs.append((vel_in.at[:, near, :], vel.at[side]))
        for src, dst in ((dam_in, dam), (stren_in, stren), (con_in, con)):
            pairs.append((src.at[near, :], dst.at[side]))
    others = run_copies(pairs, sems)
    factors = [weakness(16, flaw, side * (CX - 16)) for side in range(2)]
    for copy in others:
        copy.wait()
    limits = [stren[side] * factors[side] for side in range(2)]

    def fill(out, side):
        for k in range(15):
            width, start = halo_of(k), slab_start(k)
            held = 24 if k < 6 else 16
            rows = slice(held - width, held) if side else slice(0, width)
            if k < 6:
                part = disp[side, k, rows, :]
            elif k < 12:
                part = vel[side, k - 6, rows, :]
            elif k == 12:
                part = dam[side, rows, :]
            elif k == 13:
                part = limits[side][rows, :]
            else:
                part = con[side, rows, :].astype(F32)
            out[start : start + width, :] = part
        out[219:SLAB, :] = jnp.zeros((SLAB - 219, LANES), F32)

    even = lax.rem(lax.axis_index("transit"), 2) == 0

    @pl.when(even)
    def _():
        fill(out_a, 1)
        fill(out_b, 0)

    @pl.when(jnp.logical_not(even))
    def _():
        fill(out_a, 0)
        fill(out_b, 1)


def load_kernel(flaw_in, disp_in, vel_in, dam_in, stren_in, con_in, disp, vel, dam, lim, con, stren, flaw, sems):
    others = run_copies(
        zip(
            (flaw_in, disp_in, vel_in, dam_in, stren_in, con_in),
            (flaw, disp, vel, dam, stren, con),
        ),
        sems,
    )
    factor = weakness(CX, flaw, 0)
    for copy in others:
        copy.wait()
    lim[...] = stren[...] * factor


def edge_kernel(disp, vel, dam, lim, con, got_a, got_b, out_a, out_b, flat, ext):
    even = lax.rem(lax.axis_index("transit"), 2) == 0
    even_l = lax.rem(lax.axis_index("lateral"), 2) == 0
    for k in range(15):
        width, start = halo_of(k), slab_start(k)
        part_a = got_a[start : start + width, :]
        part_b = got_b[start : start + width, :]
        if k < 6:
            own = disp[k]
        elif k < 12:
            own = vel[k - 6]
        else:
            own = (dam, lim, con)[k - 12][...].astype(F32)
        low, high = PAD, PAD + CX
        ext[k, 0 : low - width, :] = jnp.zeros((low - width, LANES), F32)
        ext[k, low - width : low, :] = jnp.where(even, part_b, part_a)
        ext[k, low:high, :] = own
        ext[k, high : high + width, :] = jnp.where(even, part_a, part_b)
        ext[k, high + width : LANES, :] = jnp.zeros((LANES - high - width, LANES), F32)
        turned = ext[k].T
        flat[k, 8 : 8 + CY, :] = turned
        flat[k, 0:8, :] = jnp.zeros((8, LANES), F32)
        flat[k, 8 + CY : 16 + CY, :] = jnp.zeros((8, LANES), F32)
        right, left = turned[CY - width :, :], turned[:width, :]
        out_a[start : start + width, :] = jnp.where(even_l, right, left)
        out_b[start : start + width, :] = jnp.where(even_l, left, right)
    for out in (out_a, out_b):
        out[219:SLAB, :] = jnp.zeros((SLAB - 219, LANES), F32)


def split(x):
    high = x.astype(BF16)
    return high, (x - high.astype(F32)).astype(BF16)


def next_lane(x):
    return pltpu.roll(x, LANES - 1, 1)


def prev_lane(x):
    return pltpu.roll(x, 1, 1)


def products(get, put):
    c = [get(k, 0) for k in range(6)]
    x = [next_lane(c[k]) - prev_lane(c[k]) for k in range(5)]
    y = [get(k, 1) - get(k, -1) for k in range(5)]
    plane = (x[0], y[1], y[0] + x[1])
    bend = (x[3], y[4], y[3] + x[4])
    e7 = x[2] - 2.0 * c[3]
    e8 = y[2] - 2.0 * c[4]
    e9 = 0.5 * (x[1] - y[0]) - 2.0 * c[5]
    values = []
    for p, q in zip(plane, bend):
        values += [p * p, p * q, q * q]
    for ch, value in enumerate(values + [e7 * e7, e8 * e8, e9 * e9]):
        high, low = split(value)
        put(ch, slice(0, LANES), high)
        put(ch, slice(LANES, 2 * LANES), low)


def lane_sums(energy, turned, rows, band):
    for ch in range(12):
        both = jnp.dot(energy[ch, 0:rows, :], band[...], preferred_element_type=F32)
        high, low = split(both[:, :LANES] + both[:, LANES:])
        cols = slice(ch % 2 * LANES, (ch % 2 + 1) * LANES)
        turned[ch // 2, 0:rows, cols] = high
        turned[ch // 2, rows : 2 * rows, cols] = low


def row_sums(turned, pair, rows, first, second):
    return jnp.dot(first[...], turned[pair, 0 : 2 * rows, :], preferred_element_type=F32) + jnp.dot(
        second[...], turned[pair, 0:rows, :], preferred_element_type=F32
    )


def new_damage(mean, level, old, decay):
    driving = jnp.zeros((8, LANES), F32)
    for comp, threshold in enumerate((0.6, 0.6, 1.2)):
        p, q, r = (mean(3 * comp + n) for n in range(3))
        base = p - threshold * level
        for depth in (0.75, 0.25):
            centre = base + (depth * depth) * r
            swing = (2.0 * depth) * q
            driving += jnp.maximum(centre + swing, 0.0) + jnp.maximum(centre - swing, 0.0)
        if comp == 2:
            driving += jnp.maximum(r - level, 0.0)
    for ch, threshold in ((9, 1.5), (10, 1.5), (11, 1.2)):
        driving += jnp.maximum(mean(ch) - threshold * level, 0.0)
    return jnp.maximum(old, 1.0 - jnp.exp(driving * decay))


def fluxes(base, gammas, s, pairs):
    plus, minus = list(base), list(base)
    for gamma, (lead, turn, sign, stiff) in zip(gammas, pairs):
        plus[lead] = minus[lead] = base[lead] + (sign * stiff) * gamma
        half = (0.5 * stiff) * gamma
        plus[turn], minus[turn] = base[turn] + half, base[turn] - half
    out_p = [s * x for x in plus]
    return out_p, [out_p[k] if plus[k] is minus[k] else s * minus[k] for k in range(6)]


def move(f0, f1, state, off, hd, contact, rate, wp, fm, put):
    for b in range(f0 - 8, f1 + 8, 8):
        at = slice(OFF + b, OFF + b + 8)
        here = slice(off + b, off + b + 8)
        u = [state[k, here, :] for k in range(6)]
        for k in range(6):
            value = VISCOUS * state[6 + k, here, :]
            if K_STIFF[k] == 1.0:
                value = u[k] + value
            elif K_STIFF[k]:
                value = K_STIFF[k] * u[k] + value
            wp[k, at, :] = value
        for n, (lead, turn, sign, _) in enumerate(ACROSS):
            wp[6 + n, at, :] = sign * u[lead] - 0.5 * u[turn]
    for b in range(f0 - 8, f1, 8):
        at = slice(OFF + b, OFF + b + 8)
        nxt = slice(OFF + b + 1, OFF + b + 9)
        prv = slice(OFF + b - 1, OFF + b + 7)
        here = slice(off + b, off + b + 8)
        u = [state[k, here, :] for k in range(6)]
        w = [wp[k, at, :] for k in range(6)]
        h = hd[at, :]
        base = [wp[k, nxt, :] - w[k] for k in range(6)]
        gammas = [
            wp[6 + n, nxt, :] - (sign * u[lead] + 0.5 * u[turn])
            for n, (lead, turn, sign, _) in enumerate(ACROSS)
        ]
        plus, minus = fluxes(base, gammas, h + hd[nxt, :], ACROSS)
        for k in range(6):
            fm[k, at, :] = minus[k]
        if b < f0:
            continue
        total = [plus[k] - fm[k, prv, :] for k in range(6)]
        base = [next_lane(w[k]) - w[k] for k in range(6)]
        gammas = [
            next_lane(sign * u[lead] - 0.5 * u[turn]) - (sign * u[lead] + 0.5 * u[turn])
            for lead, turn, sign, _ in ALONG
        ]
        plus, minus = fluxes(base, gammas, h + next_lane(h), ALONG)
        total = [total[k] + plus[k] - prev_lane(minus[k]) for k in range(6)]
        dt = rate[EDGE + b : EDGE + b + 8, :]
        grip = 2.0 * contact(b)
        total[0] = total[0] + grip * (1.5 - u[0])
        total[2] = total[2] + grip * (-0.5 - u[2])
        for k in range(6):
            v_new = KEEP * state[6 + k, here, :] + dt * total[k]
            put(6 + k, b, v_new)
            put(k, b, u[k] + dt * v_new)


def rows_of(ref, off, b):
    return ref[off + b : off + b + 8, :]


def harm(b, row, aver, limit, old, hd, cover, decay):
    def mean(ch):
        return aver[ch // 2, row : row + 8, ch % 2 * LANES : (ch % 2 + 1) * LANES]

    tab = slice(EDGE + b, EDGE + b + 8)
    new = new_damage(mean, limit * cover[tab, :], old, decay[tab, :])
    hd[OFF + b : OFF + b + 8, :] = 0.5 - 0.5 * new
    return new


def gather(state, off, starts, energy, turned, band):
    for n, b in enumerate(starts):
        def get(k, shift):
            return state[k, off + b + shift : off + b + shift + 16, :]

        def put(ch, cols, value):
            energy[ch, 16 * n : 16 * n + 16, cols] = value

        products(get, put)
    lane_sums(energy, turned, 16 * len(starts), band)


def inner_kernel(
    flat, band, first, second, mid_1, mid_2, cover, decay, rate,
    partial, moved, harmed_1, final, harmed_2,
    next_state, energy, turned, aver, old, wp, fm, hd,
):
    for low in (0, 120):
        hd[OFF + low : OFF + low + 8, :] = jnp.full((8, LANES), 0.5, F32)
        for k in range(6):
            next_state[k, OFF + low : OFF + low + 8, :] = jnp.zeros((8, LANES), F32)
    gather(flat, 8, range(0, CY, 16), energy, turned, band)
    for pair in range(6):
        sums = row_sums(turned, pair, CY, first, second)
        partial[pair, 0:32, :] = sums[0:32]
        aver[pair] = sums[24:136]
        partial[pair, 32:64, :] = sums[128:160]

    def contact(b):
        return rows_of(flat.at[14], 8, b)

    for b in range(8, 120, 8):
        new = harm(b, b - 8, aver, rows_of(flat.at[13], 8, b), rows_of(flat.at[12], 8, b), hd, cover, decay)
        old[b - 8 : b, :] = new
    harmed_1[0:16, :] = old[8:24, :]
    harmed_1[16:32, :] = old[88:104, :]

    def put_next(k, b, value):
        next_state[k, OFF + b : OFF + b + 8, :] = value

    move(8, 120, flat, 8, hd, contact, rate, wp, fm, put_next)
    for k in range(12):
        moved[k, 0:24, :] = next_state[k, OFF + 16 : OFF + 40, :]
        moved[k, 24:48, :] = next_state[k, OFF + 88 : OFF + 112, :]
    gather(next_state, OFF, range(8, 120, 16), energy, turned, band)
    for pair in range(6):
        aver[pair, 0:96, :] = row_sums(turned, pair, 112, mid_1, mid_2)
    for b in range(16, 112, 8):
        new = harm(b, b - 16, aver, rows_of(flat.at[13], 8, b), old[b - 8 : b, :], hd, cover, decay)
        if 24 <= b < 104:
            harmed_2[b - 24 : b - 16, :] = new

    def put_last(k, b, value):
        final[k, b - 24 : b - 16, :] = value

    move(24, 104, next_state, OFF, hd, contact, rate, wp, fm, put_last)


def step_kernel(
    flat, partial, moved, harmed_1, inner, harmed_2, side_b, side_a,
    band, rim_1, rim_2, all_1, all_2, cover, decay, rate,
    out_u, out_v, out_d,
    ext, ext2, wp, fm, hd, energy, turned, aver, final, done, sems,
):
    even = lax.rem(lax.axis_index("lateral"), 2) == 0
    for k in range(15):
        width, start = halo_of(k), slab_start(k)
        part_a = side_a[start : start + width, :]
        part_b = side_b[start : start + width, :]
        ext[k, OFF - EDGE : OFF - width, :] = jnp.zeros((EDGE - width, LANES), F32)
        ext[k, OFF - width : OFF, :] = jnp.where(even, part_b, part_a)
        for low, high in ((0, 24), (104, CY)):
            ext[k, OFF + low : OFF + high, :] = flat[k, 8 + low : 8 + high, :]
        ext[k, OFF + CY : OFF + CY + width, :] = jnp.where(even, part_a, part_b)
        ext[k, OFF + CY + width : OFF + CY + EDGE, :] = jnp.zeros((EDGE - width, LANES), F32)
    for low in (-24, 144):
        for k in range(6):
            ext2[k, OFF + low : OFF + low + 8, :] = jnp.zeros((8, LANES), F32)
        hd[OFF + low : OFF + low + 8, :] = jnp.full((8, LANES), 0.5, F32)
    for k in range(12):
        ext2[k, OFF + 16 : OFF + 40, :] = moved[k, 0:24, :]
        ext2[k, OFF + 88 : OFF + 112, :] = moved[k, 24:48, :]
        final[k, 24:104, :] = inner[k]
    for n, low in ((0, 16), (16, 96)):
        ext[12, OFF + low : OFF + low + 16, :] = harmed_1[n : n + 16, :]
        hd[OFF + low : OFF + low + 16, :] = 0.5 - 0.5 * harmed_1[n : n + 16, :]

    def contact(b):
        return rows_of(ext.at[14], OFF, b)

    def spoil(row, b):
        old = rows_of(ext.at[12], OFF, b)
        new = harm(b, row, aver, rows_of(ext.at[13], OFF, b), old, hd, cover, decay)
        ext[12, OFF + b : OFF + b + 8, :] = new

    gather(ext, OFF, (-24, -8, 120, 136), energy, turned, band)
    for pair in range(6):
        aver[pair] = partial[pair] + row_sums(turned, pair, 64, rim_1, rim_2)
    for row, b in enumerate((*range(-16, 16, 8), *range(112, 144, 8))):
        spoil(8 * row, b)

    def put_next(k, b, value):
        ext2[k, OFF + b : OFF + b + 8, :] = value

    move(-16, 16, ext, OFF, hd, contact, rate, wp, fm, put_next)
    move(112, 144, ext, OFF, hd, contact, rate, wp, fm, put_next)

    gather(ext2, OFF, (-16, 0, 16, 96, 112, 128), energy, turned, band)
    for pair in range(6):
        aver[pair] = row_sums(turned, pair, 96, all_1, all_2)
    for row, b in enumerate((*range(-8, 24, 8), *range(104, 136, 8))):
        spoil(8 * row, b)
    ext[12, OFF + 24 : OFF + 104, :] = harmed_2[...]
    for low in (24, 96):
        hd[OFF + low : OFF + low + 8, :] = 0.5 - 0.5 * harmed_2[low - 24 : low - 16, :]
    copies = []

    def send(n, field, out):
        done[n] = field.T[PAD : PAD + CX, :]
        copy = pltpu.make_async_copy(done.at[n], out, sems.at[n])
        copy.start()
        copies.append(copy)

    send(12, ext[12, OFF : OFF + CY, :], out_d)

    def put_last(k, b, value):
        final[k, b : b + 8, :] = value

    move(0, 24, ext2, OFF, hd, contact, rate, wp, fm, put_last)
    move(104, CY, ext2, OFF, hd, contact, rate, wp, fm, put_last)
    for k in range(6):
        send(k, final[k], out_u.at[k])
        send(6 + k, final[6 + k], out_v.at[k])
    for copy in copies:
        copy.wait()


def tables(count_x, count_y):
    lane, row = jnp.arange(LANES), jnp.arange(SPAN)
    pos_x = lane + lax.axis_index("transit") * CX - PAD
    pos_y = row + lax.axis_index("lateral") * CY - EDGE
    in_x = (pos_x >= 0) & (pos_x < count_x)
    in_y = (pos_y >= 0) & (pos_y < count_y)

    def weight(offset, inside):
        dist = offset.astype(F32)
        return jnp.where((jnp.abs(offset) <= RADIUS) & inside, jnp.exp(-dist * dist / 32.0), 0.0)

    def parts(x):
        high = lax.reduce_precision(x, 8, 7)
        return high.astype(BF16), (x - high).astype(BF16)

    def beside(x, y):
        return jnp.concatenate([x, y], 1)

    along = weight(lane[:, None] - lane[None, :], in_x[:, None])
    across = weight(row[None, :] - row[:, None], in_y[None, :])
    cover = jnp.sum(across, 1)[:, None] * jnp.sum(along, 0)[None, :]
    inside = in_y[:, None] & in_x[None, :]
    cover = jnp.where(inside, cover, 1.0)
    decay = jnp.where(inside, -1.0 / (24.0 * cover), 0.0)
    rate = jnp.where(inside, DT, 0.0)
    high, low = parts(along)
    band = beside(high, low)
    band = jnp.concatenate([band, band], 0)
    own = (row > EDGE) & (row < EDGE + CY - 1)
    high, low = parts(jnp.where(own[None, :], across, 0.0)[16:176, EDGE : EDGE + CY])
    own_1, own_2 = beside(high, high), low
    outer = jnp.where(own[None, :], 0.0, across)

    def ends(x, n, m):
        return jnp.concatenate([x[EDGE - n : EDGE + m], x[EDGE + CY - m : EDGE + CY + n]], 0)

    high, low = parts(ends(ends(outer, 16, 16).T, 24, 8).T)
    rim_1, rim_2 = beside(high, high), low
    high, low = parts(ends(ends(across, 8, 24).T, 16, 32).T)
    all_1, all_2 = beside(high, high), low
    sure = (row >= EDGE + 11) & (row <= EDGE + 116)
    high, low = parts(jnp.where(sure[None, :], across, 0.0)[EDGE + 16 : EDGE + 112, EDGE + 8 : EDGE + 120])
    mid_1, mid_2 = beside(high, high), low
    maps = (4.0 * cover, decay, rate)
    return band, (own_1, own_2, mid_1, mid_2, *maps), (rim_1, rim_2, all_1, all_2, *maps)


def vmem(n):
    return [pl.BlockSpec(memory_space=pltpu.VMEM)] * n


def on_device(displacement, velocity, damage, strength, contact, flaw_cells):
    params = pltpu.CompilerParams(vmem_limit_bytes=48 * 1024 * 1024)
    shape = jax.ShapeDtypeStruct
    inputs = [
        pltpu.with_memory_space_constraint(x, pltpu.HBM)
        for x in (flaw_cells, displacement, velocity, damage, strength, contact)
    ]
    flaw_copy = pltpu.SMEM(flaw_cells.shape, jnp.int32)
    send_a, send_b = pl.pallas_call(
        pack_kernel,
        out_shape=[shape((SLAB, LANES), F32)] * 2,
        in_specs=[pl.BlockSpec(memory_space=pltpu.HBM)] * 6,
        out_specs=vmem(2),
        scratch_shapes=[
            pltpu.VMEM((2, 6, 24, CY), F32),
            pltpu.VMEM((2, 6, 16, CY), F32),
            pltpu.VMEM((2, 16, CY), F32),
            pltpu.VMEM((2, 16, CY), F32),
            pltpu.VMEM((2, 16, CY), jnp.int32),
            flaw_copy,
            pltpu.SemaphoreType.DMA((11,)),
        ],
        compiler_params=params,
        name="pack_rows",
    )(*inputs)
    got = swap((send_a, send_b), "transit")
    tile = shape((CX, CY), F32)
    own = pl.pallas_call(
        load_kernel,
        out_shape=[shape((6, CX, CY), F32)] * 2 + [tile, tile, shape((CX, CY), jnp.int32)],
        in_specs=[pl.BlockSpec(memory_space=pltpu.HBM)] * 6,
        out_specs=vmem(5),
        scratch_shapes=[pltpu.VMEM((CX, CY), F32), flaw_copy, pltpu.SemaphoreType.DMA((6,))],
        compiler_params=params,
        name="load_tile",
    )(*inputs)
    side_a, side_b, flat = pl.pallas_call(
        edge_kernel,
        out_shape=[shape((SLAB, LANES), F32)] * 2 + [shape((15, 16 + CY, LANES), F32)],
        in_specs=vmem(7),
        out_specs=vmem(3),
        scratch_shapes=[pltpu.VMEM((15, LANES, LANES), F32)],
        compiler_params=params,
        name="turn_and_cut",
    )(*own, *got)
    side = swap((side_a, side_b), "lateral")
    band, of_own, table = tables(CX * lax.axis_size("transit"), CY * lax.axis_size("lateral"))
    held = pltpu.VMEM((HELD, LANES), F32)
    inner = pl.pallas_call(
        inner_kernel,
        out_shape=[
            shape((6, 64, 2 * LANES), F32),
            shape((12, 48, LANES), F32),
            shape((32, LANES), F32),
            shape((12, 80, LANES), F32),
            shape((80, LANES), F32),
        ],
        in_specs=vmem(9),
        out_specs=vmem(5),
        scratch_shapes=[
            pltpu.VMEM((12, HELD, LANES), F32),
            pltpu.VMEM((12, CY, 2 * LANES), BF16),
            pltpu.VMEM((6, 2 * CY, 2 * LANES), BF16),
            pltpu.VMEM((6, 112, 2 * LANES), F32),
            pltpu.VMEM((112, LANES), F32),
            pltpu.VMEM((8, HELD, LANES), F32),
            pltpu.VMEM((6, HELD, LANES), F32),
            held,
        ],
        compiler_params=params,
        cost_estimate=pl.CostEstimate(flops=800_000_000, bytes_accessed=2_000_000, transcendentals=0),
        name="inner_rows",
    )(flat, band, *of_own)
    out = pl.pallas_call(
        step_kernel,
        out_shape=[shape((6, CX, CY), F32)] * 2 + [shape((CX, CY), F32)],
        in_specs=vmem(16),
        out_specs=[pl.BlockSpec(memory_space=pltpu.HBM)] * 3,
        scratch_shapes=[
            pltpu.VMEM((15, HELD, LANES), F32),
            pltpu.VMEM((12, HELD, LANES), F32),
            pltpu.VMEM((8, HELD, LANES), F32),
            pltpu.VMEM((6, HELD, LANES), F32),
            held,
            pltpu.VMEM((12, 96, 2 * LANES), BF16),
            pltpu.VMEM((6, 192, 2 * LANES), BF16),
            pltpu.VMEM((6, 64, 2 * LANES), F32),
            pltpu.VMEM((12, CY, LANES), F32),
            pltpu.VMEM((13, CX, CY), F32),
            pltpu.SemaphoreType.DMA((13,)),
        ],
        compiler_params=params,
        name="two_steps",
    )(flat, *inner, *side[::-1], band, *table)
    return tuple(out)


def solution(mesh):
    return jax.shard_map(
        on_device,
        mesh=mesh,
        in_specs=(
            P(None, "transit", "lateral"),
            P(None, "transit", "lateral"),
            P("transit", "lateral"),
            P("transit", "lateral"),
            P("transit", "lateral"),
            P("transit", "lateral", None),
        ),
        out_specs=(
            P(None, "transit", "lateral"),
            P(None, "transit", "lateral"),
            P("transit", "lateral"),
        ),
        check_vma=False,
    )
```

time: 21.3 us -> 20.5 us (0.962)
  waiting for transfers between devices: 4.92 us -> 2.3 us
  Pallas kernels: 5.85 us -> 7.31 us
    ppermute x4, waiting for transfers between devices: 4.92 us -> 2.3 us  [swap(): out.append(lax.ppermute(part, axis, pairs))]
    pallas_call x2 -> x3, Pallas kernels: 1.96 us -> 4.13 us  [the longest x1 1.91 us: on_device(): pl.pallas_call(inner_kernel, out_shape=[shape((6, 64, 2 * LANES), F32), s...]
    pallas_call x1, Pallas kernels: 3.53 us -> 2.82 us  [on_device(): pl.pallas_call(step_kernel, out_shape=[shape((6, CX, CY), F32)] * 2 + [sh...]
  transfers between devices with their start and end apart: 4 -> 4, of which waited for: 2 -> 2; matrix products, arithmetic and copies ran while one was open for 5% -> 7% of each run, Pallas kernels for 3% -> 15%
where the time goes in v5:
time: 20.5 us; the launch traced here: 20.3 us
  starting transfers between devices  8.49 us (41%)
  Pallas kernels  7.31 us (36%)
  waiting for transfers between devices  2.3 us (11%)
  other arithmetic  1.04 us (5%)
  between operations  0.81 us (4%)
  local copies, waits for them, and re-layouts  0.31 us (2%)
    ppermute x4, starting transfers between devices, swap(): out.append(lax.ppermute(part, axis, pairs))  8.49 us
    pallas_call x1, Pallas kernels, on_device(): pl.pallas_call(step_kernel, out_shape=[shape((6, CX, CY), F32)] * 2 + [sh...  2.82 us
    ppermute x4, waiting for transfers between devices, swap(): out.append(lax.ppermute(part, axis, pairs))  2.3 us
    pallas_call x1, Pallas kernels, on_device(): pl.pallas_call(inner_kernel, out_shape=[shape((6, 64, 2 * LANES), F32), s...  1.91 us
    pallas_call x1, Pallas kernels, on_device(): pl.pallas_call(pack_kernel, out_shape=[shape((SLAB, LANES), F32)] * 2, in...  1.13 us
    pallas_call x1, Pallas kernels, on_device(): pl.pallas_call(load_kernel, out_shape=[shape((6, CX, CY), F32)] * 2 + [ti...  1.09 us
  transfers between devices with their start and end apart: 4, of which 2 were waited for; matrix products, arithmetic and copies ran while one was open for 7% of the time, Pallas kernels for 15%

profile of v5, /device:TPU:25, one launch (start us, length us, event | category | flops | bytes accessed | tf_op | source)
XLA Modules:
  0.0 20.3 jit_solution(4724470503681669461)
XLA Ops:
  0.6 1.1 %pack_rows.1 = (f32[224,128]{1,0:T(8,128)S(1)}, f32[224,128]{1,0:T(8,128)S(1)}) custom-call(s32[1,1,32]{2,1,0:T(1,128)} %flaw_in.3, f32[6,64,128]{2,1,0:T(8,128)} %disp_in.3, f32[6,64,128]{2,1,0:T(8,128)} %vel_in.3, f32[64,128]{1,0:T(8,128)} %dam_in.3, f32[64,128]{1,0:T(8,128)} %stren_in.3, s32[64,128]{1,0:T(8,128)} %con_in.3), custom_call_target="tpu_custom_call" | custom-call | tf_op jit(solution)/shard_map/pack_rows/pallas_call | solution.py:488
  1.8 1.3 %collective-permute-start = (f32[224,128]{1,0:T(8,128)S(1)}, f32[224,128]{1,0:T(8,128)S(1)}, u32[]{:S(2)}, u32[]{:S(2)}) collective-permute-start(f32[224,128]{1,0:T(8,128)S(1)} %get-tuple-element.23), channel_id=1, source_target_pairs={{0,4},{4,0},{8,12},{12,8},{16,20},{20,16},{24,28},{28,24},{1,5},{5... | collective-permute-start | bytes 344072 | tf_op jit(solution)/shard_map/ppermute | solution.py:44
  3.1 2.0 %collective-permute-start.1 = (f32[224,128]{1,0:T(8,128)S(1)}, f32[224,128]{1,0:T(8,128)S(1)}, u32[]{:S(2)}, u32[]{:S(2)}) collective-permute-start(f32[224,128]{1,0:T(8,128)S(1)} %get-tuple-element.24), channel_id=1, source_target_pairs={{4,8},{8,4},{12,16},{16,12},{20,24},{24,20},{5,9},{9,5},{13,17},{1... | collective-permute-start | bytes 344072 | tf_op jit(solution)/shard_map/ppermute | solution.py:44
  5.2 0.1 slice.40
  5.2 0.1 slice.42
  5.3 0.1 fusion.11
  5.4 0.1 broadcast_select_fusion
  5.6 0.1 fusion.18
  5.7 0.1 fusion.15
  5.8 0.1 pad_maximum_fusion.2.all_1
  5.8 0.1 fusion.13
  5.9 0.1 fusion.6
  6.0 0.1 pad_maximum_fusion.1.mid_1
  6.1 0.1 fusion.19
  6.2 0.1 and_select_fusion.1
  6.4 0.1 fusion.14
  6.5 1.1 %load_tile.1 = (f32[6,64,128]{2,1,0:T(8,128)S(1)}, f32[6,64,128]{2,1,0:T(8,128)S(1)}, f32[64,128]{1,0:T(8,128)S(1)}, f32[64,128]{1,0:T(8,128)S(1)}, s32[64,128]{1,0:T(8,128)S(1)}) custom-call(s32[1,1,32]{2,1,0:T(1,128)} %flaw_in.3, f32[6,64,128]{2,1,0:T(8,128)} %disp_in.3, f32[6,64,128]{2,1,0:T(8,128)} %vel_in.3, f32[64,128]{1,0:T(8,128)} %dam_in.3, ...), custom_call_target="tpu_custom_call" | custom-call | tf_op jit(solution)/shard_map/load_tile/pallas_call | solution.py:507
  7.6 1.9 %collective-permute-done.1.got_b = f32[224,128]{1,0:T(8,128)S(1)} collective-permute-done((f32[224,128]{1,0:T(8,128)S(1)}, f32[224,128]{1,0:T(8,128)S(1)}, u32[]{:S(2)}, u32[]{:S(2)}) %collective-permute-start.1) | collective-permute-done | bytes 114720 | tf_op jit(solution)/shard_map/ppermute | solution.py:44
  9.5 0.4 %turn_and_cut.1 = (f32[224,128]{1,0:T(8,128)S(1)}, f32[224,128]{1,0:T(8,128)S(1)}, f32[15,144,128]{2,1,0:T(8,128)S(1)}) custom-call(f32[6,64,128]{2,1,0:T(8,128)S(1)} %get-tuple-element.18.disp, f32[6,64,128]{2,1,0:T(8,128)S(1)} %get-tuple-element.19.vel, f32[64,128]{1,0:T(8,128)S(1)} %get-tuple-element.20.dam, f32[64,128]{1,0:T(8,128)S(1)} %get-tuple-element.21.lim, ...), custom_call_target="tpu_custom_call" | custom-call | tf_op jit(solution)/shard_map/turn_and_cut/pallas_call | solution.py:516
  9.9 5.1 %collective-permute-start.2 = (f32[224,128]{1,0:T(8,128)S(1)}, f32[224,128]{1,0:T(8,128)S(1)}, u32[]{:S(2)}, u32[]{:S(2)}) collective-permute-start(f32[224,128]{1,0:T(8,128)S(1)} %get-tuple-element.31), channel_id=1, source_target_pairs={{1,2},{2,1},{5,6},{6,5},{9,10},{10,9},{13,14},{14,13},{17,18},{18,... | collective-permute-start | bytes 344072 | tf_op jit(solution)/shard_map/ppermute | solution.py:44
  15.1 0.1 pad_maximum_fusion.3.rim_1
  15.1 1.9 %inner_rows.1 = (f32[6,64,256]{2,1,0:T(8,128)S(1)}, f32[12,48,128]{2,1,0:T(8,128)S(1)}, f32[32,128]{1,0:T(8,128)S(1)}, f32[12,80,128]{2,1,0:T(8,128)S(1)}, f32[80,128]{1,0:T(8,128)S(1)}) custom-call(f32[15,144,128]{2,1,0:T(8,128)S(1)} %get-tuple-element.25.flat, bf16[256,256]{1,0:T(8,128)(2,1)S(1)} %maximum_maximum_fusion.band, ...), custom_call_target="tpu_custom_call" | custom-call | flops 800000000 | bytes 2000000 | tf_op jit(solution)/shard_map/inner_rows/pallas_call | solution.py:528
  17.1 0.4 %collective-permute-done.2.side_b = f32[224,128]{1,0:T(8,128)S(1)} collective-permute-done((f32[224,128]{1,0:T(8,128)S(1)}, f32[224,128]{1,0:T(8,128)S(1)}, u32[]{:S(2)}, u32[]{:S(2)}) %collective-permute-start.2) | collective-permute-done | bytes 114720 | tf_op jit(solution)/shard_map/ppermute | solution.py:44
  17.4 2.8 %two_steps.1 = (f32[6,64,128]{2,1,0:T(8,128)}, f32[6,64,128]{2,1,0:T(8,128)}, f32[64,128]{1,0:T(8,128)}) custom-call(f32[15,144,128]{2,1,0:T(8,128)S(1)} %get-tuple-element.25.flat, f32[6,64,256]{2,1,0:T(8,128)S(1)} %get-tuple-element.26.partial, f32[12,48,128]{2,1,0:T(8,128)S(1)} %get-tuple-element.27.moved, f32[32,128]{1,0:T(8,128)S(1)} %get-tuple-element.28.harmed_1, ...), custom_call_target="tpu_custom_call" | custom-call | tf_op jit(solution)/shard_map/two_steps/pallas_call | solution.py:553
  (12 shorter events, 0.2 us)
Async XLA Ops:
  1.8 5.8 %collective-permute-start = (f32[224,128]{1,0:T(8,128)S(1)}, f32[224,128]{1,0:T(8,128)S(1)}, u32[]{:S(2)}, u32[]{:S(2)}) collective-permute-start(f32[224,128]{1,0:T(8,128)S(1)} %get-tuple-element.23), channel_id=1, source_target_pairs={{0,4},{4,0},{8,12},{12,8},{16,20},{20,16},{24,28},{28,24},{1,5},{5... | collective-permute-start | bytes 344072 | tf_op jit(solution)/shard_map/ppermute | solution.py:44
  3.1 6.4 %collective-permute-start.1 = (f32[224,128]{1,0:T(8,128)S(1)}, f32[224,128]{1,0:T(8,128)S(1)}, u32[]{:S(2)}, u32[]{:S(2)}) collective-permute-start(f32[224,128]{1,0:T(8,128)S(1)} %get-tuple-element.24), channel_id=1, source_target_pairs={{4,8},{8,4},{12,16},{16,12},{20,24},{24,20},{5,9},{9,5},{13,17},{1... | collective-permute-start | bytes 344072 | tf_op jit(solution)/shard_map/ppermute | solution.py:44
  9.9 7.6 %collective-permute-start.2 = (f32[224,128]{1,0:T(8,128)S(1)}, f32[224,128]{1,0:T(8,128)S(1)}, u32[]{:S(2)}, u32[]{:S(2)}) collective-permute-start(f32[224,128]{1,0:T(8,128)S(1)} %get-tuple-element.31), channel_id=1, source_target_pairs={{1,2},{2,1},{5,6},{6,5},{9,10},{10,9},{13,14},{14,13},{17,18},{18,... | collective-permute-start | bytes 344072 | tf_op jit(solution)/shard_map/ppermute | solution.py:44
  15.0 2.5 %collective-permute-start.3 = (f32[224,128]{1,0:T(8,128)S(1)}, f32[224,128]{1,0:T(8,128)S(1)}, u32[]{:S(2)}, u32[]{:S(2)}) collective-permute-start(f32[224,128]{1,0:T(8,128)S(1)} %get-tuple-element.32), channel_id=1, source_target_pairs={{0,1},{1,0},{2,3},{3,2},{4,5},{5,4},{6,7},{7,6},{8,9},{9,8},{10,11... | collective-permute-start | bytes 344072 | tf_op jit(solution)/shard_map/ppermute | solution.py:44

commit v6 on v5

--- a/solution.py
+++ b/solution.py
@@ -16,6 +16,7 @@
 OFF = EDGE + 8
 HELD = CY + 2 * OFF
 LANES = 128
+GROUP = 3
 SLAB = 224
 K_STIFF = (1.0, 1.0, 0.0, 0.5, 0.5, 0.2)
 VISCOUS = 0.2
@@ -45,13 +46,13 @@
     return out
 
 
-def weakness(rows, flaw, first_row):
-    node = lax.broadcasted_iota(jnp.int32, (rows, CY), 0) * CY + lax.broadcasted_iota(
-        jnp.int32, (rows, CY), 1
-    )
-    mark = node == flaw[0, 0, 0] - first_row * CY
+def weakness(rows, flaw):
+    row = lax.broadcasted_iota(jnp.int32, (rows, CY), 0)
+    row = jnp.where(row < rows // 2, row, row + (CX - rows))
+    node = row * CY + lax.broadcasted_iota(jnp.int32, (rows, CY), 1)
+    mark = node == flaw[0, 0, 0]
     for j in range(1, flaw.shape[2]):
-        mark = mark | (node == flaw[0, 0, j] - first_row * CY)
+        mark = mark | (node == flaw[0, 0, j])
     return jnp.where(mark, 0.4, 1.0)
 
 
@@ -70,13 +71,12 @@
         near = pl.ds(side * (CX - 16), 16)
         pairs.append((disp_in.at[:, wide, :], disp.at[side]))
         pairs.append((vel_in.at[:, near, :], vel.at[side]))
-        for src, dst in ((dam_in, dam), (stren_in, stren), (con_in, con)):
-            pairs.append((src.at[near, :], dst.at[side]))
+    pairs += [(dam_in, dam), (stren_in, stren), (con_in, con)]
     others = run_copies(pairs, sems)
-    factors = [weakness(16, flaw, side * (CX - 16)) for side in range(2)]
+    factor = weakness(32, flaw)
     for copy in others:
         copy.wait()
-    limits = [stren[side] * factors[side] for side in range(2)]
+    limits = [stren[0:16, :] * factor[0:16], stren[CX - 16 :, :] * factor[16:32]]
 
     def fill(out, side):
         for k in range(15):
@@ -87,12 +87,11 @@
                 part = disp[side, k, rows, :]
             elif k < 12:
                 part = vel[side, k - 6, rows, :]
-            elif k == 12:
-                part = dam[side, rows, :]
             elif k == 13:
                 part = limits[side][rows, :]
             else:
-                part = con[side, rows, :].astype(F32)
+                rows = slice(CX - width, CX) if side else rows
+                part = (dam if k == 12 else con)[rows, :].astype(F32)
             out[start : start + width, :] = part
         out[219:SLAB, :] = jnp.zeros((SLAB - 219, LANES), F32)
 
@@ -117,7 +116,7 @@
         ),
         sems,
     )
-    factor = weakness(CX, flaw, 0)
+    factor = weakness(CX, flaw)
     for copy in others:
         copy.wait()
     lim[...] = stren[...] * factor
@@ -191,6 +190,16 @@
         cols = slice(ch % 2 * LANES, (ch % 2 + 1) * LANES)
         turned[ch // 2, 0:rows, cols] = high
         turned[ch // 2, rows : 2 * rows, cols] = low
+
+
+def block_sums(energy, turned, block, rows, band):
+    both = jnp.dot(energy[block], band[...], preferred_element_type=F32)
+    high, low = split(both[:, :LANES] + both[:, LANES:])
+    for ch in range(12):
+        cols = slice(ch % 2 * LANES, (ch % 2 + 1) * LANES)
+        part = slice(16 * ch, 16 * ch + 16)
+        turned[ch // 2, 16 * block : 16 * block + 16, cols] = high[part]
+        turned[ch // 2, rows + 16 * block : rows + 16 * block + 16, cols] = low[part]
 
 
 def row_sums(turned, pair, rows, first, second):
@@ -289,16 +298,22 @@
     return new
 
 
-def gather(state, off, starts, energy, turned, band):
+def gather(state, off, starts, energy, turned, band, by_block=False):
     for n, b in enumerate(starts):
         def get(k, shift):
             return state[k, off + b + shift : off + b + shift + 16, :]
 
         def put(ch, cols, value):
-            energy[ch, 16 * n : 16 * n + 16, cols] = value
+            if by_block:
+                energy[n, 16 * ch : 16 * ch + 16, cols] = value
+            else:
+                energy[ch, 16 * n : 16 * n + 16, cols] = value
 
         products(get, put)
-    lane_sums(energy, turned, 16 * len(starts), band)
+        if by_block:
+            block_sums(energy, turned, n, 16 * len(starts), band)
+    if not by_block:
+        lane_sums(energy, turned, 16 * len(starts), band)
 
 
 def inner_kernel(
@@ -384,7 +399,7 @@
         new = harm(b, row, aver, rows_of(ext.at[13], OFF, b), old, hd, cover, decay)
         ext[12, OFF + b : OFF + b + 8, :] = new
 
-    gather(ext, OFF, (-24, -8, 120, 136), energy, turned, band)
+    gather(ext, OFF, (-24, -8, 120, 136), energy, turned, band, True)
     for pair in range(6):
         aver[pair] = partial[pair] + row_sums(turned, pair, 64, rim_1, rim_2)
     for row, b in enumerate((*range(-16, 16, 8), *range(112, 144, 8))):
@@ -396,7 +411,7 @@
     move(-16, 16, ext, OFF, hd, contact, rate, wp, fm, put_next)
     move(112, 144, ext, OFF, hd, contact, rate, wp, fm, put_next)
 
-    gather(ext2, OFF, (-16, 0, 16, 96, 112, 128), energy, turned, band)
+    gather(ext2, OFF, (-16, 0, 16, 96, 112, 128), energy, turned, band, True)
     for pair in range(6):
         aver[pair] = row_sums(turned, pair, 96, all_1, all_2)
     for row, b in enumerate((*range(-8, 24, 8), *range(104, 136, 8))):
@@ -406,22 +421,23 @@
         hd[OFF + low : OFF + low + 8, :] = 0.5 - 0.5 * harmed_2[low - 24 : low - 16, :]
     copies = []
 
-    def send(n, field, out):
-        done[n] = field.T[PAD : PAD + CX, :]
-        copy = pltpu.make_async_copy(done.at[n], out, sems.at[n])
+    def send(start, fields, out):
+        for n, field in enumerate(fields):
+            done[start + n] = field.T[PAD : PAD + CX, :]
+        copy = pltpu.make_async_copy(done.at[pl.ds(start, len(fields))], out, sems.at[len(copies)])
         copy.start()
         copies.append(copy)
 
-    send(12, ext[12, OFF : OFF + CY, :], out_d)
+    send(12, [ext[12, OFF : OFF + CY, :]], out_d)
 
     def put_last(k, b, value):
         final[k, b : b + 8, :] = value
 
     move(0, 24, ext2, OFF, hd, contact, rate, wp, fm, put_last)
     move(104, CY, ext2, OFF, hd, contact, rate, wp, fm, put_last)
-    for k in range(6):
-        send(k, final[k], out_u.at[k])
-        send(6 + k, final[6 + k], out_v.at[k])
+    for start in range(0, 12, GROUP):
+        out = out_u if start < 6 else out_v
+        send(start, [final[start + n] for n in range(GROUP)], out.at[pl.ds(start % 6, GROUP)])
     for copy in copies:
         copy.wait()
 
@@ -493,11 +509,11 @@
         scratch_shapes=[
             pltpu.VMEM((2, 6, 24, CY), F32),
             pltpu.VMEM((2, 6, 16, CY), F32),
-            pltpu.VMEM((2, 16, CY), F32),
-            pltpu.VMEM((2, 16, CY), F32),
-            pltpu.VMEM((2, 16, CY), jnp.int32),
+            pltpu.VMEM((CX, CY), F32),
+            pltpu.VMEM((CX, CY), F32),
+            pltpu.VMEM((CX, CY), jnp.int32),
             flaw_copy,
-            pltpu.SemaphoreType.DMA((11,)),
+            pltpu.SemaphoreType.DMA((8,)),
         ],
         compiler_params=params,
         name="pack_rows",
@@ -552,7 +568,7 @@
     )(flat, band, *of_own)
     out = pl.pallas_call(
         step_kernel,
-        out_shape=[shape((6, CX, CY), F32)] * 2 + [shape((CX, CY), F32)],
+        out_shape=[shape((6, CX, CY), F32)] * 2 + [shape((1, CX, CY), F32)],
         in_specs=vmem(16),
         out_specs=[pl.BlockSpec(memory_space=pltpu.HBM)] * 3,
         scratch_shapes=[
@@ -561,17 +577,17 @@
             pltpu.VMEM((8, HELD, LANES), F32),
             pltpu.VMEM((6, HELD, LANES), F32),
             held,
-            pltpu.VMEM((12, 96, 2 * LANES), BF16),
+            pltpu.VMEM((6, 192, 2 * LANES), BF16),
             pltpu.VMEM((6, 192, 2 * LANES), BF16),
             pltpu.VMEM((6, 64, 2 * LANES), F32),
             pltpu.VMEM((12, CY, LANES), F32),
             pltpu.VMEM((13, CX, CY), F32),
-            pltpu.SemaphoreType.DMA((13,)),
+            pltpu.SemaphoreType.DMA((13 // GROUP + 1,)),
         ],
         compiler_params=params,
         name="two_steps",
     )(flat, *inner, *side[::-1], band, *table)
-    return tuple(out)
+    return out[0], out[1], out[2].reshape(CX, CY)
 
 
 def solution(mesh):

time: 20.5 us -> 20.3 us (level)
  no operation moved by 1% of the time
where the time goes in v6:
time: 20.3 us; the launch traced here: 20.1 us
  starting transfers between devices  8.49 us (42%)
  Pallas kernels  7.15 us (35%)
  waiting for transfers between devices  2.3 us (11%)
  other arithmetic  1.04 us (5%)
  between operations  0.81 us (4%)
  local copies, waits for them, and re-layouts  0.31 us (2%)
    ppermute x4, starting transfers between devices, swap(): out.append(lax.ppermute(part, axis, pairs))  8.49 us
    pallas_call x1, Pallas kernels, on_device(): pl.pallas_call(step_kernel, out_shape=[shape((6, CX, CY), F32)] * 2 + [sh...  2.74 us
    ppermute x4, waiting for transfers between devices, swap(): out.append(lax.ppermute(part, axis, pairs))  2.3 us
    pallas_call x1, Pallas kernels, on_device(): pl.pallas_call(inner_kernel, out_shape=[shape((6, 64, 2 * LANES), F32), s...  1.91 us
    pallas_call x1, Pallas kernels, on_device(): pl.pallas_call(load_kernel, out_shape=[shape((6, CX, CY), F32)] * 2 + [ti...  1.09 us
    pallas_call x1, Pallas kernels, on_device(): pl.pallas_call(pack_kernel, out_shape=[shape((SLAB, LANES), F32)] * 2, in...  1.06 us
  transfers between devices with their start and end apart: 4, of which 2 were waited for; matrix products, arithmetic and copies ran while one was open for 7% of the time, Pallas kernels for 15%

profile of v6, /device:TPU:25, one launch (start us, length us, event | category | flops | bytes accessed | tf_op | source)
XLA Modules:
  0.0 20.1 jit_solution(16511640722068161001)
XLA Ops:
  0.6 1.1 %pack_rows.1 = (f32[224,128]{1,0:T(8,128)S(1)}, f32[224,128]{1,0:T(8,128)S(1)}) custom-call(s32[1,1,32]{2,1,0:T(1,128)} %flaw_in.3, f32[6,64,128]{2,1,0:T(8,128)} %disp_in.3, f32[6,64,128]{2,1,0:T(8,128)} %vel_in.3, f32[64,128]{1,0:T(8,128)} %dam_in.3, f32[64,128]{1,0:T(8,128)} %stren_in.3, s32[64,128]{1,0:T(8,128)} %con_in.3), custom_call_target="tpu_custom_call" | custom-call | tf_op jit(solution)/shard_map/pack_rows/pallas_call | solution.py:504
  1.7 1.3 %collective-permute-start = (f32[224,128]{1,0:T(8,128)S(1)}, f32[224,128]{1,0:T(8,128)S(1)}, u32[]{:S(2)}, u32[]{:S(2)}) collective-permute-start(f32[224,128]{1,0:T(8,128)S(1)} %get-tuple-element.26), channel_id=1, source_target_pairs={{0,4},{4,0},{8,12},{12,8},{16,20},{20,16},{24,28},{28,24},{1,5},{5... | collective-permute-start | bytes 344072 | tf_op jit(solution)/shard_map/ppermute | solution.py:45
  3.0 2.0 %collective-permute-start.1 = (f32[224,128]{1,0:T(8,128)S(1)}, f32[224,128]{1,0:T(8,128)S(1)}, u32[]{:S(2)}, u32[]{:S(2)}) collective-permute-start(f32[224,128]{1,0:T(8,128)S(1)} %get-tuple-element.27), channel_id=1, source_target_pairs={{4,8},{8,4},{12,16},{16,12},{20,24},{24,20},{5,9},{9,5},{13,17},{1... | collective-permute-start | bytes 344072 | tf_op jit(solution)/shard_map/ppermute | solution.py:45
  5.1 0.1 slice.40
  5.2 0.1 slice.42
  5.2 0.1 fusion.11
  5.3 0.1 broadcast_select_fusion
  5.5 0.1 fusion.18
  5.6 0.1 fusion.15
  5.7 0.1 pad_maximum_fusion.2.all_1
  5.8 0.1 fusion.13
  5.9 0.1 fusion.6
  6.0 0.1 pad_maximum_fusion.1.mid_1
  6.1 0.1 fusion.19
  6.2 0.1 and_select_fusion.1
  6.3 0.1 fusion.14
  6.4 1.1 %load_tile.1 = (f32[6,64,128]{2,1,0:T(8,128)S(1)}, f32[6,64,128]{2,1,0:T(8,128)S(1)}, f32[64,128]{1,0:T(8,128)S(1)}, f32[64,128]{1,0:T(8,128)S(1)}, s32[64,128]{1,0:T(8,128)S(1)}) custom-call(s32[1,1,32]{2,1,0:T(1,128)} %flaw_in.3, f32[6,64,128]{2,1,0:T(8,128)} %disp_in.3, f32[6,64,128]{2,1,0:T(8,128)} %vel_in.3, f32[64,128]{1,0:T(8,128)} %dam_in.3, ...), custom_call_target="tpu_custom_call" | custom-call | tf_op jit(solution)/shard_map/load_tile/pallas_call | solution.py:523
  7.5 1.9 %collective-permute-done.1.got_b = f32[224,128]{1,0:T(8,128)S(1)} collective-permute-done((f32[224,128]{1,0:T(8,128)S(1)}, f32[224,128]{1,0:T(8,128)S(1)}, u32[]{:S(2)}, u32[]{:S(2)}) %collective-permute-start.1) | collective-permute-done | bytes 114720 | tf_op jit(solution)/shard_map/ppermute | solution.py:45
  9.4 0.4 %turn_and_cut.1 = (f32[224,128]{1,0:T(8,128)S(1)}, f32[224,128]{1,0:T(8,128)S(1)}, f32[15,144,128]{2,1,0:T(8,128)S(1)}) custom-call(f32[6,64,128]{2,1,0:T(8,128)S(1)} %get-tuple-element.21.disp, f32[6,64,128]{2,1,0:T(8,128)S(1)} %get-tuple-element.22.vel, f32[64,128]{1,0:T(8,128)S(1)} %get-tuple-element.23.dam, f32[64,128]{1,0:T(8,128)S(1)} %get-tuple-element.24.lim, ...), custom_call_target="tpu_custom_call" | custom-call | tf_op jit(solution)/shard_map/turn_and_cut/pallas_call | solution.py:532
  9.8 5.1 %collective-permute-start.2 = (f32[224,128]{1,0:T(8,128)S(1)}, f32[224,128]{1,0:T(8,128)S(1)}, u32[]{:S(2)}, u32[]{:S(2)}) collective-permute-start(f32[224,128]{1,0:T(8,128)S(1)} %get-tuple-element.34), channel_id=1, source_target_pairs={{1,2},{2,1},{5,6},{6,5},{9,10},{10,9},{13,14},{14,13},{17,18},{18,... | collective-permute-start | bytes 344072 | tf_op jit(solution)/shard_map/ppermute | solution.py:45
  15.0 0.1 pad_maximum_fusion.3.rim_1
  15.1 1.9 %inner_rows.1 = (f32[6,64,256]{2,1,0:T(8,128)S(1)}, f32[12,48,128]{2,1,0:T(8,128)S(1)}, f32[32,128]{1,0:T(8,128)S(1)}, f32[12,80,128]{2,1,0:T(8,128)S(1)}, f32[80,128]{1,0:T(8,128)S(1)}) custom-call(f32[15,144,128]{2,1,0:T(8,128)S(1)} %get-tuple-element.28.flat, bf16[256,256]{1,0:T(8,128)(2,1)S(1)} %maximum_maximum_fusion.band, ...), custom_call_target="tpu_custom_call" | custom-call | flops 800000000 | bytes 2000000 | tf_op jit(solution)/shard_map/inner_rows/pallas_call | solution.py:544
  17.0 0.4 %collective-permute-done.2.side_b = f32[224,128]{1,0:T(8,128)S(1)} collective-permute-done((f32[224,128]{1,0:T(8,128)S(1)}, f32[224,128]{1,0:T(8,128)S(1)}, u32[]{:S(2)}, u32[]{:S(2)}) %collective-permute-start.2) | collective-permute-done | bytes 114720 | tf_op jit(solution)/shard_map/ppermute | solution.py:45
  17.4 2.7 %two_steps.1 = (f32[6,64,128]{2,1,0:T(8,128)}, f32[6,64,128]{2,1,0:T(8,128)}, f32[1,64,128]{2,1,0:T(8,128)}) custom-call(f32[15,144,128]{2,1,0:T(8,128)S(1)} %get-tuple-element.28.flat, f32[6,64,256]{2,1,0:T(8,128)S(1)} %get-tuple-element.29.partial, f32[12,48,128]{2,1,0:T(8,128)S(1)} %get-tuple-element.30.moved, f32[32,128]{1,0:T(8,128)S(1)} %get-tuple-element.31.harmed_1, ...), custom_call_target="tpu_custom_call" | custom-call | tf_op jit(solution)/shard_map/two_steps/pallas_call | solution.py:569
  (12 shorter events, 0.2 us)
Async XLA Ops:
  1.7 5.8 %collective-permute-start = (f32[224,128]{1,0:T(8,128)S(1)}, f32[224,128]{1,0:T(8,128)S(1)}, u32[]{:S(2)}, u32[]{:S(2)}) collective-permute-start(f32[224,128]{1,0:T(8,128)S(1)} %get-tuple-element.26), channel_id=1, source_target_pairs={{0,4},{4,0},{8,12},{12,8},{16,20},{20,16},{24,28},{28,24},{1,5},{5... | collective-permute-start | bytes 344072 | tf_op jit(solution)/shard_map/ppermute | solution.py:45
  3.0 6.4 %collective-permute-start.1 = (f32[224,128]{1,0:T(8,128)S(1)}, f32[224,128]{1,0:T(8,128)S(1)}, u32[]{:S(2)}, u32[]{:S(2)}) collective-permute-start(f32[224,128]{1,0:T(8,128)S(1)} %get-tuple-element.27), channel_id=1, source_target_pairs={{4,8},{8,4},{12,16},{16,12},{20,24},{24,20},{5,9},{9,5},{13,17},{1... | collective-permute-start | bytes 344072 | tf_op jit(solution)/shard_map/ppermute | solution.py:45
  9.8 7.6 %collective-permute-start.2 = (f32[224,128]{1,0:T(8,128)S(1)}, f32[224,128]{1,0:T(8,128)S(1)}, u32[]{:S(2)}, u32[]{:S(2)}) collective-permute-start(f32[224,128]{1,0:T(8,128)S(1)} %get-tuple-element.34), channel_id=1, source_target_pairs={{1,2},{2,1},{5,6},{6,5},{9,10},{10,9},{13,14},{14,13},{17,18},{18,... | collective-permute-start | bytes 344072 | tf_op jit(solution)/shard_map/ppermute | solution.py:45
  14.9 2.5 %collective-permute-start.3 = (f32[224,128]{1,0:T(8,128)S(1)}, f32[224,128]{1,0:T(8,128)S(1)}, u32[]{:S(2)}, u32[]{:S(2)}) collective-permute-start(f32[224,128]{1,0:T(8,128)S(1)} %get-tuple-element.35), channel_id=1, source_target_pairs={{0,1},{1,0},{2,3},{3,2},{4,5},{5,4},{6,7},{7,6},{8,9},{9,8},{10,11... | collective-permute-start | bytes 344072 | tf_op jit(solution)/shard_map/ppermute | solution.py:45

commit v7 on v6

--- a/solution.py
+++ b/solution.py
@@ -108,7 +108,7 @@
         fill(out_b, 1)
 
 
-def load_kernel(flaw_in, disp_in, vel_in, dam_in, stren_in, con_in, disp, vel, dam, lim, con, stren, flaw, sems):
+def load_kernel(flaw_in, disp_in, vel_in, dam_in, stren_in, con_in, own, disp, vel, dam, stren, con, flaw, sems):
     others = run_copies(
         zip(
             (flaw_in, disp_in, vel_in, dam_in, stren_in, con_in),
@@ -119,35 +119,44 @@
     factor = weakness(CX, flaw)
     for copy in others:
         copy.wait()
-    lim[...] = stren[...] * factor
-
-
-def edge_kernel(disp, vel, dam, lim, con, got_a, got_b, out_a, out_b, flat, ext):
+    before, behind = jnp.zeros((PAD, CY), F32), jnp.zeros((LANES - PAD - CX, CY), F32)
+    fields = [disp[k] for k in range(6)] + [vel[k] for k in range(6)]
+    fields += [dam[...], stren[...] * factor, con[...].astype(F32)]
+    for k, field in enumerate(fields):
+        own[k] = jnp.concatenate([before, field, behind], 0).T
+
+
+def turned_halo(got_a, got_b):
     even = lax.rem(lax.axis_index("transit"), 2) == 0
-    even_l = lax.rem(lax.axis_index("lateral"), 2) == 0
+    lower, upper = [], []
+    for rows in (slice(0, LANES), slice(SLAB - LANES, SLAB)):
+        part_a, part_b = got_a[rows, :].T, got_b[rows, :].T
+        lower.append(jnp.where(even, part_b, part_a))
+        upper.append(jnp.where(even, part_a, part_b))
+    return lower, upper
+
+
+def with_halo(k, rows, own, halo):
+    width, start = halo_of(k), slab_start(k)
+    piece = int(start + width > LANES)
+    start -= piece * (SLAB - LANES)
+    lower, upper = (x[piece][rows, :] for x in halo)
+    lane = lax.broadcasted_iota(jnp.int32, lower.shape, 1)
+    lower = pltpu.roll(lower, (PAD - width - start) % LANES, 1)
+    upper = pltpu.roll(upper, (PAD + CX - start) % LANES, 1)
+    return jnp.where(lane < PAD, lower, jnp.where(lane < PAD + CX, own[k, rows, :], upper))
+
+
+def edge_kernel(own, got_a, got_b, out_a, out_b):
+    even = lax.rem(lax.axis_index("lateral"), 2) == 0
+    halo = turned_halo(got_a, got_b)
     for k in range(15):
         width, start = halo_of(k), slab_start(k)
-        part_a = got_a[start : start + width, :]
-        part_b = got_b[start : start + width, :]
-        if k < 6:
-            own = disp[k]
-        elif k < 12:
-            own = vel[k - 6]
-        else:
-            own = (dam, lim, con)[k - 12][...].astype(F32)
-        low, high = PAD, PAD + CX
-        ext[k, 0 : low - width, :] = jnp.zeros((low - width, LANES), F32)
-        ext[k, low - width : low, :] = jnp.where(even, part_b, part_a)
-        ext[k, low:high, :] = own
-        ext[k, high : high + width, :] = jnp.where(even, part_a, part_b)
-        ext[k, high + width : LANES, :] = jnp.zeros((LANES - high - width, LANES), F32)
-        turned = ext[k].T
-        flat[k, 8 : 8 + CY, :] = turned
-        flat[k, 0:8, :] = jnp.zeros((8, LANES), F32)
-        flat[k, 8 + CY : 16 + CY, :] = jnp.zeros((8, LANES), F32)
-        right, left = turned[CY - width :, :], turned[:width, :]
-        out_a[start : start + width, :] = jnp.where(even_l, right, left)
-        out_b[start : start + width, :] = jnp.where(even_l, left, right)
+        held = 24 if k < 6 else 16
+        left = with_halo(k, slice(0, held), own, halo)[:width]
+        right = with_halo(k, slice(CY - held, CY), own, halo)[held - width :]
+        out_a[start : start + width, :] = jnp.where(even, right, left)
+        out_b[start : start + width, :] = jnp.where(even, left, right)
     for out in (out_a, out_b):
         out[219:SLAB, :] = jnp.zeros((SLAB - 219, LANES), F32)
 
@@ -317,10 +326,15 @@
 
 
 def inner_kernel(
-    flat, band, first, second, mid_1, mid_2, cover, decay, rate,
-    partial, moved, harmed_1, final, harmed_2,
+    own, got_a, got_b, band, first, second, mid_1, mid_2, cover, decay, rate,
+    flat, partial, moved, harmed_1, final, harmed_2,
     next_state, energy, turned, aver, old, wp, fm, hd,
 ):
+    halo = turned_halo(got_a, got_b)
+    for k in range(15):
+        flat[k, 0:8, :] = jnp.zeros((8, LANES), F32)
+        flat[k, 8 : 8 + CY, :] = with_halo(k, slice(0, CY), own, halo)
+        flat[k, 8 + CY : 16 + CY, :] = jnp.zeros((8, LANES), F32)
     for low in (0, 120):
         hd[OFF + low : OFF + low + 8, :] = jnp.full((8, LANES), 0.5, F32)
         for k in range(6):
@@ -519,39 +533,47 @@
         name="pack_rows",
     )(*inputs)
     got = swap((send_a, send_b), "transit")
-    tile = shape((CX, CY), F32)
+    tile = pltpu.VMEM((CX, CY), F32)
     own = pl.pallas_call(
         load_kernel,
-        out_shape=[shape((6, CX, CY), F32)] * 2 + [tile, tile, shape((CX, CY), jnp.int32)],
+        out_shape=shape((15, CY, LANES), F32),
         in_specs=[pl.BlockSpec(memory_space=pltpu.HBM)] * 6,
-        out_specs=vmem(5),
-        scratch_shapes=[pltpu.VMEM((CX, CY), F32), flaw_copy, pltpu.SemaphoreType.DMA((6,))],
+        out_specs=vmem(1)[0],
+        scratch_shapes=[
+            pltpu.VMEM((6, CX, CY), F32),
+            pltpu.VMEM((6, CX, CY), F32),
+            tile,
+            tile,
+            pltpu.VMEM((CX, CY), jnp.int32),
+            flaw_copy,
+            pltpu.SemaphoreType.DMA((6,)),
+        ],
         compiler_params=params,
         name="load_tile",
     )(*inputs)
-    side_a, side_b, flat = pl.pallas_call(
+    side = pl.pallas_call(
         edge_kernel,
-        out_shape=[shape((SLAB, LANES), F32)] * 2 + [shape((15, 16 + CY, LANES), F32)],
-        in_specs=vmem(7),
-        out_specs=vmem(3),
-        scratch_shapes=[pltpu.VMEM((15, LANES, LANES), F32)],
+        out_shape=[shape((SLAB, LANES), F32)] * 2,
+        in_specs=vmem(3),
+        out_specs=vmem(2),
         compiler_params=params,
-        name="turn_and_cut",
-    )(*own, *got)
-    side = swap((side_a, side_b), "lateral")
+        name="cut_columns",
+    )(own, *got)
+    side = swap(side, "lateral")
     band, of_own, table = tables(CX * lax.axis_size("transit"), CY * lax.axis_size("lateral"))
     held = pltpu.VMEM((HELD, LANES), F32)
     inner = pl.pallas_call(
         inner_kernel,
         out_shape=[
+            shape((15, 16 + CY, LANES), F32),
             shape((6, 64, 2 * LANES), F32),
             shape((12, 48, LANES), F32),
             shape((32, LANES), F32),
             shape((12, 80, LANES), F32),
             shape((80, LANES), F32),
         ],
-        in_specs=vmem(9),
-        out_specs=vmem(5),
+        in_specs=vmem(11),
+        out_specs=vmem(6),
         scratch_shapes=[
             pltpu.VMEM((12, HELD, LANES), F32),
             pltpu.VMEM((12, CY, 2 * LANES), BF16),
@@ -565,7 +587,7 @@
         compiler_params=params,
         cost_estimate=pl.CostEstimate(flops=800_000_000, bytes_accessed=2_000_000, transcendentals=0),
         name="inner_rows",
-    )(flat, band, *of_own)
+    )(own, *got, band, *of_own)
     out = pl.pallas_call(
         step_kernel,
         out_shape=[shape((6, CX, CY), F32)] * 2 + [shape((1, CX, CY), F32)],
@@ -586,7 +608,7 @@
         ],
         compiler_params=params,
         name="two_steps",
-    )(flat, *inner, *side[::-1], band, *table)
+    )(*inner, *side[::-1], band, *table)
     return out[0], out[1], out[2].reshape(CX, CY)
 
 

time: 20.3 us -> 20.3 us (level)
  Pallas kernels: 7.15 us -> 7.87 us
  waiting for transfers between devices: 2.3 us -> 1.58 us
    ppermute x4, waiting for transfers between devices: 2.3 us -> 1.58 us  [swap(): out.append(lax.ppermute(part, axis, pairs))]
    pallas_call x3, Pallas kernels: 3.36 us -> 4.07 us  [the longest x1 2.34 us: on_device(): pl.pallas_call(inner_kernel, out_shape=[shape((15, 16 + CY, LANES), F32),...]
  transfers between devices with their start and end apart: 4 -> 4, of which waited for: 2 -> 1; matrix products, arithmetic and copies ran while one was open for 7% -> 7% of each run, Pallas kernels for 15% -> 19%
where the time goes in v7:
time: 20.3 us; the launch traced here: 20.1 us
  starting transfers between devices  8.49 us (42%)
  Pallas kernels  7.87 us (39%)
  waiting for transfers between devices  1.58 us (8%)
  other arithmetic  1.03 us (5%)
  between operations  0.83 us (4%)
  local copies, waits for them, and re-layouts  0.31 us (2%)
    ppermute x4, starting transfers between devices, swap(): out.append(lax.ppermute(part, axis, pairs))  8.49 us
    pallas_call x1, Pallas kernels, on_device(): pl.pallas_call(step_kernel, out_shape=[shape((6, CX, CY), F32)] * 2 + [sh...  2.74 us
    pallas_call x1, Pallas kernels, on_device(): pl.pallas_call(inner_kernel, out_shape=[shape((15, 16 + CY, LANES), F32),...  2.34 us
    ppermute x4, waiting for transfers between devices, swap(): out.append(lax.ppermute(part, axis, pairs))  1.58 us
    pallas_call x1, Pallas kernels, on_device(): pl.pallas_call(load_kernel, out_shape=shape((15, CY, LANES), F32), in_spe...  1.43 us
    pallas_call x1, Pallas kernels, on_device(): pl.pallas_call(pack_kernel, out_shape=[shape((SLAB, LANES), F32)] * 2, in...  1.06 us
  transfers between devices with their start and end apart: 4, of which 1 were waited for; matrix products, arithmetic and copies ran while one was open for 7% of the time, Pallas kernels for 19%

profile of v7, /device:TPU:25, one launch (start us, length us, event | category | flops | bytes accessed | tf_op | source)
XLA Modules:
  0.0 20.1 jit_solution(11894967538867194953)
XLA Ops:
  0.6 1.1 %pack_rows.1 = (f32[224,128]{1,0:T(8,128)S(1)}, f32[224,128]{1,0:T(8,128)S(1)}) custom-call(s32[1,1,32]{2,1,0:T(1,128)} %flaw_in.3, f32[6,64,128]{2,1,0:T(8,128)} %disp_in.3, f32[6,64,128]{2,1,0:T(8,128)} %vel_in.3, f32[64,128]{1,0:T(8,128)} %dam_in.3, f32[64,128]{1,0:T(8,128)} %stren_in.3, s32[64,128]{1,0:T(8,128)} %con_in.3), custom_call_target="tpu_custom_call" | custom-call | tf_op jit(solution)/shard_map/pack_rows/pallas_call | solution.py:518
  1.7 1.3 %collective-permute-start = (f32[224,128]{1,0:T(8,128)S(1)}, f32[224,128]{1,0:T(8,128)S(1)}, u32[]{:S(2)}, u32[]{:S(2)}) collective-permute-start(f32[224,128]{1,0:T(8,128)S(1)} %get-tuple-element.16), channel_id=1, source_target_pairs={{0,4},{4,0},{8,12},{12,8},{16,20},{20,16},{24,28},{28,24},{1,5},{5... | collective-permute-start | bytes 344072 | tf_op jit(solution)/shard_map/ppermute | solution.py:45
  3.0 2.0 %collective-permute-start.1 = (f32[224,128]{1,0:T(8,128)S(1)}, f32[224,128]{1,0:T(8,128)S(1)}, u32[]{:S(2)}, u32[]{:S(2)}) collective-permute-start(f32[224,128]{1,0:T(8,128)S(1)} %get-tuple-element.17), channel_id=1, source_target_pairs={{4,8},{8,4},{12,16},{16,12},{20,24},{24,20},{5,9},{9,5},{13,17},{1... | collective-permute-start | bytes 344072 | tf_op jit(solution)/shard_map/ppermute | solution.py:45
  5.1 0.1 slice.40
  5.2 0.1 slice.42
  5.2 0.1 fusion.11
  5.3 0.1 broadcast_select_fusion
  5.5 0.1 fusion.18
  5.6 0.1 fusion.15
  5.7 0.1 pad_maximum_fusion.2.all_1
  5.8 0.1 fusion.13
  5.9 0.1 fusion.6
  6.0 0.1 pad_maximum_fusion.1.mid_1
  6.1 0.1 fusion.19
  6.2 0.1 and_select_fusion.1
  6.3 0.1 fusion.14
  6.4 1.4 %load_tile.1.own = f32[15,128,128]{2,1,0:T(8,128)S(1)} custom-call(s32[1,1,32]{2,1,0:T(1,128)} %flaw_in.3, f32[6,64,128]{2,1,0:T(8,128)} %disp_in.3, f32[6,64,128]{2,1,0:T(8,128)} %vel_in.3, f32[64,128]{1,0:T(8,128)} %dam_in.3, f32[64,128]{1,0:T(8,128)} %stren_in.3, s32[64,128]{1,0:T(8,128)} %con_in.3), custom_call_target="tpu_custom_call" | custom-call | tf_op jit(solution)/shard_map/load_tile/pallas_call | solution.py:537
  7.9 1.6 %collective-permute-done.1.got_b = f32[224,128]{1,0:T(8,128)S(1)} collective-permute-done((f32[224,128]{1,0:T(8,128)S(1)}, f32[224,128]{1,0:T(8,128)S(1)}, u32[]{:S(2)}, u32[]{:S(2)}) %collective-permute-start.1) | collective-permute-done | bytes 114720 | tf_op jit(solution)/shard_map/ppermute | solution.py:45
  9.4 0.3 %cut_columns.1 = (f32[224,128]{1,0:T(8,128)S(1)}, f32[224,128]{1,0:T(8,128)S(1)}) custom-call(f32[15,128,128]{2,1,0:T(8,128)S(1)} %load_tile.1.own, f32[224,128]{1,0:T(8,128)S(1)} %collective-permute-done.got_a, f32[224,128]{1,0:T(8,128)S(1)} %collective-permute-done.1.got_b), custom_call_target="tpu_custom_call" | custom-call | tf_op jit(solution)/shard_map/cut_columns/pallas_call | solution.py:554
  9.7 5.1 %collective-permute-start.2 = (f32[224,128]{1,0:T(8,128)S(1)}, f32[224,128]{1,0:T(8,128)S(1)}, u32[]{:S(2)}, u32[]{:S(2)}) collective-permute-start(f32[224,128]{1,0:T(8,128)S(1)} %get-tuple-element.24), channel_id=1, source_target_pairs={{1,2},{2,1},{5,6},{6,5},{9,10},{10,9},{13,14},{14,13},{17,18},{18,... | collective-permute-start | bytes 344072 | tf_op jit(solution)/shard_map/ppermute | solution.py:45
  14.9 0.1 collective-permute-start.3
  14.9 0.1 pad_maximum_fusion.3.rim_1
  15.0 2.3 %inner_rows.1 = (f32[15,144,128]{2,1,0:T(8,128)S(1)}, f32[6,64,256]{2,1,0:T(8,128)S(1)}, f32[12,48,128]{2,1,0:T(8,128)S(1)}, f32[32,128]{1,0:T(8,128)S(1)}, f32[...) custom-call(f32[15,128,128]{2,1,0:T(8,128)S(1)} %load_tile.1.own, f32[224,128]{1,0:T(8,128)S(1)} %collective-permute-done.got_a, ...), custom_call_target="tpu_custom_call" | custom-call | flops 800000000 | bytes 2000000 | tf_op jit(solution)/shard_map/inner_rows/pallas_call | solution.py:565
  17.4 2.7 %two_steps.1 = (f32[6,64,128]{2,1,0:T(8,128)}, f32[6,64,128]{2,1,0:T(8,128)}, f32[1,64,128]{2,1,0:T(8,128)}) custom-call(f32[15,144,128]{2,1,0:T(8,128)S(1)} %get-tuple-element.18.flat, f32[6,64,256]{2,1,0:T(8,128)S(1)} %get-tuple-element.19.partial, f32[12,48,128]{2,1,0:T(8,128)S(1)} %get-tuple-element.20.moved, f32[32,128]{1,0:T(8,128)S(1)} %get-tuple-element.21.harmed_1, ...), custom_call_target="tpu_custom_call" | custom-call | tf_op jit(solution)/shard_map/two_steps/pallas_call | solution.py:591
  (12 shorter events, 0.1 us)
Async XLA Ops:
  1.7 6.2 %collective-permute-start = (f32[224,128]{1,0:T(8,128)S(1)}, f32[224,128]{1,0:T(8,128)S(1)}, u32[]{:S(2)}, u32[]{:S(2)}) collective-permute-start(f32[224,128]{1,0:T(8,128)S(1)} %get-tuple-element.16), channel_id=1, source_target_pairs={{0,4},{4,0},{8,12},{12,8},{16,20},{20,16},{24,28},{28,24},{1,5},{5... | collective-permute-start | bytes 344072 | tf_op jit(solution)/shard_map/ppermute | solution.py:45
  3.0 6.4 %collective-permute-start.1 = (f32[224,128]{1,0:T(8,128)S(1)}, f32[224,128]{1,0:T(8,128)S(1)}, u32[]{:S(2)}, u32[]{:S(2)}) collective-permute-start(f32[224,128]{1,0:T(8,128)S(1)} %get-tuple-element.17), channel_id=1, source_target_pairs={{4,8},{8,4},{12,16},{16,12},{20,24},{24,20},{5,9},{9,5},{13,17},{1... | collective-permute-start | bytes 344072 | tf_op jit(solution)/shard_map/ppermute | solution.py:45
  9.7 7.6 %collective-permute-start.2 = (f32[224,128]{1,0:T(8,128)S(1)}, f32[224,128]{1,0:T(8,128)S(1)}, u32[]{:S(2)}, u32[]{:S(2)}) collective-permute-start(f32[224,128]{1,0:T(8,128)S(1)} %get-tuple-element.24), channel_id=1, source_target_pairs={{1,2},{2,1},{5,6},{6,5},{9,10},{10,9},{13,14},{14,13},{17,18},{18,... | collective-permute-start | bytes 344072 | tf_op jit(solution)/shard_map/ppermute | solution.py:45
  14.9 2.5 %collective-permute-start.3 = (f32[224,128]{1,0:T(8,128)S(1)}, f32[224,128]{1,0:T(8,128)S(1)}, u32[]{:S(2)}, u32[]{:S(2)}) collective-permute-start(f32[224,128]{1,0:T(8,128)S(1)} %get-tuple-element.25), channel_id=1, source_target_pairs={{0,1},{1,0},{2,3},{3,2},{4,5},{5,4},{6,7},{7,6},{8,9},{9,8},{10,11... | collective-permute-start | bytes 344072 | tf_op jit(solution)/shard_map/ppermute | solution.py:45

commit v8 on v5

--- a/solution.py
+++ b/solution.py
@@ -37,7 +37,7 @@
 def swap(block, axis):
     count = lax.axis_size(axis)
     out = []
-    for first, part in zip((0, 1), block):
+    for first, part in block:
         pairs = []
         for i in range(first, count - 1, 2):
             pairs += [(i, i + 1), (i + 1, i)]
@@ -63,94 +63,135 @@
     return copies[1:]
 
 
-def pack_kernel(flaw_in, disp_in, vel_in, dam_in, stren_in, con_in, out_a, out_b, disp, vel, dam, stren, con, flaw, sems):
-    pairs = [(flaw_in, flaw)]
-    for side in range(2):
-        wide = pl.ds(side * (CX - 24), 24)
-        near = pl.ds(side * (CX - 16), 16)
-        pairs.append((disp_in.at[:, wide, :], disp.at[side]))
-        pairs.append((vel_in.at[:, near, :], vel.at[side]))
-        for src, dst in ((dam_in, dam), (stren_in, stren), (con_in, con)):
-            pairs.append((src.at[near, :], dst.at[side]))
-    others = run_copies(pairs, sems)
-    factors = [weakness(16, flaw, side * (CX - 16)) for side in range(2)]
-    for copy in others:
-        copy.wait()
-    limits = [stren[side] * factors[side] for side in range(2)]
-
-    def fill(out, side):
-        for k in range(15):
-            width, start = halo_of(k), slab_start(k)
-            held = 24 if k < 6 else 16
-            rows = slice(held - width, held) if side else slice(0, width)
-            if k < 6:
-                part = disp[side, k, rows, :]
-            elif k < 12:
-                part = vel[side, k - 6, rows, :]
-            elif k == 12:
-                part = dam[side, rows, :]
-            elif k == 13:
-                part = limits[side][rows, :]
-            else:
-                part = con[side, rows, :].astype(F32)
-            out[start : start + width, :] = part
-        out[219:SLAB, :] = jnp.zeros((SLAB - 219, LANES), F32)
-
-    even = lax.rem(lax.axis_index("transit"), 2) == 0
-
-    @pl.when(even)
+def corner_place(k):
+    if k < 6:
+        return WIDE * (k // 3), 2 * WIDE * (k % 3)
+    return 2 * WIDE + NEAR * ((k - 6) // 5), 2 * NEAR * ((k - 6) % 5)
+
+
+def edge_rows(k, side, disp, vel, dam, lim, con):
+    width = halo_of(k)
+    rows = slice(CX - width, CX) if side else slice(0, width)
+    if k < 6:
+        return disp[k, rows, :]
+    if k < 12:
+        return vel[k - 6, rows, :]
+    return (dam, lim, con)[k - 12][rows, :].astype(F32)
+
+
+def fill(out, side, own):
+    for k in range(15):
+        out[slab_start(k) : slab_start(k) + halo_of(k), :] = edge_rows(k, side, *own)
+    out[219:SLAB, :] = jnp.zeros((SLAB - 219, LANES), F32)
+
+
+def on_parity(action):
+    odd = lax.rem(lax.axis_index("transit"), 2) == 1
+
+    @pl.when(odd)
     def _():
-        fill(out_a, 1)
-        fill(out_b, 0)
-
-    @pl.when(jnp.logical_not(even))
+        action(1)
+
+    @pl.when(jnp.logical_not(odd))
     def _():
-        fill(out_a, 0)
-        fill(out_b, 1)
-
-
-def load_kernel(flaw_in, disp_in, vel_in, dam_in, stren_in, con_in, disp, vel, dam, lim, con, stren, flaw, sems):
+        action(0)
+
+
+def load_kernel(
+    flaw_in, disp_in, vel_in, dam_in, stren_in, con_in, out_a, disp, vel, dam, lim, con, stren, flaw, sems
+):
     others = run_copies(
-        zip(
-            (flaw_in, disp_in, vel_in, dam_in, stren_in, con_in),
-            (flaw, disp, vel, dam, stren, con),
-        ),
+        zip((flaw_in, disp_in, vel_in, dam_in, stren_in, con_in), (flaw, disp, vel, dam, stren, con)),
         sems,
     )
     factor = weakness(CX, flaw, 0)
     for copy in others:
         copy.wait()
     lim[...] = stren[...] * factor
-
-
-def edge_kernel(disp, vel, dam, lim, con, got_a, got_b, out_a, out_b, flat, ext):
-    even = lax.rem(lax.axis_index("transit"), 2) == 0
-    even_l = lax.rem(lax.axis_index("lateral"), 2) == 0
+    on_parity(lambda side: fill(out_a, side, (disp, vel, dam, lim, con)))
+
+
+def near_kernel(disp, vel, dam, lim, con, corner, out_b):
+    own = (disp, vel, dam, lim, con)
+
+    def action(a_above):
+        side = 1 - a_above
+        for first, last in ((0, 3), (3, 6), (6, 11), (11, 15)):
+            width = halo_of(first)
+            lane = lax.broadcasted_iota(jnp.int32, (width, LANES), 1)
+            block = jnp.zeros((width, LANES), F32)
+            for k in range(first, last):
+                row, start = corner_place(k)
+                moved = pltpu.roll(edge_rows(k, side, *own), width + start, 1)
+                block = jnp.where((lane >= start) & (lane < start + 2 * width), moved, block)
+            corner[row : row + width, :] = block
+        corner[62:64, :] = jnp.zeros((2, LANES), F32)
+        fill(out_b, side, own)
+
+    on_parity(action)
+
+
+def own_field(k, disp, vel, dam, lim, con):
+    if k < 6:
+        return disp[k]
+    if k < 12:
+        return vel[k - 6]
+    return (dam, lim, con)[k - 12][...].astype(F32)
+
+
+def stack_rows(ext, k, part_a, part_b, own, even):
+    width = halo_of(k)
+    low, high = PAD, PAD + CX
+    ext[k, 0 : low - width, :] = jnp.zeros((low - width, LANES), F32)
+    ext[k, low - width : low, :] = jnp.where(even, part_b, part_a)
+    ext[k, low:high, :] = own
+    ext[k, high : high + width, :] = jnp.where(even, part_a, part_b)
+    ext[k, high + width : LANES, :] = jnp.zeros((LANES - high - width, LANES), F32)
+
+
+def turn_tile_kernel(disp, vel, dam, lim, con, own):
+    before, behind = jnp.zeros((PAD, CY), F32), jnp.zeros((LANES - PAD - CX, CY), F32)
     for k in range(15):
-        width, start = halo_of(k), slab_start(k)
-        part_a = got_a[start : start + width, :]
-        part_b = got_b[start : start + width, :]
-        if k < 6:
-            own = disp[k]
-        elif k < 12:
-            own = vel[k - 6]
-        else:
-            own = (dam, lim, con)[k - 12][...].astype(F32)
-        low, high = PAD, PAD + CX
-        ext[k, 0 : low - width, :] = jnp.zeros((low - width, LANES), F32)
-        ext[k, low - width : low, :] = jnp.where(even, part_b, part_a)
-        ext[k, low:high, :] = own
-        ext[k, high : high + width, :] = jnp.where(even, part_a, part_b)
-        ext[k, high + width : LANES, :] = jnp.zeros((LANES - high - width, LANES), F32)
-        turned = ext[k].T
-        flat[k, 8 : 8 + CY, :] = turned
+        own[k] = jnp.concatenate([before, own_field(k, disp, vel, dam, lim, con), behind], 0).T
+
+
+def cut_kernel(own, got_a, corner, out_a, out_b):
+    even = lax.rem(lax.axis_index("lateral"), 2) == 0
+    rows_a = [got_a[rows, :].T for rows in (slice(0, LANES), slice(SLAB - LANES, SLAB))]
+    ends_b = jnp.concatenate([corner[...], corner[...]], 0).T
+
+    def action(a_above):
+        for k in range(15):
+            width, start = halo_of(k), slab_start(k)
+            piece = int(start + width > LANES)
+            lane_a = start - piece * (SLAB - LANES)
+            lane_b, place_b = corner_place(k)
+            lane = lax.broadcasted_iota(jnp.int32, (width, LANES), 1)
+            spots = [(PAD - width, lane < PAD), (PAD + CX, lane >= PAD + CX)]
+            (spot_b, of_b), (spot_a, of_a) = spots if a_above else spots[::-1]
+            found = []
+            for rows, first in ((slice(CY - width, CY), place_b), (slice(0, width), place_b + width)):
+                from_a = pltpu.roll(rows_a[piece][rows, :], (spot_a - lane_a) % LANES, 1)
+                from_b = pltpu.roll(ends_b[first : first + width, :], (spot_b - lane_b) % LANES, 1)
+                found.append(jnp.where(of_a, from_a, jnp.where(of_b, from_b, own[k, rows, :])))
+            right, left = found
+            out_a[start : start + width, :] = jnp.where(even, right, left)
+            out_b[start : start + width, :] = jnp.where(even, left, right)
+
+    on_parity(action)
+    for out in (out_a, out_b):
+        out[219:SLAB, :] = jnp.zeros((SLAB - 219, LANES), F32)
+
+
+def turn_kernel(disp, vel, dam, lim, con, got_a, got_b, flat, ext):
+    even = lax.rem(lax.axis_index("transit"), 2) == 1
+    for k in range(15):
+        rows = slice(slab_start(k), slab_start(k) + halo_of(k))
+        own = own_field(k, disp, vel, dam, lim, con)
+        stack_rows(ext, k, got_a[rows, :], got_b[rows, :], own, even)
+        flat[k, 8 : 8 + CY, :] = ext[k].T
         flat[k, 0:8, :] = jnp.zeros((8, LANES), F32)
         flat[k, 8 + CY : 16 + CY, :] = jnp.zeros((8, LANES), F32)
-        right, left = turned[CY - width :, :], turned[:width, :]
-        out_a[start : start + width, :] = jnp.where(even_l, right, left)
-        out_b[start : start + width, :] = jnp.where(even_l, left, right)
-    for out in (out_a, out_b):
-        out[219:SLAB, :] = jnp.zeros((SLAB - 219, LANES), F32)
 
 
 def split(x):
@@ -191,6 +232,16 @@
         cols = slice(ch % 2 * LANES, (ch % 2 + 1) * LANES)
         turned[ch // 2, 0:rows, cols] = high
         turned[ch // 2, rows : 2 * rows, cols] = low
+
+
+def block_sums(energy, turned, block, rows, band):
+    both = jnp.dot(energy[block], band[...], preferred_element_type=F32)
+    high, low = split(both[:, :LANES] + both[:, LANES:])
+    for ch in range(12):
+        cols = slice(ch % 2 * LANES, (ch % 2 + 1) * LANES)
+        part = slice(16 * ch, 16 * ch + 16)
+        turned[ch // 2, 16 * block : 16 * block + 16, cols] = high[part]
+        turned[ch // 2, rows + 16 * block : rows + 16 * block + 16, cols] = low[part]
 
 
 def row_sums(turned, pair, rows, first, second):
@@ -289,16 +340,22 @@
     return new
 
 
-def gather(state, off, starts, energy, turned, band):
+def gather(state, off, starts, energy, turned, band, by_block=False):
     for n, b in enumerate(starts):
         def get(k, shift):
             return state[k, off + b + shift : off + b + shift + 16, :]
 
         def put(ch, cols, value):
-            energy[ch, 16 * n : 16 * n + 16, cols] = value
+            if by_block:
+                energy[n, 16 * ch : 16 * ch + 16, cols] = value
+            else:
+                energy[ch, 16 * n : 16 * n + 16, cols] = value
 
         products(get, put)
-    lane_sums(energy, turned, 16 * len(starts), band)
+        if by_block:
+            block_sums(energy, turned, n, 16 * len(starts), band)
+    if not by_block:
+        lane_sums(energy, turned, 16 * len(starts), band)
 
 
 def inner_kernel(
@@ -384,7 +441,7 @@
         new = harm(b, row, aver, rows_of(ext.at[13], OFF, b), old, hd, cover, decay)
         ext[12, OFF + b : OFF + b + 8, :] = new
 
-    gather(ext, OFF, (-24, -8, 120, 136), energy, turned, band)
+    gather(ext, OFF, (-24, -8, 120, 136), energy, turned, band, True)
     for pair in range(6):
         aver[pair] = partial[pair] + row_sums(turned, pair, 64, rim_1, rim_2)
     for row, b in enumerate((*range(-16, 16, 8), *range(112, 144, 8))):
@@ -396,7 +453,7 @@
     move(-16, 16, ext, OFF, hd, contact, rate, wp, fm, put_next)
     move(112, 144, ext, OFF, hd, contact, rate, wp, fm, put_next)
 
-    gather(ext2, OFF, (-16, 0, 16, 96, 112, 128), energy, turned, band)
+    gather(ext2, OFF, (-16, 0, 16, 96, 112, 128), energy, turned, band, True)
     for pair in range(6):
         aver[pair] = row_sums(turned, pair, 96, all_1, all_2)
     for row, b in enumerate((*range(-8, 24, 8), *range(104, 136, 8))):
@@ -484,45 +541,58 @@
         pltpu.with_memory_space_constraint(x, pltpu.HBM)
         for x in (flaw_cells, displacement, velocity, damage, strength, contact)
     ]
-    flaw_copy = pltpu.SMEM(flaw_cells.shape, jnp.int32)
-    send_a, send_b = pl.pallas_call(
-        pack_kernel,
-        out_shape=[shape((SLAB, LANES), F32)] * 2,
+    tile = shape((CX, CY), F32)
+    send_a, *own = pl.pallas_call(
+        load_kernel,
+        out_shape=[shape((SLAB, LANES), F32)]
+        + [shape((6, CX, CY), F32)] * 2
+        + [tile, tile, shape((CX, CY), jnp.int32)],
         in_specs=[pl.BlockSpec(memory_space=pltpu.HBM)] * 6,
-        out_specs=vmem(2),
+        out_specs=vmem(6),
         scratch_shapes=[
-            pltpu.VMEM((2, 6, 24, CY), F32),
-            pltpu.VMEM((2, 6, 16, CY), F32),
-            pltpu.VMEM((2, 16, CY), F32),
-            pltpu.VMEM((2, 16, CY), F32),
-            pltpu.VMEM((2, 16, CY), jnp.int32),
-            flaw_copy,
-            pltpu.SemaphoreType.DMA((11,)),
+            pltpu.VMEM((CX, CY), F32),
+            pltpu.SMEM(flaw_cells.shape, jnp.int32),
+            pltpu.SemaphoreType.DMA((6,)),
         ],
-        compiler_params=params,
-        name="pack_rows",
-    )(*inputs)
-    got = swap((send_a, send_b), "transit")
-    tile = shape((CX, CY), F32)
-    own = pl.pallas_call(
-        load_kernel,
-        out_shape=[shape((6, CX, CY), F32)] * 2 + [tile, tile, shape((CX, CY), jnp.int32)],
-        in_specs=[pl.BlockSpec(memory_space=pltpu.HBM)] * 6,
-        out_specs=vmem(5),
-        scratch_shapes=[pltpu.VMEM((CX, CY), F32), flaw_copy, pltpu.SemaphoreType.DMA((6,))],
         compiler_params=params,
         name="load_tile",
     )(*inputs)
-    side_a, side_b, flat = pl.pallas_call(
-        edge_kernel,
-        out_shape=[shape((SLAB, LANES), F32)] * 2 + [shape((15, 16 + CY, LANES), F32)],
+    corner, send_b = pl.pallas_call(
+        near_kernel,
+        out_shape=[shape((64, LANES), F32), shape((SLAB, LANES), F32)],
+        in_specs=vmem(5),
+        out_specs=vmem(2),
+        compiler_params=params,
+        name="near_rows",
+    )(*own)
+    got_a, got_corner, got_b = swap(((1, send_a), (0, corner), (0, send_b)), "transit")
+    fields = pltpu.VMEM((15, LANES, LANES), F32)
+    turned = pl.pallas_call(
+        turn_tile_kernel,
+        out_shape=shape((15, CY, LANES), F32),
+        in_specs=vmem(5),
+        out_specs=vmem(1)[0],
+        compiler_params=params,
+        name="turn_tile",
+    )(*own)
+    side = pl.pallas_call(
+        cut_kernel,
+        out_shape=[shape((SLAB, LANES), F32)] * 2,
+        in_specs=vmem(3),
+        out_specs=vmem(2),
+        compiler_params=params,
+        name="cut_columns",
+    )(turned, got_a, got_corner)
+    side = swap(enumerate(side), "lateral")
+    flat = pl.pallas_call(
+        turn_kernel,
+        out_shape=shape((15, 16 + CY, LANES), F32),
         in_specs=vmem(7),
-        out_specs=vmem(3),
-        scratch_shapes=[pltpu.VMEM((15, LANES, LANES), F32)],
+        out_specs=vmem(1)[0],
+        scratch_shapes=[fields],
         compiler_params=params,
-        name="turn_and_cut",
-    )(*own, *got)
-    side = swap((side_a, side_b), "lateral")
+        name="turn_fields",
+    )(*own, got_a, got_b)
     band, of_own, table = tables(CX * lax.axis_size("transit"), CY * lax.axis_size("lateral"))
     held = pltpu.VMEM((HELD, LANES), F32)
     inner = pl.pallas_call(
@@ -561,7 +631,7 @@
             pltpu.VMEM((8, HELD, LANES), F32),
             pltpu.VMEM((6, HELD, LANES), F32),
             held,
-            pltpu.VMEM((12, 96, 2 * LANES), BF16),
+            pltpu.VMEM((6, 192, 2 * LANES), BF16),
             pltpu.VMEM((6, 192, 2 * LANES), BF16),
             pltpu.VMEM((6, 64, 2 * LANES), F32),
             pltpu.VMEM((12, CY, LANES), F32),

time: 20.5 us -> 19.9 us (0.971)
  Pallas kernels: 7.31 us -> 6.96 us
  starting transfers between devices: 8.49 us -> 8.22 us
    pallas_call x3 -> x5, Pallas kernels: 2.58 us -> 2.26 us  [the longest x1 1.1 us: on_device(): pl.pallas_call(load_kernel, out_shape=[shape((SLAB, LANES), F32)] + [shap...]
    ppermute x4 -> x5, starting transfers between devices: 8.49 us -> 8.22 us  [swap(): out.append(lax.ppermute(part, axis, pairs))]
    ppermute x4 -> x5, waiting for transfers between devices: 2.3 us -> 2.2 us  [swap(): out.append(lax.ppermute(part, axis, pairs))]
  transfers between devices with their start and end apart: 4 -> 5, of which waited for: 2 -> 1; matrix products, arithmetic and copies ran while one was open for 7% -> 7% of each run, Pallas kernels for 15% -> 16%
where the time goes in v8:
time: 19.9 us; the launch traced here: 19.5 us
  starting transfers between devices  8.22 us (41%)
  Pallas kernels  6.96 us (35%)
  waiting for transfers between devices  2.2 us (11%)
  other arithmetic  1.03 us (5%)
  between operations  0.82 us (4%)
  local copies, waits for them, and re-layouts  0.31 us (2%)
    ppermute x5, starting transfers between devices, swap(): out.append(lax.ppermute(part, axis, pairs))  8.22 us
    pallas_call x1, Pallas kernels, on_device(): pl.pallas_call(step_kernel, out_shape=[shape((6, CX, CY), F32)] * 2 + [sh...  2.77 us
    ppermute x5, waiting for transfers between devices, swap(): out.append(lax.ppermute(part, axis, pairs))  2.2 us
    pallas_call x1, Pallas kernels, on_device(): pl.pallas_call(inner_kernel, out_shape=[shape((6, 64, 2 * LANES), F32), s...  1.93 us
    pallas_call x1, Pallas kernels, on_device(): pl.pallas_call(load_kernel, out_shape=[shape((SLAB, LANES), F32)] + [shap...  1.1 us
  transfers between devices with their start and end apart: 5, of which 1 were waited for; matrix products, arithmetic and copies ran while one was open for 7% of the time, Pallas kernels for 16%

profile of v8, /device:TPU:25, one launch (start us, length us, event | category | flops | bytes accessed | tf_op | source)
XLA Modules:
  0.0 19.5 jit_solution(4216303367808727548)
XLA Ops:
  0.6 1.1 %load_tile.1 = (f32[224,128]{1,0:T(8,128)S(1)}, f32[6,64,128]{2,1,0:T(8,128)S(1)}, f32[6,64,128]{2,1,0:T(8,128)S(1)}, f32[64,128]{1,0:T(8,128)S(1)}, f32[64,128]{1,0:T(8,128)S(1)}, /*index=5*/s32[64,128]{1,0:T(8,128)S(1)}) custom-call(s32[1,1,32]{2,1,0:T(1,128)} %flaw_in.1, f32[6,64,128]{2,1,0:T(8,128)} %disp_in.1, f32[6,64,128]{2,1,0:T(8,128)} %vel_in.1, ...), custom_call_target="tpu_custom_call" | custom-call | tf_op jit(solution)/shard_map/load_tile/pallas_call | solution.py:545
  1.7 3.0 %collective-permute-start = (f32[224,128]{1,0:T(8,128)S(1)}, f32[224,128]{1,0:T(8,128)S(1)}, u32[]{:S(2)}, u32[]{:S(2)}) collective-permute-start(f32[224,128]{1,0:T(8,128)S(1)} %get-tuple-element.23), channel_id=1, source_target_pairs={{4,8},{8,4},{12,16},{16,12},{20,24},{24,20},{5,9},{9,5},{13,17},{1... | collective-permute-start | bytes 344072 | tf_op jit(solution)/shard_map/ppermute | solution.py:44
  4.8 0.1 near_rows.1
  5.0 1.5 %collective-permute-start.1 = (f32[224,128]{1,0:T(8,128)S(1)}, f32[224,128]{1,0:T(8,128)S(1)}, u32[]{:S(2)}, u32[]{:S(2)}) collective-permute-start(f32[224,128]{1,0:T(8,128)S(1)} %get-tuple-element.24), channel_id=1, source_target_pairs={{0,4},{4,0},{8,12},{12,8},{16,20},{20,16},{24,28},{28,24},{1,5},{5... | collective-permute-start | bytes 344072 | tf_op jit(solution)/shard_map/ppermute | solution.py:44
  6.5 0.1 slice.40
  6.6 0.1 fusion.11
  6.7 0.1 broadcast_select_fusion
  6.9 0.1 fusion.18
  7.0 0.1 fusion.13
  7.1 0.1 fusion.6
  7.2 0.1 pad_maximum_fusion.1.mid_1
  7.3 0.1 fusion.19
  7.4 0.1 fusion.15
  7.5 0.1 and_select_fusion.1
  7.6 0.1 pad_maximum_fusion.2.all_1
  7.7 0.1 fusion.14
  7.8 0.3 %turn_tile.1.own = f32[15,128,128]{2,1,0:T(8,128)S(1)} custom-call(f32[6,64,128]{2,1,0:T(8,128)S(1)} %get-tuple-element.18.disp, f32[6,64,128]{2,1,0:T(8,128)S(1)} %get-tuple-element.19.vel, f32[64,128]{1,0:T(8,128)S(1)} %get-tuple-element.20.dam, f32[64,128]{1,0:T(8,128)S(1)} %get-tuple-element.21.lim, s32[64,128]{1,0:T(8,128)S(1)} %get-tuple-element.22.con), custom_call_target="tpu_custom_call" | custom-call | tf_op jit(solution)/shard_map/turn_tile/pallas_call | solution.py:570
  8.2 2.1 %collective-permute-done.2.corner = f32[64,128]{1,0:T(8,128)S(1)} collective-permute-done((f32[64,128]{1,0:T(8,128)S(1)}, f32[64,128]{1,0:T(8,128)S(1)}, u32[]{:S(2)}, u32[]{:S(2)}) %collective-permute-start.2) | collective-permute-done | bytes 32800 | tf_op jit(solution)/shard_map/ppermute | solution.py:44
  10.3 0.3 %cut_columns.1 = (f32[224,128]{1,0:T(8,128)S(1)}, f32[224,128]{1,0:T(8,128)S(1)}) custom-call(f32[15,128,128]{2,1,0:T(8,128)S(1)} %turn_tile.1.own, f32[224,128]{1,0:T(8,128)S(1)} %collective-permute-done.got_a, f32[64,128]{1,0:T(8,128)S(1)} %collective-permute-done.2.corner), custom_call_target="tpu_custom_call" | custom-call | tf_op jit(solution)/shard_map/cut_columns/pallas_call | solution.py:578
  10.7 3.6 %collective-permute-start.3 = (f32[224,128]{1,0:T(8,128)S(1)}, f32[224,128]{1,0:T(8,128)S(1)}, u32[]{:S(2)}, u32[]{:S(2)}) collective-permute-start(f32[224,128]{1,0:T(8,128)S(1)} %get-tuple-element.31), channel_id=1, source_target_pairs={{1,2},{2,1},{5,6},{6,5},{9,10},{10,9},{13,14},{14,13},{17,18},{18,... | collective-permute-start | bytes 344072 | tf_op jit(solution)/shard_map/ppermute | solution.py:44
  14.3 0.1 pad_maximum_fusion.3.rim_1
  14.4 0.4 %turn_fields.1.flat = f32[15,144,128]{2,1,0:T(8,128)S(1)} custom-call(f32[6,64,128]{2,1,0:T(8,128)S(1)} %get-tuple-element.18.disp, f32[6,64,128]{2,1,0:T(8,128)S(1)} %get-tuple-element.19.vel, f32[64,128]{1,0:T(8,128)S(1)} %get-tuple-element.20.dam, f32[64,128]{1,0:T(8,128)S(1)} %get-tuple-element.21.lim, s32[64,128]{1,0:T(8,128)S(1)} %get-tuple-element.22.con, ...), custom_call_target="tpu_custom_call" | custom-call | tf_op jit(solution)/shard_map/turn_fields/pallas_call | solution.py:587
  14.8 1.9 %inner_rows.1 = (f32[6,64,256]{2,1,0:T(8,128)S(1)}, f32[12,48,128]{2,1,0:T(8,128)S(1)}, f32[32,128]{1,0:T(8,128)S(1)}, f32[12,80,128]{2,1,0:T(8,128)S(1)}, f32[80,128]{1,0:T(8,128)S(1)}) custom-call(f32[15,144,128]{2,1,0:T(8,128)S(1)} %turn_fields.1.flat, bf16[256,256]{1,0:T(8,128)(2,1)S(1)} %maximum_maximum_fusion.band, ...), custom_call_target="tpu_custom_call" | custom-call | flops 800000000 | bytes 2000000 | tf_op jit(solution)/shard_map/inner_rows/pallas_call | solution.py:598
  16.8 2.8 %two_steps.1 = (f32[6,64,128]{2,1,0:T(8,128)}, f32[6,64,128]{2,1,0:T(8,128)}, f32[64,128]{1,0:T(8,128)}) custom-call(f32[15,144,128]{2,1,0:T(8,128)S(1)} %turn_fields.1.flat, f32[6,64,256]{2,1,0:T(8,128)S(1)} %get-tuple-element.25.partial, f32[12,48,128]{2,1,0:T(8,128)S(1)} %get-tuple-element.26.moved, f32[32,128]{1,0:T(8,128)S(1)} %get-tuple-element.27.harmed_1, ...), custom_call_target="tpu_custom_call" | custom-call | tf_op jit(solution)/shard_map/two_steps/pallas_call | solution.py:623
  (16 shorter events, 0.4 us)
Async XLA Ops:
  1.7 8.6 %collective-permute-start = (f32[224,128]{1,0:T(8,128)S(1)}, f32[224,128]{1,0:T(8,128)S(1)}, u32[]{:S(2)}, u32[]{:S(2)}) collective-permute-start(f32[224,128]{1,0:T(8,128)S(1)} %get-tuple-element.23), channel_id=1, source_target_pairs={{4,8},{8,4},{12,16},{16,12},{20,24},{24,20},{5,9},{9,5},{13,17},{1... | collective-permute-start | bytes 344072 | tf_op jit(solution)/shard_map/ppermute | solution.py:44
  4.9 5.4 %collective-permute-start.2 = (f32[64,128]{1,0:T(8,128)S(1)}, f32[64,128]{1,0:T(8,128)S(1)}, u32[]{:S(2)}, u32[]{:S(2)}) collective-permute-start(f32[64,128]{1,0:T(8,128)S(1)} %get-tuple-element.30), channel_id=1, source_target_pairs={{0,4},{4,0},{8,12},{12,8},{16,20},{20,16},{24,28},{28,24},{1,5},{5... | collective-permute-start | bytes 98312 | tf_op jit(solution)/shard_map/ppermute | solution.py:44
  5.0 9.4 %collective-permute-start.1 = (f32[224,128]{1,0:T(8,128)S(1)}, f32[224,128]{1,0:T(8,128)S(1)}, u32[]{:S(2)}, u32[]{:S(2)}) collective-permute-start(f32[224,128]{1,0:T(8,128)S(1)} %get-tuple-element.24), channel_id=1, source_target_pairs={{0,4},{4,0},{8,12},{12,8},{16,20},{20,16},{24,28},{28,24},{1,5},{5... | collective-permute-start | bytes 344072 | tf_op jit(solution)/shard_map/ppermute | solution.py:44
  10.7 6.1 %collective-permute-start.3 = (f32[224,128]{1,0:T(8,128)S(1)}, f32[224,128]{1,0:T(8,128)S(1)}, u32[]{:S(2)}, u32[]{:S(2)}) collective-permute-start(f32[224,128]{1,0:T(8,128)S(1)} %get-tuple-element.31), channel_id=1, source_target_pairs={{1,2},{2,1},{5,6},{6,5},{9,10},{10,9},{13,14},{14,13},{17,18},{18,... | collective-permute-start | bytes 344072 | tf_op jit(solution)/shard_map/ppermute | solution.py:44
  14.3 2.5 %collective-permute-start.4 = (f32[224,128]{1,0:T(8,128)S(1)}, f32[224,128]{1,0:T(8,128)S(1)}, u32[]{:S(2)}, u32[]{:S(2)}) collective-permute-start(f32[224,128]{1,0:T(8,128)S(1)} %get-tuple-element.32), channel_id=1, source_target_pairs={{0,1},{1,0},{2,3},{3,2},{4,5},{5,4},{6,7},{7,6},{8,9},{9,8},{10,11... | collective-permute-start | bytes 344072 | tf_op jit(solution)/shard_map/ppermute | solution.py:44
